TPU v7x, 32 devices: a whole 2x2x4 slice. The times are simulated.
32 devices in a mesh: fsdp: 8 (over z, x), tp: 4 (over y, core).
Axes of the slice: x: 2, y: 2, z: 4, core: 2. Of those that a mesh axis runs over, the one named last changes fastest.
Arguments:
- inputs: bfloat16 [4096, 2304], P(('fsdp', 'tp')), may hold values from -6 to 6
- segments: int32 [4096], P('fsdp'), may hold values from 0 to 5, never falling along the last dimension, each value on 1 to 2000 neighbouring positions
- cotangent: bfloat16 [4096, 2304], P(('fsdp', 'tp')), may hold values from -6 to 6
- project_weight: float32 [2304, 4, 4, 256], P('fsdp', 'tp'), may hold values from -3 to 3
- output_weight: float32 [2048, 2304], P('tp', 'fsdp'), may hold values from -0.125 to 0.125
- gate_up_weight: float32 [2304, 2, 9216], P('fsdp', None, 'tp'), may hold values from -0.125 to 0.125
- down_weight: float32 [9216, 2304], P('tp', 'fsdp'), may hold values from -0.0625 to 0.0625
- norm_gains: float32 [4, 2304], P(None, ('fsdp', 'tp')), may hold values from 0.5 to 1.5
- project_mean: float32 [2304, 4, 4, 256], P('fsdp', 'tp'), may hold values from -40 to 40
- project_power: float32 [2304, 4, 4, 256], P('fsdp', 'tp'), may hold values from 204.8 to 819.2
- output_mean: float32 [2048, 2304], P('tp', 'fsdp'), may hold values from -40 to 40
- output_power: float32 [2048, 2304], P('tp', 'fsdp'), may hold values from 204.8 to 819.2
- gate_up_mean: float32 [2304, 2, 9216], P('fsdp', None, 'tp'), may hold values from -40 to 40
- gate_up_power: float32 [2304, 2, 9216], P('fsdp', None, 'tp'), may hold values from 204.8 to 819.2
- down_mean: float32 [9216, 2304], P('tp', 'fsdp'), may hold values from -40 to 40
- down_power: float32 [9216, 2304], P('tp', 'fsdp'), may hold values from 204.8 to 819.2
- gains_mean: float32 [4, 2304], P(None, ('fsdp', 'tp')), may hold values from -40 to 40
- gains_power: float32 [4, 2304], P(None, ('fsdp', 'tp')), may hold values from 204.8 to 819.2
Outputs:
- layer_output: bfloat16 [4096, 2304], P(('fsdp', 'tp'))
- input_grad: float32 [4096, 2304], P(('fsdp', 'tp'))
- project_grad: float32 [2304, 4, 4, 256], P('fsdp', 'tp')
- project_new: float32 [2304, 4, 4, 256], P('fsdp', 'tp')
- project_mean_new: float32 [2304, 4, 4, 256], P('fsdp', 'tp')
- project_power_new: float32 [2304, 4, 4, 256], P('fsdp', 'tp')
- output_grad: float32 [2048, 2304], P('tp', 'fsdp')
- output_new: float32 [2048, 2304], P('tp', 'fsdp')
- output_mean_new: float32 [2048, 2304], P('tp', 'fsdp')
- output_power_new: float32 [2048, 2304], P('tp', 'fsdp')
- gate_up_grad: float32 [2304, 2, 9216], P('fsdp', None, 'tp')
- gate_up_new: float32 [2304, 2, 9216], P('fsdp', None, 'tp')
- gate_up_mean_new: float32 [2304, 2, 9216], P('fsdp', None, 'tp')
- gate_up_power_new: float32 [2304, 2, 9216], P('fsdp', None, 'tp')
- down_grad: float32 [9216, 2304], P('tp', 'fsdp')
- down_new: float32 [9216, 2304], P('tp', 'fsdp')
- down_mean_new: float32 [9216, 2304], P('tp', 'fsdp')
- down_power_new: float32 [9216, 2304], P('tp', 'fsdp')
- gains_grad: float32 [4, 2304], P(None, ('fsdp', 'tp'))
- gains_step: float32 [4, 2304], P(None, ('fsdp', 'tp'))
- gains_mean_new: float32 [4, 2304], P(None, ('fsdp', 'tp'))
- gains_power_new: float32 [4, 2304], P(None, ('fsdp', 'tp'))
Inputs may be any that keep to these rules, and one draw needn't show every extreme that they name: `segments`: segment numbers never decrease along the tokens; one number marks one document, and a document may continue across the boundary between sequences.
All inputs are finite; a program needn't handle non-finite values.
Results may differ from a plain program's by a relative error of at most 0.025.
Values may be sent and summed in bfloat16 or wider, within the bound.
No kernel may reach another device: no remote copies, remote signals or barrier semaphores. Data moves between devices by JAX's collectives and lax.ppermute only.
A program may use at most 256 MiB of HBM per device.

v0:
```python
import jax
import jax.numpy as jnp
from jax import lax
from jax.sharding import PartitionSpec as P

SEQ = 512


norm_eps = 1e-06
soft_cap = 50.0
rope_base = 10000.0
beta_first = 0.9
beta_second = 0.95
learn_rate = 0.02
decay_rate = 0.1
adam_eps = 1e-08
step_number = 3.0


def norm_forward(values, gain_vec):
    factor = lax.rsqrt(jnp.mean(values * values, axis=-1, keepdims=True) + norm_eps)
    return (values * factor * gain_vec, factor)


def norm_backward(values, factor, gain_vec, incoming):
    unit_rows = values * factor
    gain_part = jnp.sum(incoming * unit_rows, axis=0)
    scaled = incoming * gain_vec
    return (
        factor * (scaled - unit_rows * jnp.mean(scaled * unit_rows, axis=-1, keepdims=True)),
        gain_part,
    )


def rope_tables(length, head_width):
    half_width = head_width // 2
    frequency = rope_base ** (-2.0 * jnp.arange(half_width, dtype=jnp.float32) / head_width)
    angles = jnp.arange(length, dtype=jnp.float32)[:, None] * frequency[None, :]
    return (jnp.cos(angles), jnp.sin(angles))


def rotate(values, cosine_table, sine_table):
    half_width = values.shape[-1] // 2
    first_half = values[..., :half_width]
    second_half = values[..., half_width:]
    return jnp.concatenate(
        [
            first_half * cosine_table - second_half * sine_table,
            second_half * cosine_table + first_half * sine_table,
        ],
        axis=-1,
    )


def unrotate(slopes, cosine_table, sine_table):
    half_width = slopes.shape[-1] // 2
    first_half = slopes[..., :half_width]
    second_half = slopes[..., half_width:]
    return jnp.concatenate(
        [
            first_half * cosine_table + second_half * sine_table,
            second_half * cosine_table - first_half * sine_table,
        ],
        axis=-1,
    )


def allowed_pairs(seg_row):
    places = jnp.arange(seg_row.shape[0])
    return (seg_row[:, None] == seg_row[None, :]) & (places[None, :] <= places[:, None])


def attend_forward(element):
    queries, key_vectors, value_rows, seg_row = element
    scores = jnp.einsum("qhgd,khd->hgqk", queries, key_vectors, preferred_element_type=jnp.float32)
    capped = soft_cap * jnp.tanh(scores / soft_cap)
    capped = jnp.where(allowed_pairs(seg_row), capped, -jnp.inf)
    row_max = jnp.max(capped, axis=-1, keepdims=True)
    exp_scores = jnp.exp(capped - row_max)
    row_total = jnp.sum(exp_scores, axis=-1, keepdims=True)
    prob_values = (exp_scores / row_total).astype(jnp.bfloat16)
    context = jnp.einsum(
        "hgqk,khd->qhgd", prob_values, value_rows, preferred_element_type=jnp.float32
    )
    return (context, row_max + jnp.log(row_total))


def attend_backward(element):
    queries, key_vectors, value_rows, seg_row, logsum, context_slope = element
    scores = jnp.einsum("qhgd,khd->hgqk", queries, key_vectors, preferred_element_type=jnp.float32)
    tanh_value = jnp.tanh(scores / soft_cap)
    capped = soft_cap * tanh_value
    prob_values = jnp.where(allowed_pairs(seg_row), jnp.exp(capped - logsum), 0.0)
    prob_slope = jnp.einsum(
        "qhgd,khd->hgqk", context_slope, value_rows, preferred_element_type=jnp.float32
    )
    value_slope = jnp.einsum(
        "hgqk,qhgd->khd",
        prob_values.astype(jnp.bfloat16),
        context_slope,
        preferred_element_type=jnp.float32,
    )
    inner_sum = jnp.sum(prob_values * prob_slope, axis=-1, keepdims=True)
    score_slope = (prob_values * (prob_slope - inner_sum) * (1.0 - tanh_value * tanh_value)).astype(
        jnp.bfloat16
    )
    query_slope = jnp.einsum(
        "hgqk,khd->qhgd", score_slope, key_vectors, preferred_element_type=jnp.float32
    )
    key_slope = jnp.einsum(
        "hgqk,qhgd->khd", score_slope, queries, preferred_element_type=jnp.float32
    )
    return (query_slope, key_slope, value_slope)


def gelu_product(gate_in, up_in):
    return jax.nn.gelu(gate_in, approximate=True) * up_in


def adam_step(weight, gradient, mean_old, power_old):
    mean_new = beta_first * mean_old + (1.0 - beta_first) * gradient
    power_new = beta_second * power_old + (1.0 - beta_second) * gradient * gradient
    mean_hat = mean_new / (1.0 - beta_first**step_number)
    power_hat = power_new / (1.0 - beta_second**step_number)
    change = -learn_rate * (mean_hat / (jnp.sqrt(power_hat) + adam_eps) + decay_rate * weight)
    return (weight + change, mean_new, power_new, change)


def per_device(
    inputs,
    segments,
    cotangent,
    project_weight,
    output_weight,
    gate_up_weight,
    down_weight,
    norm_gains,
    project_mean,
    project_power,
    output_mean,
    output_power,
    gate_up_mean,
    gate_up_power,
    down_mean,
    down_power,
    gains_mean,
    gains_power,
):
    float_type = jnp.float32
    half_type = jnp.bfloat16
    gains_all = lax.all_gather(norm_gains, ("fsdp", "tp"), axis=1, tiled=True)
    full_project, full_output, full_gate_up, full_down = (
        lax.all_gather(project_weight.astype(half_type), "fsdp", axis=0, tiled=True),
        lax.all_gather(output_weight.astype(half_type), "fsdp", axis=1, tiled=True),
        lax.all_gather(gate_up_weight.astype(half_type), "fsdp", axis=0, tiled=True),
        lax.all_gather(down_weight.astype(half_type), "fsdp", axis=1, tiled=True),
    )
    residual_in = inputs.astype(float_type)
    normed_one, factor_one = norm_forward(residual_in, gains_all[0])
    rows_one = lax.all_gather(normed_one.astype(half_type), "tp", axis=0, tiled=True)
    total_rows = rows_one.shape[0]
    seq_count = total_rows // SEQ
    mixed_rows = jnp.einsum(
        "rd,dhjc->rhjc", rows_one, full_project, preferred_element_type=float_type
    )
    kv_local = mixed_rows.shape[1]
    group_size = mixed_rows.shape[2] - 2
    head_width = mixed_rows.shape[3]
    query_scale = head_width ** (-0.5)
    cosine_table, sine_table = rope_tables(SEQ, head_width)
    cosine_query = cosine_table[:, None, None, :]
    sine_query = sine_table[:, None, None, :]
    cosine_key = cosine_table[:, None, :]
    sine_key = sine_table[:, None, :]
    shaped = mixed_rows.reshape(seq_count, SEQ, kv_local, group_size + 2, head_width)
    queries = (rotate(shaped[:, :, :, :group_size], cosine_query, sine_query) * query_scale).astype(
        half_type
    )
    key_vectors = rotate(shaped[:, :, :, group_size], cosine_key, sine_key).astype(half_type)
    value_rows = shaped[:, :, :, group_size + 1].astype(half_type)
    seg_rows = segments.reshape(seq_count, SEQ)
    context, logsum = lax.map(attend_forward, (queries, key_vectors, value_rows, seg_rows))
    context_flat = context.astype(half_type).reshape(total_rows, kv_local * group_size * head_width)
    attend_sum = lax.psum_scatter(
        jnp.dot(context_flat, full_output, preferred_element_type=float_type),
        "tp",
        scatter_dimension=0,
        tiled=True,
    )
    post_one, factor_two = norm_forward(attend_sum, gains_all[1])
    hidden_state = residual_in + post_one
    normed_two, factor_three = norm_forward(hidden_state, gains_all[2])
    rows_two = lax.all_gather(normed_two.astype(half_type), "tp", axis=0, tiled=True)
    gate_up = jnp.einsum("rd,djf->rjf", rows_two, full_gate_up, preferred_element_type=float_type)
    gate_value = gate_up[:, 0]
    up_value = gate_up[:, 1]
    activated = gelu_product(gate_value, up_value).astype(half_type)
    feed_sum = lax.psum_scatter(
        jnp.dot(activated, full_down, preferred_element_type=float_type),
        "tp",
        scatter_dimension=0,
        tiled=True,
    )
    post_two, factor_four = norm_forward(feed_sum, gains_all[3])
    layer_output = hidden_state + post_two
    upstream = cotangent.astype(float_type)
    feed_slope, gain_four = norm_backward(feed_sum, factor_four, gains_all[3], upstream)
    feed_slope_rows = lax.all_gather(feed_slope.astype(half_type), "tp", axis=0, tiled=True)
    activated_slope = jnp.einsum(
        "rd,fd->rf", feed_slope_rows, full_down, preferred_element_type=float_type
    )
    down_grad = jnp.einsum(
        "rf,rd->fd", activated, feed_slope_rows, preferred_element_type=float_type
    )
    unused_value, gelu_pull = jax.vjp(gelu_product, gate_value, up_value)
    gate_slope, up_slope = gelu_pull(activated_slope)
    gate_up_slope = jnp.stack([gate_slope, up_slope], axis=1).astype(half_type)
    gate_up_grad = jnp.einsum(
        "rd,rjf->djf", rows_two, gate_up_slope, preferred_element_type=float_type
    )
    normed_two_slope = lax.psum_scatter(
        jnp.einsum("rjf,djf->rd", gate_up_slope, full_gate_up, preferred_element_type=float_type),
        "tp",
        scatter_dimension=0,
        tiled=True,
    )
    hidden_part, gain_three = norm_backward(
        hidden_state, factor_three, gains_all[2], normed_two_slope
    )
    hidden_slope = upstream + hidden_part
    attend_slope, gain_two = norm_backward(attend_sum, factor_two, gains_all[1], hidden_slope)
    attend_slope_rows = lax.all_gather(attend_slope.astype(half_type), "tp", axis=0, tiled=True)
    context_slope = jnp.einsum(
        "rd,cd->rc", attend_slope_rows, full_output, preferred_element_type=float_type
    ).astype(half_type)
    output_grad = jnp.einsum(
        "rc,rd->cd", context_flat, attend_slope_rows, preferred_element_type=float_type
    )
    context_slope = context_slope.reshape(seq_count, SEQ, kv_local, group_size, head_width)
    query_slope, key_slope, value_slope = lax.map(
        attend_backward, (queries, key_vectors, value_rows, seg_rows, logsum, context_slope)
    )
    query_pre_slope = unrotate(query_slope * query_scale, cosine_query, sine_query)
    key_pre_slope = unrotate(key_slope, cosine_key, sine_key)
    mixed_slope = jnp.concatenate(
        [query_pre_slope, key_pre_slope[:, :, :, None], value_slope[:, :, :, None]], axis=3
    ).astype(half_type)
    mixed_slope = mixed_slope.reshape(total_rows, kv_local, group_size + 2, head_width)
    project_grad = jnp.einsum(
        "rd,rhjc->dhjc", rows_one, mixed_slope, preferred_element_type=float_type
    )
    normed_one_slope = lax.psum_scatter(
        jnp.einsum(
            "rhjc,dhjc->rd", mixed_slope, full_project, preferred_element_type=float_type
        ).astype(jnp.bfloat16),
        "tp",
        scatter_dimension=0,
        tiled=True,
    ).astype(jnp.float32)
    input_part, gain_one = norm_backward(residual_in, factor_one, gains_all[0], normed_one_slope)
    input_grad = hidden_slope + input_part
    project_grad, output_grad, gate_up_grad, down_grad = (
        lax.psum_scatter(
            project_grad.astype(jnp.bfloat16), "fsdp", scatter_dimension=0, tiled=True
        ).astype(jnp.float32),
        lax.psum_scatter(
            output_grad.astype(jnp.bfloat16), "fsdp", scatter_dimension=1, tiled=True
        ).astype(jnp.float32),
        lax.psum_scatter(
            gate_up_grad.astype(jnp.bfloat16), "fsdp", scatter_dimension=0, tiled=True
        ).astype(jnp.float32),
        lax.psum_scatter(
            down_grad.astype(jnp.bfloat16), "fsdp", scatter_dimension=1, tiled=True
        ).astype(jnp.float32),
    )
    gains_grad = lax.psum_scatter(
        jnp.stack([gain_one, gain_two, gain_three, gain_four], axis=0),
        ("fsdp", "tp"),
        scatter_dimension=1,
        tiled=True,
    )
    project_new, project_mean_new, project_power_new, unused_one = adam_step(
        project_weight, project_grad, project_mean, project_power
    )
    output_new, output_mean_new, output_power_new, unused_two = adam_step(
        output_weight, output_grad, output_mean, output_power
    )
    gate_up_new, gate_up_mean_new, gate_up_power_new, unused_three = adam_step(
        gate_up_weight, gate_up_grad, gate_up_mean, gate_up_power
    )
    down_new, down_mean_new, down_power_new, unused_four = adam_step(
        down_weight, down_grad, down_mean, down_power
    )
    unused_five, gains_mean_new, gains_power_new, gains_step = adam_step(
        norm_gains, gains_grad, gains_mean, gains_power
    )
    return (
        layer_output.astype(half_type),
        input_grad,
        project_grad,
        project_new,
        project_mean_new,
        project_power_new,
        output_grad,
        output_new,
        output_mean_new,
        output_power_new,
        gate_up_grad,
        gate_up_new,
        gate_up_mean_new,
        gate_up_power_new,
        down_grad,
        down_new,
        down_mean_new,
        down_power_new,
        gains_grad,
        gains_step,
        gains_mean_new,
        gains_power_new,
    )


def solution(mesh):
    in_specs = (
        P(("fsdp", "tp"), None),
        P("fsdp"),
        P(("fsdp", "tp"), None),
        P("fsdp", "tp", None, None),
        P("tp", "fsdp"),
        P("fsdp", None, "tp"),
        P("tp", "fsdp"),
        P(None, ("fsdp", "tp")),
        P("fsdp", "tp", None, None),
        P("fsdp", "tp", None, None),
        P("tp", "fsdp"),
        P("tp", "fsdp"),
        P("fsdp", None, "tp"),
        P("fsdp", None, "tp"),
        P("tp", "fsdp"),
        P("tp", "fsdp"),
        P(None, ("fsdp", "tp")),
        P(None, ("fsdp", "tp")),
    )
    out_specs = (
        P(("fsdp", "tp"), None),
        P(("fsdp", "tp"), None),
        P("fsdp", "tp", None, None),
        P("fsdp", "tp", None, None),
        P("fsdp", "tp", None, None),
        P("fsdp", "tp", None, None),
        P("tp", "fsdp"),
        P("tp", "fsdp"),
        P("tp", "fsdp"),
        P("tp", "fsdp"),
        P("fsdp", None, "tp"),
        P("fsdp", None, "tp"),
        P("fsdp", None, "tp"),
        P("fsdp", None, "tp"),
        P("tp", "fsdp"),
        P("tp", "fsdp"),
        P("tp", "fsdp"),
        P("tp", "fsdp"),
        P(None, ("fsdp", "tp")),
        P(None, ("fsdp", "tp")),
        P(None, ("fsdp", "tp")),
        P(None, ("fsdp", "tp")),
    )
    return jax.shard_map(
        per_device, mesh=mesh, in_specs=in_specs, out_specs=out_specs, check_vma=False
    )
```

profile of v0, /device:TPU:1, one launch (start us, length us, event | category | flops | bytes accessed | tf_op | source)
XLA Modules:
  0.0 1814.7 jit_solution(12845876142496261712)
XLA Ops:
  7.3 2.3 convert_element_type.132
  9.7 44.0 %all-gather = f32[32,72,4]{1,2,0:T(4,128)S(1)} all-gather(f32[1,72,4]{1,2,0:T(4,128)S(1)} %bitcast.210), channel_id=1, replica_groups=mesh['fsdp'=8,'tp'=4] {'fsdp','tp'}, dimensions={0}, use_global_device_ids=true | all-gather | bytes 38016 | tf_op jit(solution)/shard_map/all_gather | solution.py:151
  57.7 34.3 %all-gather.12.cloned.1.call-done = bf16[2304,1,4,256]{3,2,1,0:T(4,128)(2,1)} async-done(((bf16[288,1,4,256]{3,2,1,0:T(4,128)(2,1)}), bf16[2304,1,4,256]{3,2,1,0:T(4,128)(2,1)}) %all-gather.12.cloned.1.call-update) | async-done | bytes 4718608 | tf_op jit(solution)/shard_map/all_gather | solution.py:153
  92.0 8.4 copy.104
  100.4 17.4 all-gather.10.cloned.1.call-done
  117.8 5.2 fusion.36
  127.8 43.2 %all-gather.14.cloned.1.call-done = bf16[512,2304]{0,1:T(8,128)(2,1)} async-done(((bf16[512,288]{0,1:T(8,128)(2,1)}), bf16[512,2304]{0,1:T(8,128)(2,1)}) %all-gather.14.cloned.1.call-update) | async-done | bytes 2359312 | tf_op jit(solution)/shard_map/all_gather | solution.py:154
  171.1 5.3 fusion.111
  176.4 47.7 %reduce-scatter.10.cloned.1.call-done = f32[128,2304]{1,0:T(8,128)} async-done(((f32[512,2304]{1,0:T(8,128)}), f32[128,2304]{1,0:T(8,128)}) %reduce-scatter.10.cloned.1.call-update) | async-done | bytes 1179664 | tf_op jit(solution)/shard_map/reduce_scatter | solution.py:184
  228.3 4.3 copy.171
  232.7 2.9 convert_element_type.144
  235.9 17.0 all-gather.16.cloned.1.call-done
  252.9 408.4 %all-gather.18.cloned.1.call-done = bf16[2304,2,2304]{2,0,1:T(8,128)(2,1)} async-done(((bf16[288,2,2304]{2,0,1:T(8,128)(2,1)}), bf16[2304,2,2304]{2,0,1:T(8,128)(2,1)}) %all-gather.18.cloned.1.call-update) | async-done | bytes 21233680 | tf_op jit(solution)/shard_map/all_gather | solution.py:155
  661.3 15.2 fusion.19
  676.5 3.5 copy-done.6
  680.0 2.6 multiply_convert_fusion.1
  682.6 133.7 %all-gather.20.cloned.1.call-done = bf16[2304,2304]{0,1:T(8,128)(2,1)} async-done(((bf16[2304,288]{0,1:T(8,128)(2,1)}), bf16[2304,2304]{0,1:T(8,128)(2,1)}) %all-gather.20.cloned.1.call-update) | async-done | bytes 10616848 | tf_op jit(solution)/shard_map/all_gather | solution.py:156
  816.3 11.7 fusion.112
  828.1 46.5 %reduce-scatter.12.cloned.1.call-done = f32[128,2304]{1,0:T(8,128)} async-done(((f32[512,2304]{1,0:T(8,128)}), f32[128,2304]{1,0:T(8,128)}) %reduce-scatter.12.cloned.1.call-update) | async-done | bytes 1179664 | tf_op jit(solution)/shard_map/reduce_scatter | solution.py:198
  876.2 2.3 fusion.56
  880.3 24.3 %all-gather.22.cloned.1.call-done = bf16[512,2304]{1,0:T(8,128)(2,1)} async-done(((bf16[128,2304]{1,0:T(8,128)(2,1)}), bf16[512,2304]{1,0:T(8,128)(2,1)}) %all-gather.22.cloned.1.call-update) | async-done | bytes 2359312 | tf_op jit(solution)/shard_map/all_gather | solution.py:208
  904.6 14.2 fusion.23
  921.0 15.8 convolution_bitcast_fusion.1
  936.8 47.5 %reduce-scatter.14.cloned.1.call-done = f32[128,2304]{1,0:T(8,128)} async-done(((f32[512,2304]{1,0:T(8,128)}), f32[128,2304]{1,0:T(8,128)}) %reduce-scatter.14.cloned.1.call-update) | async-done | bytes 1179664 | tf_op jit(solution)/shard_map/reduce_scatter | solution.py:221
  984.4 2.3 multiply_reduce_fusion
  990.7 24.1 %all-gather.24.cloned.1.call-done = bf16[512,2304]{1,0:T(8,128)(2,1)} async-done(((bf16[128,2304]{1,0:T(8,128)(2,1)}), bf16[512,2304]{1,0:T(8,128)(2,1)}) %all-gather.24.cloned.1.call-update) | async-done | bytes 2359312 | tf_op jit(solution)/shard_map/all_gather | solution.py:232
  1014.8 3.8 convolution_convert_fusion.5
  1018.6 2.0 fusion.25
  1026.9 3.9 fusion.13
  1031.8 4.5 convolution_convert_fusion.3
  1038.0 10.1 convolution_convert_fusion.1
  1049.2 6.1 fusion.2
  1056.9 17.1 convolution_convert_fusion
  1076.4 39.5 %all-reduce = f32[4,2304]{1,0:T(4,128)S(1)} all-reduce(f32[4,2304]{1,0:T(4,128)S(1)} %pad_maximum_fusion.6), channel_id=10, replica_groups=mesh['fsdp'=8,'tp'=4] {'fsdp','tp'}, use_global_device_ids=true, to_apply=%region_23.24.clone | all-reduce | flops 9216 | bytes 73728
  1117.2 19.0 %reduce-scatter.20.cloned.1.call-done = bf16[512,288]{0,1:T(8,128)(2,1)} async-done(((bf16[512,2304]{0,1:T(8,128)(2,1)}), bf16[512,288]{0,1:T(8,128)(2,1)}) %reduce-scatter.20.cloned.1.call-update) | async-done | bytes 294928 | tf_op jit(solution)/shard_map/reduce_scatter | solution.py:266
  1136.2 2.7 multiply_add_fusion.4
  1140.4 179.3 %reduce-scatter.24.cloned.1.call-done = bf16[2304,288]{0,1:T(8,128)(2,1)} async-done(((bf16[2304,2304]{0,1:T(8,128)(2,1)}), bf16[2304,288]{0,1:T(8,128)(2,1)}) %reduce-scatter.24.cloned.1.call-update) | async-done | bytes 1327120 | tf_op jit(solution)/shard_map/reduce_scatter | solution.py:272
  1319.7 8.3 multiply_add_fusion.1
  1328.0 90.5 %reduce-scatter.18.cloned.1.call-done = bf16[288,1,4,256]{3,0,2,1:T(8,128)(2,1)} async-done(((bf16[2304,1,4,256]{3,0,2,1:T(8,128)(2,1)}), bf16[288,1,4,256]{3,0,2,1:T(8,128)(2,1)}) %reduce-scatter.18.cloned.1.call-update) | async-done | bytes 589840 | tf_op jit(solution)/shard_map/reduce_scatter | solution.py:263
  1418.5 2.6 multiply_add_fusion.3
  1421.1 1.8 copy.128
  1422.9 1.8 copy.129
  1427.9 342.1 %reduce-scatter.22.cloned.1.call-done = bf16[288,2,2304]{2,0,1:T(8,128)(2,1)} async-done(((bf16[2304,2,2304]{2,0,1:T(8,128)(2,1)}), bf16[288,2,2304]{2,0,1:T(8,128)(2,1)}) %reduce-scatter.22.cloned.1.call-update) | async-done | bytes 2654224 | tf_op jit(solution)/shard_map/reduce_scatter | solution.py:269
  1770.0 10.4 multiply_add_fusion
  1780.4 9.0 copy.132
  1789.4 6.5 copy.133
  1795.9 6.7 copy.134
  1802.6 5.1 copy.131
  (218 shorter events, 42.4 us)
Async XLA Ops:
  7.2 46.7 %copy-start.1 = (bf16[128,2304]{1,0:T(8,128)(2,1)S(1)}, bf16[128,2304]{1,0:T(8,128)(2,1)}, u32[]{:S(2)}) copy-start(bf16[128,2304]{1,0:T(8,128)(2,1)} %param.18) | copy-start | bytes 1769476
  7.2 84.8 %all-gather.12.cloned.1.call-start = ((), (), s32[]{:S(2)}) async-start(), calls=%async_computation.9 | async-start | bytes 5308416 | tf_op jit(solution)/shard_map/all_gather | solution.py:153
  9.6 46.0 %copy-start.12 = (f32[512,288]{0,1:T(8,128)S(1)}, f32[512,288]{0,1:T(8,128)}, u32[]{:S(2)}) copy-start(f32[512,288]{0,1:T(8,128)} %param.22) | copy-start | bytes 1769476
  9.6 46.8 %copy-start.47 = (s32[512]{0:T(512)S(1)}, s32[512]{0:T(512)}, u32[]{:S(2)}) copy-start(s32[512]{0:T(512)} %param.19) | copy-start | bytes 6148
  9.6 108.1 %all-gather.10.cloned.1.call-start = ((), (), s32[]{:S(2)}) async-start(), calls=%async_computation.8 | async-start | bytes 2949120 | tf_op jit(solution)/shard_map/all_gather | solution.py:160
  53.9 173.3 %copy-start.40 = (f32[2304]{0:T(1024)}, f32[2304]{0:T(1024)S(1)}, u32[]{:S(2)}) copy-start(f32[2304]{0:T(1024)S(1)} %get-tuple-element.148) | copy-start | bytes 27652
  55.6 115.5 %all-gather.14.cloned.1.call-start = ((), (), s32[]{:S(2)}) async-start(), calls=%async_computation.10 | async-start | bytes 2654208 | tf_op jit(solution)/shard_map/all_gather | solution.py:154
  56.4 167.7 %reduce-scatter.10.cloned.1.call-start = ((), (), s32[]{:S(2)}) async-start(), calls=%async_computation.11 | async-start | bytes 5898240 | tf_op jit(solution)/shard_map/reduce_scatter | solution.py:184
  56.5 66.6 %copy-start.52 = (f32[128]{0:T(128)}, f32[128]{0:T(128)S(1)}, u32[]{:S(2)}) copy-start(f32[128]{0:T(128)S(1)} %multiply_power_fusion) | copy-start | bytes 1540
  56.7 69.4 %copy-start.21 = (pred[512,512]{0,1:T(8,128)(4,1)}, pred[512,512]{0,1:T(8,128)(4,1)S(1)}, u32[]{:S(2)}) copy-start(pred[512,512]{0,1:T(8,128)(4,1)S(1)} %fusion.70) | copy-start | bytes 786436
  57.7 66.6 %copy-start.15 = (f32[512,128]{0,1:T(8,128)}, f32[512,128]{0,1:T(8,128)S(1)}, u32[]{:S(2)}) copy-start(f32[512,128]{0,1:T(8,128)S(1)} %get-tuple-element.184) | copy-start | bytes 786436
  57.7 66.6 %copy-start.17 = (f32[512,128]{0,1:T(8,128)}, f32[512,128]{0,1:T(8,128)S(1)}, u32[]{:S(2)}) copy-start(f32[512,128]{0,1:T(8,128)S(1)} %get-tuple-element.185) | copy-start | bytes 786436
  123.0 3.1 copy-start.27
  127.8 48.5 %copy-start.34 = (bf16[256,2,512]{2,0,1:T(8,128)(2,1)}, bf16[256,2,512]{2,0,1:T(8,128)(2,1)S(1)}, u32[]{:S(2)}) copy-start(bf16[256,2,512]{2,0,1:T(8,128)(2,1)S(1)} %convolution_convert_fusion.4) | copy-start | bytes 1572868
  176.4 76.5 %all-gather.16.cloned.1.call-start = ((), (), s32[]{:S(2)}) async-start(), calls=%async_computation.12 | async-start | bytes 2949120 | tf_op jit(solution)/shard_map/all_gather | solution.py:193
  227.2 5.4 copy-start.54
  228.2 433.0 %all-gather.18.cloned.1.call-start = ((), (), s32[]{:S(2)}) async-start(), calls=%async_computation.13 | async-start | bytes 23887872 | tf_op jit(solution)/shard_map/all_gather | solution.py:155
  232.6 583.7 %all-gather.20.cloned.1.call-start = ((), (), s32[]{:S(2)}) async-start(), calls=%async_computation.14 | async-start | bytes 11943936 | tf_op jit(solution)/shard_map/all_gather | solution.py:156
  235.6 639.0 %reduce-scatter.12.cloned.1.call-start = ((), (), s32[]{:S(2)}) async-start(), calls=%async_computation.15 | async-start | bytes 5898240 | tf_op jit(solution)/shard_map/reduce_scatter | solution.py:198
  676.5 3.5 copy-start.6
  828.0 48.2 %copy-start.9 = (bf16[128,2304]{1,0:T(8,128)(2,1)S(1)}, bf16[128,2304]{1,0:T(8,128)(2,1)}, u32[]{:S(2)}) copy-start(bf16[128,2304]{1,0:T(8,128)(2,1)} %param.20) | copy-start | bytes 1769476
  828.0 76.6 %all-gather.22.cloned.1.call-start = ((), (), s32[]{:S(2)}) async-start(), calls=%async_computation.16 | async-start | bytes 2949120 | tf_op jit(solution)/shard_map/all_gather | solution.py:208
  874.6 3.9 copy-start.5
  880.0 104.4 %reduce-scatter.14.cloned.1.call-start = ((), (), s32[]{:S(2)}) async-start(), calls=%async_computation.17 | async-start | bytes 5898240 | tf_op jit(solution)/shard_map/reduce_scatter | solution.py:221
  936.8 49.9 %copy-start = (f32[128,2304]{1,0:T(8,128)S(1)}, f32[128,2304]{1,0:T(8,128)}, u32[]{:S(2)}) copy-start(f32[128,2304]{1,0:T(8,128)} %reduce-scatter.10.cloned.1.call-done) | copy-start | bytes 3538948
  936.8 78.0 %all-gather.24.cloned.1.call-start = ((), (), s32[]{:S(2)}) async-start(), calls=%async_computation.18 | async-start | bytes 2949120 | tf_op jit(solution)/shard_map/all_gather | solution.py:232
  990.1 84.7 %reduce-scatter.16.cloned.1.call-start = ((), (), s32[]{:S(2)}) async-start(), calls=%async_computation.19 | async-start | bytes 2949120 | tf_op jit(solution)/shard_map/reduce_scatter | solution.py:252
  990.7 27.9 %copy-start.8 = (f32[512,512,2]{1,0,2:T(8,128)S(1)}, f32[512,512,2]{1,0,2:T(8,128)}, u32[]{:S(2)}) copy-start(f32[512,512,2]{1,0,2:T(8,128)} %copy-done.7) | copy-start | bytes 6291460
  990.7 27.9 %copy-start.22 = (pred[512,512]{0,1:T(8,128)(4,1)S(1)}, pred[512,512]{0,1:T(8,128)(4,1)}, u32[]{:S(2)}) copy-start(pred[512,512]{0,1:T(8,128)(4,1)} %copy-done.21) | copy-start | bytes 786436
  1021.6 4.6 copy-start.62
  1021.6 5.3 slice-start
  1022.9 4.0 slice-start.1
  1030.8 105.4 %reduce-scatter.20.cloned.1.call-start = ((), (), s32[]{:S(2)}) async-start(), calls=%async_computation.21 | async-start | bytes 2654208 | tf_op jit(solution)/shard_map/reduce_scatter | solution.py:266
  1036.3 283.4 %reduce-scatter.24.cloned.1.call-start = ((), (), s32[]{:S(2)}) async-start(), calls=%async_computation.23 | async-start | bytes 11943936 | tf_op jit(solution)/shard_map/reduce_scatter | solution.py:272
  1048.1 370.4 %reduce-scatter.18.cloned.1.call-start = ((), (), s32[]{:S(2)}) async-start(), calls=%async_computation.20 | async-start | bytes 5308416 | tf_op jit(solution)/shard_map/reduce_scatter | solution.py:263
  1055.3 714.7 %reduce-scatter.22.cloned.1.call-start = ((), (), s32[]{:S(2)}) async-start(), calls=%async_computation.22 | async-start | bytes 23887872 | tf_op jit(solution)/shard_map/reduce_scatter | solution.py:269
  1074.1 42.4 %copy-start.49 = (f32[4,72]{1,0:T(4,128)S(1)}, f32[4,72]{1,0:T(4,128)}, u32[]{:S(2)}) copy-start(f32[4,72]{1,0:T(4,128)} %param.25) | copy-start | bytes 3460
  1074.1 42.4 %copy-start.58 = (f32[4,72]{1,0:T(4,128)S(1)}, f32[4,72]{1,0:T(4,128)}, u32[]{:S(2)}) copy-start(f32[4,72]{1,0:T(4,128)} %param.34) | copy-start | bytes 3460
  1074.1 42.4 %copy-start.59 = (f32[4,72]{1,0:T(4,128)S(1)}, f32[4,72]{1,0:T(4,128)}, u32[]{:S(2)}) copy-start(f32[4,72]{1,0:T(4,128)} %param.35) | copy-start | bytes 3460
  1074.1 62.1 %copy-start.13 = (f32[512,288]{0,1:T(8,128)S(1)}, f32[512,288]{0,1:T(8,128)}, u32[]{:S(2)}) copy-start(f32[512,288]{0,1:T(8,128)} %param.22) | copy-start | bytes 1769476
  1074.1 62.1 %copy-start.29 = (f32[512,288]{0,1:T(8,128)S(1)}, f32[512,288]{0,1:T(8,128)}, u32[]{:S(2)}) copy-start(f32[512,288]{0,1:T(8,128)} %param.28) | copy-start | bytes 1769476
  1117.2 21.8 %copy-start.4 = (f32[128,2304]{1,0:T(8,128)S(1)}, f32[128,2304]{1,0:T(8,128)}, u32[]{:S(2)}) copy-start(f32[128,2304]{1,0:T(8,128)} %copy-done.3) | copy-start | bytes 3538948
  1117.2 21.8 %copy-start.14 = (bf16[128,2304]{1,0:T(8,128)(2,1)S(1)}, bf16[128,2304]{1,0:T(8,128)(2,1)}, u32[]{:S(2)}) copy-start(bf16[128,2304]{1,0:T(8,128)(2,1)} %reduce-scatter.16.cloned.1.call-done) | copy-start | bytes 1769476
  1136.2 2.7 copy-start.60
  1140.4 278.1 %copy-start.11 = (f32[288,1,4,256]{3,2,1,0:T(4,128)S(1)}, f32[288,1,4,256]{3,2,1,0:T(4,128)}, u32[]{:S(2)}) copy-start(f32[288,1,4,256]{3,2,1,0:T(4,128)} %param.21) | copy-start | bytes 3538948
  1140.4 278.1 %copy-start.28 = (f32[288,1,4,256]{3,2,1,0:T(4,128)S(1)}, f32[288,1,4,256]{3,2,1,0:T(4,128)}, u32[]{:S(2)}) copy-start(f32[288,1,4,256]{3,2,1,0:T(4,128)} %param.26) | copy-start | bytes 3538948
  1422.9 3.6 copy-start.20
  1795.9 6.7 copy-start.2
  (36 other events, 51.0 us)
Sparse Core Ops, SparseCore 0:
  10.8 81.1 all-gather.11
  94.1 23.6 all-gather.9
  120.5 50.4 all-gather.13
  176.5 47.5 reduce-scatter.9
  228.4 24.4 all-gather.15
  254.9 406.2 all-gather.17
  664.3 152.0 all-gather.19
  828.2 46.4 reduce-scatter.11
  880.1 24.4 all-gather.21
  936.9 47.4 reduce-scatter.13
  990.2 24.4 all-gather.23
  1030.9 32.6 reduce-scatter.15
  1067.7 68.4 reduce-scatter.19
  1139.6 180.0 reduce-scatter.23
  1324.2 94.2 reduce-scatter.17
  1422.7 347.2 reduce-scatter.21
where the time goes:
time: 1820 us; the launch traced here: 1810 us
  waiting for transfers between devices  1480 us (81%)
  matrix products  118 us (6%)
  blocking collectives  83.5 us (5%)
  local copies, waits for them, and re-layouts  62.6 us (3%)
  other arithmetic  57.8 us (3%)
    all_gather x1, waiting for transfers between devices, per_device(): lax.all_gather(gate_up_weight.astype(half_type), 'fsdp', axis=0, tiled=True)  408 us
    reduce_scatter x1, waiting for transfers between devices, per_device(): lax.psum_scatter(gate_up_grad.astype(jnp.bfloat16), 'fsdp', scatter_dimen...  342 us
    reduce_scatter x1, waiting for transfers between devices, per_device(): lax.psum_scatter(down_grad.astype(jnp.bfloat16), 'fsdp', scatter_dimensio...  179 us
    all_gather x1, waiting for transfers between devices, per_device(): lax.all_gather(down_weight.astype(half_type), 'fsdp', axis=1, tiled=True)  134 us
    reduce_scatter x1, waiting for transfers between devices, per_device(): lax.psum_scatter(project_grad.astype(jnp.bfloat16), 'fsdp', scatter_dimen...  90.5 us
    unnamed x146, local copies, waits for them, and re-layouts  54 us
    reduce_scatter x1, waiting for transfers between devices, per_device(): lax.psum_scatter(jnp.dot(context_flat, full_output, preferred_element_typ...  47.7 us
    reduce_scatter x1, waiting for transfers between devices, per_device(): lax.psum_scatter(jnp.einsum('rjf,djf->rd', gate_up_slope, full_gate_up, p...  47.5 us
  transfers between devices with their start and end apart: 16, of which 15 were waited for; matrix products, arithmetic and copies ran while one was open for 6% of the time, Pallas kernels for 0%

commit v1 on v0

v1 whole, which is shorter than its diff:
```python
import jax
import jax.numpy as jnp
from jax import lax
from jax.sharding import Mesh
from jax.sharding import PartitionSpec as P

SEQ = 512

norm_eps = 1e-06
soft_cap = 50.0
rope_base = 10000.0
beta_first = 0.9
beta_second = 0.95
learn_rate = 0.02
decay_rate = 0.1
adam_eps = 1e-08
step_number = 3.0

F32 = jnp.float32
BF16 = jnp.bfloat16


def norm_forward(values, gain_vec):
    factor = lax.rsqrt(jnp.mean(values * values, axis=-1, keepdims=True) + norm_eps)
    return (values * factor * gain_vec, factor)


def norm_backward(values, factor, gain_vec, incoming):
    unit_rows = values * factor
    gain_part = jnp.sum(incoming * unit_rows, axis=0)
    scaled = incoming * gain_vec
    return (
        factor * (scaled - unit_rows * jnp.mean(scaled * unit_rows, axis=-1, keepdims=True)),
        gain_part,
    )


def rotate(values, cosine_table, sine_table):
    half_width = values.shape[-1] // 2
    first_half = values[..., :half_width]
    second_half = values[..., half_width:]
    return jnp.concatenate(
        [
            first_half * cosine_table - second_half * sine_table,
            second_half * cosine_table + first_half * sine_table,
        ],
        axis=-1,
    )


def unrotate(slopes, cosine_table, sine_table):
    return rotate(slopes, cosine_table, -sine_table)


def adam_step(weight, gradient, mean_old, power_old):
    mean_new = beta_first * mean_old + (1.0 - beta_first) * gradient
    power_new = beta_second * power_old + (1.0 - beta_second) * gradient * gradient
    mean_hat = mean_new / (1.0 - beta_first**step_number)
    power_hat = power_new / (1.0 - beta_second**step_number)
    change = -learn_rate * (mean_hat / (jnp.sqrt(power_hat) + adam_eps) + decay_rate * weight)
    return (weight + change, mean_new, power_new, change)


def swap(value, axis):
    return lax.ppermute(value, axis, [(0, 1), (1, 0)])


def from_ahead(value, axis, size, step):
    return lax.ppermute(value, axis, [(j, (j - step) % size) for j in range(size)])


def swap_two(value, first, second):
    return lax.ppermute(value, (first, second), [(0, 3), (3, 0), (1, 2), (2, 1)])


def ordered(own, other, place):
    straight = jnp.stack([own, other])
    return jnp.where(place == 0, straight, straight[::-1])


def rolled(value, place, axis):
    count = value.shape[axis]
    result = value
    for step in range(1, count):
        result = jnp.where(place == step, jnp.roll(value, -step, axis), result)
    return result


def make_device(far_size):
    def per_device(
        inputs,
        segments,
        cotangent,
        project_weight,
        output_weight,
        gate_up_weight,
        down_weight,
        norm_gains,
        project_mean,
        project_power,
        output_mean,
        output_power,
        gate_up_mean,
        gate_up_power,
        down_mean,
        down_power,
        gains_mean,
        gains_power,
    ):
        far, near, side, row, core = (lax.axis_index(name) for name in ("zh", "zl", "x", "y", "c"))
        own_rows, width = inputs.shape
        block = project_weight.shape[0]
        head_width = project_weight.shape[3]
        slots = project_weight.shape[2]
        group_size = slots - 2
        kv_local = project_weight.shape[1]
        mix_width = kv_local * slots * head_width
        context_width = output_weight.shape[0]
        hidden = down_weight.shape[0]
        half = hidden // 2
        total_rows = 4 * own_rows
        seq_count = total_rows // SEQ

        def arrange(value):
            lead = value.shape[0]
            value = value.reshape(lead, far_size, 2, 2, block).transpose(0, 3, 1, 2, 4)
            return rolled(rolled(value, side, 1), far, 2).reshape(lead, width)

        def unarrange(value):
            lead = value.shape[0]
            value = value.reshape(lead, 2, far_size, 2, block)
            value = rolled(rolled(value, side, 1), (far_size - far) % far_size, 2)
            return value.transpose(0, 2, 3, 1, 4).reshape(lead, width)

        attend_own = jnp.concatenate(
            [project_weight.astype(BF16).reshape(block, mix_width), output_weight.astype(BF16).T],
            axis=1,
        )
        rows_own = arrange(inputs)

        def gather_sequence(value):
            there = swap(value, "y")
            return jnp.concatenate([value, swap(value, "c"), there, swap(there, "c")], axis=0)

        def scatter_sequence(partial):
            part = partial.reshape(2, 2, own_rows, width)
            mine = part[:, 0] + swap(part[:, 1].astype(BF16), "c").astype(F32)
            return mine[0] + swap(mine[1].astype(BF16), "y").astype(F32)

        def gather_group(value):
            cross = [value, swap(value, "y"), swap(value, "zl"), swap_two(value, "zl", "y")]
            outer = swap(jnp.concatenate(cross[1:], axis=0), "c")
            inner = swap(value, "c")
            parts = [value, inner]
            for place in range(3):
                parts += [cross[place + 1], outer[place * own_rows : (place + 1) * own_rows]]
            return jnp.concatenate(parts, axis=0)

        def scatter_group(partial):
            part = partial.reshape(2, 2, 2, own_rows, width)
            mine = part[:, :, 0] + swap(part[:, :, 1].astype(BF16), "c").astype(F32)
            low = mine.astype(BF16)
            return (
                mine[0, 0]
                + swap(low[0, 1], "y").astype(F32)
                + swap(low[1, 0], "zl").astype(F32)
                + swap_two(low[1, 1], "zl", "y").astype(F32)
            )

        rows_in = gather_sequence(rows_own)

        gains_parts = norm_gains[None]
        for axis, place in (("c", core), ("y", row)):
            gains_parts = ordered(gains_parts, swap(gains_parts, axis), place)
        gains_parts = gains_parts.reshape((4,) + norm_gains.shape)
        gains_parts = ordered(gains_parts, swap(gains_parts, "zl"), near)
        gains_parts = jnp.stack(
            [gains_parts]
            + [from_ahead(gains_parts, "zh", far_size, step) for step in range(1, far_size)]
        )
        gains_parts = jnp.stack([gains_parts, swap(gains_parts, "x")])
        gains_all = gains_parts.reshape(-1, 4, norm_gains.shape[1]).transpose(1, 0, 2).reshape(4, width)

        attend_far = [attend_own] + [
            from_ahead(attend_own, "zh", far_size, step) for step in range(1, far_size)
        ]
        attend_side = [attend_far, [swap(piece, "x") for piece in attend_far]]
        attend_all = jnp.concatenate(
            [
                ordered(piece, swap(piece, "zl"), near).reshape(2 * block, mix_width + context_width)
                for pieces in attend_side
                for piece in pieces
            ],
            axis=0,
        )
        full_project = attend_all[:, :mix_width]
        full_output = attend_all[:, mix_width:]

        def collect(weight):
            halves = [weight[:, :half], weight[:, half:]]
            keep = jnp.where(near == 0, halves[0], halves[1])
            send = jnp.where(near == 0, halves[1], halves[0])
            own = ordered(keep, swap(send, "zl"), near).reshape(2 * block, half)
            pieces = [own] + [from_ahead(own, "zh", far_size, step) for step in range(1, far_size)]
            return jnp.concatenate(pieces + [swap(piece, "x") for piece in pieces], axis=0)

        full_gate = collect(gate_up_weight[:, 0].astype(BF16))
        full_up = collect(gate_up_weight[:, 1].astype(BF16))
        full_down = collect(down_weight.astype(BF16).T)

        residual_in = rows_own.astype(F32)
        factor_one = lax.rsqrt(jnp.mean(residual_in * residual_in, axis=-1, keepdims=True) + norm_eps)
        rows_one = norm_forward(rows_in.astype(F32), gains_all[0])[0].astype(BF16)
        mixed_rows = jnp.dot(rows_one, full_project, preferred_element_type=F32)
        query_scale = head_width ** (-0.5)
        start = jnp.stack(
            [
                ((row ^ dr) * 2 + (core ^ dc)) * own_rows
                for dr in range(2)
                for dc in range(2)
            ]
        )
        order = (start[:, None] + jnp.arange(own_rows)[None, :]).reshape(total_rows)
        seg_parts = segments.reshape(2, 2, own_rows)
        seg_parts = rolled(rolled(seg_parts, row, 0), core, 1)
        seg_rows = seg_parts.reshape(total_rows)
        places = order % SEQ
        half_width = head_width // 2
        frequency = rope_base ** (-2.0 * jnp.arange(half_width, dtype=F32) / head_width)
        angles = places.astype(F32)[:, None] * frequency[None, :]
        cosine_table, sine_table = jnp.cos(angles), jnp.sin(angles)
        shaped = mixed_rows.reshape(total_rows, kv_local, slots, head_width)
        cosine_query = cosine_table[:, None, None, :]
        sine_query = sine_table[:, None, None, :]
        cosine_key = cosine_table[:, None, :]
        sine_key = sine_table[:, None, :]
        queries = (rotate(shaped[:, :, :group_size], cosine_query, sine_query) * query_scale).astype(BF16)
        key_vectors = rotate(shaped[:, :, group_size], cosine_key, sine_key).astype(BF16)
        value_rows = shaped[:, :, group_size + 1].astype(BF16)
        allowed = (
            (seg_rows[:, None] == seg_rows[None, :])
            & (order[None, :] <= order[:, None])
            & (order[None, :] // SEQ == order[:, None] // SEQ)
        )

        scores = jnp.einsum("qhgd,khd->hgqk", queries, key_vectors, preferred_element_type=F32)
        tanh_value = jnp.tanh(scores / soft_cap)
        capped = jnp.where(allowed, soft_cap * tanh_value, -jnp.inf)
        row_max = jnp.max(capped, axis=-1, keepdims=True)
        exp_scores = jnp.exp(capped - row_max)
        row_total = jnp.sum(exp_scores, axis=-1, keepdims=True)
        prob_values = exp_scores / row_total
        context = jnp.einsum(
            "hgqk,khd->qhgd", prob_values.astype(BF16), value_rows, preferred_element_type=F32
        )
        context_flat = context.astype(BF16).reshape(total_rows, context_width)
        attend_sum = scatter_sequence(
            lax.dot_general(
                context_flat, full_output, (((1,), (1,)), ((), ())), preferred_element_type=F32
            )
        )
        post_one, factor_two = norm_forward(attend_sum, gains_all[1])
        hidden_state = residual_in + post_one
        normed_two, factor_three = norm_forward(hidden_state, gains_all[2])

        rows_two = gather_group(normed_two.astype(BF16))
        gate_value = jnp.dot(rows_two, full_gate, preferred_element_type=F32)
        up_value = jnp.dot(rows_two, full_up, preferred_element_type=F32)

        def gelu_product(gate_in, up_in):
            return jax.nn.gelu(gate_in, approximate=True) * up_in

        activated = gelu_product(gate_value, up_value).astype(BF16)
        feed_sum = scatter_group(
            lax.dot_general(activated, full_down, (((1,), (1,)), ((), ())), preferred_element_type=F32)
        )
        post_two, factor_four = norm_forward(feed_sum, gains_all[3])
        layer_output = unarrange((hidden_state + post_two).astype(BF16))

        upstream = arrange(cotangent).astype(F32)
        feed_slope, gain_four = norm_backward(feed_sum, factor_four, gains_all[3], upstream)
        feed_slope_rows = gather_group(feed_slope.astype(BF16))
        activated_slope = jnp.dot(feed_slope_rows, full_down, preferred_element_type=F32)
        unused_value, gelu_pull = jax.vjp(gelu_product, gate_value, up_value)
        gate_slope, up_slope = gelu_pull(activated_slope)
        gate_slope = gate_slope.astype(BF16)
        up_slope = up_slope.astype(BF16)
        contract_last = (((1,), (1,)), ((), ()))
        normed_two_slope = scatter_group(
            lax.dot_general(gate_slope, full_gate, contract_last, preferred_element_type=F32)
            + lax.dot_general(up_slope, full_up, contract_last, preferred_element_type=F32)
        )

        side_rows = width // 2
        far_rows = 2 * block

        def transposed(left, right):
            return lax.dot_general(left, right, (((0,), (0,)), ((), ())), preferred_element_type=F32)

        def reduce_ffn(left, right):
            sent = transposed(left[:, side_rows:], right).astype(BF16)
            kept = transposed(left[:, :side_rows], right)
            total = kept + swap(sent, "x").astype(F32)
            mine = total[:far_rows]
            low = total.astype(BF16)
            for step in range(1, far_size):
                there = low[step * far_rows : (step + 1) * far_rows]
                mine = mine + from_ahead(there, "zh", far_size, far_size - step).astype(F32)
            mine = mine.astype(BF16).reshape(2, block, half)
            keep = jnp.where(near == 0, mine[0], mine[1])
            send = jnp.where(near == 0, mine[1], mine[0])
            other = swap(send, "zl")
            first = jnp.where(near == 0, keep, other)
            second = jnp.where(near == 0, other, keep)
            return jnp.concatenate([first, second], axis=1).astype(F32)

        down_grad = reduce_ffn(feed_slope_rows, activated).T
        gate_grad = reduce_ffn(rows_two, gate_slope)
        up_grad = reduce_ffn(rows_two, up_slope)
        gate_up_grad = jnp.stack([gate_grad, up_grad], axis=1)

        hidden_part, gain_three = norm_backward(
            hidden_state, factor_three, gains_all[2], normed_two_slope
        )
        hidden_slope = upstream + hidden_part
        attend_slope, gain_two = norm_backward(attend_sum, factor_two, gains_all[1], hidden_slope)

        attend_slope_rows = gather_sequence(attend_slope.astype(BF16))
        context_slope = jnp.dot(attend_slope_rows, full_output, preferred_element_type=F32).astype(BF16)
        context_slope = context_slope.reshape(total_rows, kv_local, group_size, head_width)
        prob_slope = jnp.einsum(
            "qhgd,khd->hgqk", context_slope, value_rows, preferred_element_type=F32
        )
        value_slope = jnp.einsum(
            "hgqk,qhgd->khd", prob_values.astype(BF16), context_slope, preferred_element_type=F32
        )
        inner_sum = jnp.sum(prob_values * prob_slope, axis=-1, keepdims=True)
        score_slope = (
            prob_values * (prob_slope - inner_sum) * (1.0 - tanh_value * tanh_value)
        ).astype(BF16)
        query_slope = jnp.einsum(
            "hgqk,khd->qhgd", score_slope, key_vectors, preferred_element_type=F32
        )
        key_slope = jnp.einsum("hgqk,qhgd->khd", score_slope, queries, preferred_element_type=F32)
        query_pre_slope = unrotate(query_slope * query_scale, cosine_query, sine_query)
        key_pre_slope = unrotate(key_slope, cosine_key, sine_key)
        mixed_slope = (
            jnp.concatenate(
                [query_pre_slope, key_pre_slope[:, :, None], value_slope[:, :, None]], axis=2
            )
            .astype(BF16)
            .reshape(total_rows, mix_width)
        )
        normed_one_slope = scatter_sequence(
            lax.dot_general(mixed_slope, full_project, contract_last, preferred_element_type=F32)
        )

        def reduce_attend(left, right):
            columns = right.shape[1]
            lower = transposed(left[:, side_rows:], right).reshape(far_size, 2, block, columns)
            upper = transposed(left[:, :side_rows], right).reshape(far_size, 2, block, columns)

            def over_near(part):
                keep = jnp.where(near == 0, part[:, 0], part[:, 1])
                send = jnp.where(near == 0, part[:, 1], part[:, 0]).astype(BF16)
                return keep + swap(send, "zl").astype(F32)

            lower = over_near(lower)
            upper = over_near(upper)
            total = upper + swap(lower.astype(BF16), "x").astype(F32)
            low = total.astype(BF16)
            mine = total[0]
            for step in range(1, far_size):
                mine = mine + from_ahead(low[step], "zh", far_size, far_size - step).astype(F32)
            return mine

        output_grad = reduce_attend(attend_slope_rows, context_flat).T
        project_grad = reduce_attend(rows_one, mixed_slope).reshape(project_weight.shape)
        input_part, gain_one = norm_backward(residual_in, factor_one, gains_all[0], normed_one_slope)
        input_grad = unarrange(hidden_slope + input_part)

        gain_sum = jnp.stack([gain_one, gain_two, gain_three, gain_four], axis=0)
        gain_sum = gain_sum.reshape(4, 2, far_size, 2, 2, 2, norm_gains.shape[1])
        gain_sum = gain_sum.transpose(1, 2, 3, 4, 5, 0, 6)
        gain_sum = gain_sum[0] + swap(gain_sum[1], "x")
        gain_far = gain_sum[0]
        for step in range(1, far_size):
            gain_far = gain_far + from_ahead(gain_sum[step], "zh", far_size, far_size - step)
        for axis, place in (("zl", near), ("y", row), ("c", core)):
            keep = jnp.where(place == 0, gain_far[0], gain_far[1])
            send = jnp.where(place == 0, gain_far[1], gain_far[0])
            gain_far = keep + swap(send, axis)
        gains_grad = gain_far

        project_new, project_mean_new, project_power_new, unused_one = adam_step(
            project_weight, project_grad, project_mean, project_power
        )
        output_new, output_mean_new, output_power_new, unused_two = adam_step(
            output_weight, output_grad, output_mean, output_power
        )
        gate_up_new, gate_up_mean_new, gate_up_power_new, unused_three = adam_step(
            gate_up_weight, gate_up_grad, gate_up_mean, gate_up_power
        )
        down_new, down_mean_new, down_power_new, unused_four = adam_step(
            down_weight, down_grad, down_mean, down_power
        )
        unused_five, gains_mean_new, gains_power_new, gains_step = adam_step(
            norm_gains, gains_grad, gains_mean, gains_power
        )
        return (
            layer_output,
            input_grad,
            project_grad,
            project_new,
            project_mean_new,
            project_power_new,
            output_grad,
            output_new,
            output_mean_new,
            output_power_new,
            gate_up_grad,
            gate_up_new,
            gate_up_mean_new,
            gate_up_power_new,
            down_grad,
            down_new,
            down_mean_new,
            down_power_new,
            gains_grad,
            gains_step,
            gains_mean_new,
            gains_power_new,
        )

    return per_device


def solution(mesh):
    fsdp_size = mesh.shape["fsdp"]
    far_size = fsdp_size // 4
    fine = Mesh(mesh.devices.reshape(far_size, 2, 2, 2, 2), ("zh", "zl", "x", "y", "c"))
    fsdp = ("zh", "zl", "x")
    tp = ("y", "c")
    both = fsdp + tp
    rows = P(both, None)
    project = P(fsdp, tp, None, None)
    across = P(tp, fsdp)
    gate_up = P(fsdp, None, tp)
    gains = P(None, both)
    in_specs = (
        (rows, P(fsdp), rows, project, across, gate_up, across, gains)
        + (project,) * 2
        + (across,) * 2
        + (gate_up,) * 2
        + (across,) * 2
        + (gains,) * 2
    )
    out_specs = (
        (rows, rows)
        + (project,) * 4
        + (across,) * 4
        + (gate_up,) * 4
        + (across,) * 4
        + (gains,) * 4
    )
    return jax.shard_map(
        make_device(far_size), mesh=fine, in_specs=in_specs, out_specs=out_specs, check_vma=False
    )
```

time: 1820 us -> 1100 us (0.60)
  waiting for transfers between devices: 1480 us -> 667 us
  blocking collectives: 83.5 us -> 0 us
  starting transfers between devices: 1.77 us -> 69.3 us
  local copies, waits for them, and re-layouts: 62.6 us -> 116 us
  other arithmetic: 57.8 us -> 111 us
    reduce_scatter x8 -> x0, waiting for transfers between devices: 773 us -> none  [the longest x1 342 us: per_device(): lax.psum_scatter(gate_up_grad.astype(jnp.bfloat16), 'fsdp', scatter_dimen...]
    all_gather x8 -> x0, waiting for transfers between devices: 702 us -> none  [the longest x1 408 us: per_device(): lax.all_gather(gate_up_weight.astype(half_type), 'fsdp', axis=0, tiled=True)]
    ppermute x0 -> x74, waiting for transfers between devices: none -> 667 us  [the longest x59 384 us: swap(): return lax.ppermute(value, axis, [(0, 1), (1, 0)])]
    ppermute x0 -> x74, starting transfers between devices: none -> 69.3 us  [the longest x59 50.6 us: swap(): return lax.ppermute(value, axis, [(0, 1), (1, 0)])]
    all_gather x1 -> x0, blocking collectives: 44 us -> none  [per_device(): gains_all = lax.all_gather(norm_gains, ('fsdp', 'tp'), axis=1, tiled=True)]
    unnamed x1 -> x0, blocking collectives: 39.5 us -> none
    unnamed x146 -> x346, local copies, waits for them, and re-layouts: 54 us -> 67.7 us
    dot_general x18 -> x26, matrix products: 118 us -> 132 us  [the longest x10 40.7 us: transposed(): lax.dot_general(left, right, (((0,), (0,)), ((), ())), preferred_element_...]
  transfers between devices with their start and end apart: 16 -> 74, of which waited for: 15 -> 37; matrix products, arithmetic and copies ran while one was open for 6% -> 23% of each run, Pallas kernels for 0% -> 0%
where the time goes in v1:
time: 1100 us
  waiting for transfers between devices  667 us (61%)
  matrix products  132 us (12%)
  local copies, waits for them, and re-layouts  116 us (11%)
  other arithmetic  111 us (10%)
  starting transfers between devices  69.3 us (6%)
    ppermute x59, waiting for transfers between devices, swap(): return lax.ppermute(value, axis, [(0, 1), (1, 0)])  384 us
    ppermute x11, waiting for transfers between devices, from_ahead(): lax.ppermute(value, axis, [(j, (j - step) % size) for j in range(size)])  242 us
    unnamed x346, local copies, waits for them, and re-layouts  67.7 us
    ppermute x59, starting transfers between devices, swap(): return lax.ppermute(value, axis, [(0, 1), (1, 0)])  50.6 us
    dot_general x10, matrix products, transposed(): lax.dot_general(left, right, (((0,), (0,)), ((), ())), preferred_element_...  40.7 us
    ppermute x4, waiting for transfers between devices, swap_two(): lax.ppermute(value, (first, second), [(0, 3), (3, 0), (1, 2), (2, 1)])  40.6 us
    add x4, other arithmetic, adam_step(): return (weight + change, mean_new, power_new, change)  23.3 us
  transfers between devices with their start and end apart: 74, of which 37 were waited for; matrix products, arithmetic and copies ran while one was open for 23% of the time, Pallas kernels for 0%

profile of v1, /device:TPU:1, one launch (start us, length us, event | category | flops | bytes accessed | tf_op | source)
XLA Modules:
  0.0 1098.6 jit_solution(5562171694659966864)
XLA Ops:
  25.6 5.8 collective-permute-done.4
  31.6 14.8 %collective-permute-done.5 = f32[4,4,72]{2,1,0:T(4,128)S(1)} collective-permute-done((f32[4,4,72]{2,1,0:T(4,128)S(1)}, f32[4,4,72]{2,1,0:T(4,128)S(1)}, u32[]{:S(2)}, u32[]{:S(2)}) %collective-permute-start.5) | collective-permute-done | bytes 4640 | tf_op jit(solution)/shard_map/ppermute | solution.py:65
  64.6 14.9 %collective-permute-done.13 = bf16[288,1536]{1,0:T(8,128)(2,1)S(1)} collective-permute-done((bf16[288,1536]{1,0:T(8,128)(2,1)}, bf16[288,1536]{1,0:T(8,128)(2,1)S(1)}, u32[]{:S(2)}, u32[]{:S(2)}) %collective-permute-start.13) | collective-permute-done | bytes 884768 | tf_op jit(solution)/shard_map/ppermute | solution.py:65
  80.8 32.0 %collective-permute-done.12 = bf16[288,1536]{1,0:T(8,128)(2,1)S(1)} collective-permute-done((bf16[288,1536]{1,0:T(8,128)(2,1)}, bf16[288,1536]{1,0:T(8,128)(2,1)S(1)}, u32[]{:S(2)}, u32[]{:S(2)}) %collective-permute-start.12) | collective-permute-done | bytes 884768 | tf_op jit(solution)/shard_map/ppermute | solution.py:65
  116.2 15.6 %collective-permute-done.14 = bf16[288,1536]{1,0:T(8,128)(2,1)S(1)} collective-permute-done((bf16[288,1536]{1,0:T(8,128)(2,1)S(1)}, bf16[288,1536]{1,0:T(8,128)(2,1)S(1)}, u32[]{:S(2)}, u32[]{:S(2)}) %collective-permute-start.14) | collective-permute-done | bytes 884768 | tf_op jit(solution)/shard_map/ppermute | solution.py:65
  178.0 7.3 collective-permute-done.16
  193.6 8.2 collective-permute-done.18
  202.0 37.9 %collective-permute-done.19 = bf16[128,2304]{1,0:T(8,128)(2,1)S(1)} collective-permute-done((bf16[128,2304]{1,0:T(8,128)(2,1)S(1)}, bf16[128,2304]{1,0:T(8,128)(2,1)S(1)}, u32[]{:S(2)}, u32[]{:S(2)}) %collective-permute-start.19) | collective-permute-done | bytes 589856 | tf_op jit(solution)/shard_map/ppermute | solution.py:65
  240.0 13.7 %collective-permute-done.20 = bf16[128,2304]{1,0:T(8,128)(2,1)S(1)} collective-permute-done((bf16[128,2304]{1,0:T(8,128)(2,1)S(1)}, bf16[128,2304]{1,0:T(8,128)(2,1)S(1)}, u32[]{:S(2)}, u32[]{:S(2)}) %collective-permute-start.20) | collective-permute-done | bytes 589856 | tf_op jit(solution)/shard_map/ppermute | solution.py:73
  259.7 83.9 %collective-permute-done.27 = bf16[576,1152]{1,0:T(8,128)(2,1)S(1)} collective-permute-done((bf16[576,1152]{1,0:T(8,128)(2,1)S(1)}, bf16[576,1152]{1,0:T(8,128)(2,1)S(1)}, u32[]{:S(2)}, u32[]{:S(2)}) %collective-permute-start.27) | collective-permute-done | bytes 1327136 | tf_op jit(solution)/shard_map/ppermute | solution.py:69
  345.6 26.4 %collective-permute-done.31 = bf16[576,1152]{1,0:T(8,128)(2,1)S(1)} collective-permute-done((bf16[576,1152]{1,0:T(8,128)(2,1)S(1)}, bf16[576,1152]{1,0:T(8,128)(2,1)S(1)}, u32[]{:S(2)}, u32[]{:S(2)}) %collective-permute-start.31) | collective-permute-done | bytes 1327136 | tf_op jit(solution)/shard_map/ppermute | solution.py:69
  373.8 8.5 fusion.86
  382.3 19.9 %collective-permute-done.29 = bf16[576,1152]{1,0:T(8,128)(2,1)S(1)} collective-permute-done((bf16[576,1152]{1,0:T(8,128)(2,1)S(1)}, bf16[576,1152]{1,0:T(8,128)(2,1)S(1)}, u32[]{:S(2)}, u32[]{:S(2)}) %collective-permute-start.29) | collective-permute-done | bytes 1327136 | tf_op jit(solution)/shard_map/ppermute | solution.py:65
  402.3 11.8 %multiply_convert_fusion.1 = (bf16[1024,1152]{1,0:T(8,128)(2,1)}, f32[1024,1152]{1,0:T(8,128)}) fusion(f32[1024,1152]{1,0:T(8,128)} %fusion.86, bf16[1024,2304]{1,0:T(8,128)(2,1)S(1)} %slice_dynamic-update-slice_fusion.3, bf16[576,1152]{1,0:T(8,128)(2,1)S(1)} %collective-permute-done.29, bf16[576,1152]{1,0:T(8,128)(2,1)S(1)} %collective-permute-done.28, ...), kind=kOutput, calls=%fused_computation.41 | convolution fusion | flops 5468848128 | bytes 21823488 | tf_op jit(solution)/shard_map/dot_general | solution.py:268
  414.1 16.5 %collective-permute-done.32 = bf16[576,1152]{1,0:T(8,128)(2,1)S(1)} collective-permute-done((bf16[576,1152]{1,0:T(8,128)(2,1)S(1)}, bf16[576,1152]{1,0:T(8,128)(2,1)S(1)}, u32[]{:S(2)}, u32[]{:S(2)}) %collective-permute-start.32) | collective-permute-done | bytes 1327136 | tf_op jit(solution)/shard_map/ppermute | solution.py:65
  430.7 28.4 %collective-permute-done.33 = bf16[576,1152]{1,0:T(8,128)(2,1)S(1)} collective-permute-done((bf16[576,1152]{1,0:T(8,128)(2,1)S(1)}, bf16[576,1152]{1,0:T(8,128)(2,1)S(1)}, u32[]{:S(2)}, u32[]{:S(2)}) %collective-permute-start.33) | collective-permute-done | bytes 1327136 | tf_op jit(solution)/shard_map/ppermute | solution.py:65
  460.2 8.7 fusion.83
  482.5 11.3 %collective-permute-done.35 = bf16[128,2304]{1,0:T(8,128)(2,1)} collective-permute-done((bf16[128,2304]{1,0:T(8,128)(2,1)}, bf16[128,2304]{1,0:T(8,128)(2,1)}, u32[]{:S(2)}, u32[]{:S(2)}) %collective-permute-start.35) | collective-permute-done | bytes 589856 | tf_op jit(solution)/shard_map/ppermute | solution.py:65
  493.8 13.5 %collective-permute-done.37 = bf16[128,2304]{1,0:T(8,128)(2,1)} collective-permute-done((bf16[128,2304]{1,0:T(8,128)(2,1)}, bf16[128,2304]{1,0:T(8,128)(2,1)}, u32[]{:S(2)}, u32[]{:S(2)}) %collective-permute-start.37) | collective-permute-done | bytes 589856 | tf_op jit(solution)/shard_map/ppermute | solution.py:73
  516.9 8.1 collective-permute-done.39
  525.0 13.4 %collective-permute-done.41 = bf16[128,2304]{1,0:T(8,128)(2,1)S(1)} collective-permute-done((bf16[128,2304]{1,0:T(8,128)(2,1)}, bf16[128,2304]{1,0:T(8,128)(2,1)S(1)}, u32[]{:S(2)}, u32[]{:S(2)}) %collective-permute-start.41) | collective-permute-done | bytes 589856 | tf_op jit(solution)/shard_map/ppermute | solution.py:73
  558.8 15.1 %fusion.11 = (bf16[1024,1152]{1,0:T(8,128)(2,1)}, bf16[1024,1152]{1,0:T(8,128)(2,1)S(1)}) fusion(f32[1024,1152]{1,0:T(8,128)} %fusion.86, f32[1024,1152]{1,0:T(8,128)} %get-tuple-element.183, bf16[1024,2304]{1,0:T(8,128)(2,1)} %slice_dynamic-update-slice_fusion, bf16[576,1152]{1,0:T(8,128)(2,1)S(1)} %copy-done.135, bf16[576,1152]{1,0:T(8,128)(2,1)S(1)} %copy-done.133, ...), kind=kOutput, calls=%fused_computation.31 | convolution fusion | flops 5485363200 | bytes 24182784 | tf_op jit(solution)/shard_map/dot_general | solution.py:283
  573.9 12.9 %fusion.84 = f32[1024,2304]{1,0:T(8,128)} fusion(bf16[1024,1152]{1,0:T(8,128)(2,1)S(1)} %get-tuple-element.113, bf16[576,1152]{1,0:T(8,128)(2,1)S(1)} %copy-done.131, bf16[576,1152]{1,0:T(8,128)(2,1)S(1)} %copy-done.126, bf16[576,1152]{1,0:T(8,128)(2,1)S(1)} %copy-done.124, bf16[576,1152]{1,0:T(8,128)(2,1)S(1)} %bitcast.547), kind=kOutput, calls=%fused_computation.202 | convolution fusion | flops 5457051648 | bytes 17104896 | tf_op jit(solution)/shard_map/dot_general | solution.py:291
  586.8 14.1 %convolution_add_fusion.3 = f32[1024,2304]{1,0:T(8,128)} fusion(f32[1024,2304]{1,0:T(8,128)} %fusion.84, bf16[1024,1152]{1,0:T(8,128)(2,1)} %get-tuple-element.112, bf16[576,1152]{1,0:T(8,128)(2,1)} %copy-done.127, bf16[576,1152]{1,0:T(8,128)(2,1)S(1)} %copy-done.122, bf16[576,1152]{1,0:T(8,128)(2,1)S(1)} %copy-done.120, bf16[576,1152]{1,0:T(8,128)(2,1)S(1)} %bitcast.543), kind=kOutput, calls=%fused_computation.10 | convolution fusion | flops 5459410944 | bytes 26542080 | tf_op jit(solution)/shard_map/dot_general | solution.py:290
  610.7 7.3 convolution_convert_fusion
  618.2 6.6 convolution_convert_fusion.2
  626.1 4.8 convolution_convert_fusion.1
  634.3 42.6 %collective-permute-done.66 = bf16[1152,1152]{1,0:T(8,128)(2,1)} collective-permute-done((bf16[1152,1152]{1,0:T(8,128)(2,1)}, bf16[1152,1152]{1,0:T(8,128)(2,1)}, u32[]{:S(2)}, u32[]{:S(2)}) %collective-permute-start.66) | collective-permute-done | bytes 2654240 | tf_op jit(solution)/shard_map/ppermute | solution.py:65
  677.2 5.3 convolution_add_fusion
  683.8 50.0 %collective-permute-done.60 = bf16[1152,1152]{1,0:T(8,128)(2,1)} collective-permute-done((bf16[1152,1152]{1,0:T(8,128)(2,1)}, bf16[1152,1152]{1,0:T(8,128)(2,1)}, u32[]{:S(2)}, u32[]{:S(2)}) %collective-permute-start.60) | collective-permute-done | bytes 2654240 | tf_op jit(solution)/shard_map/ppermute | solution.py:65
  734.0 5.8 convolution_add_fusion.2
  746.7 43.9 %collective-permute-done.63 = bf16[1152,1152]{1,0:T(8,128)(2,1)S(1)} collective-permute-done((bf16[1152,1152]{1,0:T(8,128)(2,1)}, bf16[1152,1152]{1,0:T(8,128)(2,1)S(1)}, u32[]{:S(2)}, u32[]{:S(2)}) %collective-permute-start.63) | collective-permute-done | bytes 2654240 | tf_op jit(solution)/shard_map/ppermute | solution.py:65
  799.6 51.7 %collective-permute-done.67 = bf16[576,1152]{1,0:T(8,128)(2,1)} collective-permute-done((bf16[576,1152]{1,0:T(8,128)(2,1)}, bf16[576,1152]{1,0:T(8,128)(2,1)}, u32[]{:S(2)}, u32[]{:S(2)}) %collective-permute-start.67) | collective-permute-done | bytes 1327136 | tf_op jit(solution)/shard_map/ppermute | solution.py:69
  854.7 25.1 %collective-permute-done.61 = bf16[576,1152]{1,0:T(8,128)(2,1)} collective-permute-done((bf16[576,1152]{1,0:T(8,128)(2,1)}, bf16[576,1152]{1,0:T(8,128)(2,1)}, u32[]{:S(2)}, u32[]{:S(2)}) %collective-permute-start.61) | collective-permute-done | bytes 1327136 | tf_op jit(solution)/shard_map/ppermute | solution.py:69
  883.6 24.6 %collective-permute-done.64 = bf16[576,1152]{1,0:T(8,128)(2,1)} collective-permute-done((bf16[576,1152]{1,0:T(8,128)(2,1)S(1)}, bf16[576,1152]{1,0:T(8,128)(2,1)}, u32[]{:S(2)}, u32[]{:S(2)}) %collective-permute-start.64) | collective-permute-done | bytes 1327136 | tf_op jit(solution)/shard_map/ppermute | solution.py:69
  923.1 5.0 fusion.14
  957.3 9.8 multiply_add_fusion
  969.0 7.2 collective-permute-done.57
  978.0 6.4 multiply_add_fusion.1
  984.4 9.0 copy.165
  993.4 6.5 copy.166
  999.9 6.7 copy.167
  1007.0 6.5 copy.164
  1021.6 9.0 collective-permute-done.59
  1040.3 7.3 collective-permute-done.69
  1063.1 5.6 collective-permute-start.73
  1071.6 16.8 %collective-permute-done.55 = bf16[288,1024]{1,0:T(8,128)(2,1)} collective-permute-done((bf16[288,1024]{1,0:T(8,128)(2,1)}, bf16[288,1024]{1,0:T(8,128)(2,1)}, u32[]{:S(2)}, u32[]{:S(2)}) %collective-permute-start.55) | collective-permute-done | bytes 589856 | tf_op jit(solution)/shard_map/ppermute | solution.py:69
  1092.9 5.6 multiply_add_fusion.3
  (652 shorter events, 283.2 us)
Async XLA Ops:
  3.4 55.3 %collective-permute-start.9 = (bf16[288,1536]{1,0:T(8,128)(2,1)}, bf16[288,1536]{1,0:T(8,128)(2,1)}, u32[]{:S(2)}, u32[]{:S(2)}) collective-permute-start(bf16[288,1536]{1,0:T(8,128)(2,1)} %get-tuple-element.150), channel_id=1, source_target_pairs={{0,16},{16,0},{1,17},{17,1},{2,18},{18,2},{3,19},{19,3},{4,20},{20... | collective-permute-start | bytes 2654216 | tf_op jit(solution)/shard_map/ppermute | solution.py:69
  6.6 55.4 %collective-permute-start.11 = (bf16[288,1536]{1,0:T(8,128)(2,1)}, bf16[288,1536]{1,0:T(8,128)(2,1)}, u32[]{:S(2)}, u32[]{:S(2)}) collective-permute-start(bf16[288,1536]{1,0:T(8,128)(2,1)} %get-tuple-element.150), channel_id=1, source_target_pairs={{0,4},{4,0},{1,5},{5,1},{2,6},{6,2},{3,7},{7,3},{8,12},{12,8},{9,1... | collective-permute-start | bytes 2654216 | tf_op jit(solution)/shard_map/ppermute | solution.py:65
  7.8 51.0 %collective-permute-start.8 = (bf16[288,1536]{1,0:T(8,128)(2,1)}, bf16[288,1536]{1,0:T(8,128)(2,1)}, u32[]{:S(2)}, u32[]{:S(2)}) collective-permute-start(bf16[288,1536]{1,0:T(8,128)(2,1)} %get-tuple-element.150), channel_id=1, source_target_pairs={{0,8},{8,0},{1,9},{9,1},{2,10},{10,2},{3,11},{11,3},{4,12},{12,4},... | collective-permute-start | bytes 2654216 | tf_op jit(solution)/shard_map/ppermute | solution.py:65
  16.1 40.7 %collective-permute-start.1 = (bf16[128,2304]{0,1:T(8,128)(2,1)S(1)}, bf16[128,2304]{0,1:T(8,128)(2,1)S(1)}, u32[]{:S(2)}, u32[]{:S(2)}) collective-permute-start(bf16[128,2304]{0,1:T(8,128)(2,1)S(1)} %bitcast.504), channel_id=1, source_target_pairs={{0,2},{2,0},{1,3},{3,1},{4,6},{6,4},{5,7},{7,5},{8,10},{10,8},{9,1... | collective-permute-start | bytes 1769480 | tf_op jit(solution)/shard_map/ppermute | solution.py:65
  58.7 117.8 %collective-permute-start.22 = (bf16[288,1152]{1,0:T(8,128)(2,1)}, bf16[288,1152]{1,0:T(8,128)(2,1)}, u32[]{:S(2)}, u32[]{:S(2)}) collective-permute-start(bf16[288,1152]{1,0:T(8,128)(2,1)} %get-tuple-element.141), channel_id=1, source_target_pairs={{0,8},{8,0},{1,9},{9,1},{2,10},{10,2},{3,11},{11,3},{4,12},{12,4},... | collective-permute-start | bytes 1990664 | tf_op jit(solution)/shard_map/ppermute | solution.py:65
  61.3 52.9 %collective-permute-start.10 = (bf16[288,1536]{1,0:T(8,128)(2,1)}, bf16[288,1536]{1,0:T(8,128)(2,1)S(1)}, u32[]{:S(2)}, u32[]{:S(2)}) collective-permute-start(bf16[288,1536]{1,0:T(8,128)(2,1)} %collective-permute-done.9), channel_id=1, source_target_pairs={{0,8},{8,0},{1,9},{9,1},{2,10},{10,2},{3,11},{11,3},{4,12},{12,4},... | collective-permute-start | bytes 2654216 | tf_op jit(solution)/shard_map/ppermute | solution.py:65
  62.0 50.9 %collective-permute-start.12 = (bf16[288,1536]{1,0:T(8,128)(2,1)}, bf16[288,1536]{1,0:T(8,128)(2,1)S(1)}, u32[]{:S(2)}, u32[]{:S(2)}) collective-permute-start(bf16[288,1536]{1,0:T(8,128)(2,1)} %collective-permute-done.11), channel_id=1, source_target_pairs={{0,8},{8,0},{1,9},{9,1},{2,10},{10,2},{3,11},{11,3},{4,12},{12,4},... | collective-permute-start | bytes 2654216 | tf_op jit(solution)/shard_map/ppermute | solution.py:65
  79.6 52.3 %collective-permute-start.14 = (bf16[288,1536]{1,0:T(8,128)(2,1)S(1)}, bf16[288,1536]{1,0:T(8,128)(2,1)S(1)}, u32[]{:S(2)}, u32[]{:S(2)}) collective-permute-start(bf16[288,1536]{1,0:T(8,128)(2,1)S(1)} %collective-permute-done.13), channel_id=1, source_target_pairs={{0,8},{8,0},{1,9},{9,1},{2,10},{10,2},{3,11},{11,3},{4,12},{12,4},... | collective-permute-start | bytes 2654216 | tf_op jit(solution)/shard_map/ppermute | solution.py:65
  172.9 82.1 %collective-permute-start.30 = (bf16[288,1152]{1,0:T(8,128)(2,1)}, bf16[288,1152]{1,0:T(8,128)(2,1)}, u32[]{:S(2)}, u32[]{:S(2)}) collective-permute-start(bf16[288,1152]{1,0:T(8,128)(2,1)} %get-tuple-element.139), channel_id=1, source_target_pairs={{0,8},{8,0},{1,9},{9,1},{2,10},{10,2},{3,11},{11,3},{4,12},{12,4},... | collective-permute-start | bytes 1990664 | tf_op jit(solution)/shard_map/ppermute | solution.py:65
  189.2 50.8 %collective-permute-start.19 = (bf16[128,2304]{1,0:T(8,128)(2,1)S(1)}, bf16[128,2304]{1,0:T(8,128)(2,1)S(1)}, u32[]{:S(2)}, u32[]{:S(2)}) collective-permute-start(bf16[128,2304]{1,0:T(8,128)(2,1)S(1)} %get-tuple-element.109), channel_id=1, source_target_pairs={{0,8},{8,0},{1,9},{9,1},{2,10},{10,2},{3,11},{11,3},{4,12},{12,4},... | collective-permute-start | bytes 1769480 | tf_op jit(solution)/shard_map/ppermute | solution.py:65
  189.6 64.0 %collective-permute-start.20 = (bf16[128,2304]{1,0:T(8,128)(2,1)S(1)}, bf16[128,2304]{1,0:T(8,128)(2,1)S(1)}, u32[]{:S(2)}, u32[]{:S(2)}) collective-permute-start(bf16[128,2304]{1,0:T(8,128)(2,1)S(1)} %get-tuple-element.109), channel_id=1, source_target_pairs={{0,10},{10,0},{2,8},{8,2},{1,11},{11,1},{3,9},{9,3},{4,14},{14,4},... | collective-permute-start | bytes 1769480 | tf_op jit(solution)/shard_map/ppermute | solution.py:73
  190.8 68.3 %collective-permute-start.23 = (bf16[576,1152]{1,0:T(8,128)(2,1)S(1)}, bf16[576,1152]{1,0:T(8,128)(2,1)S(1)}, u32[]{:S(2)}, u32[]{:S(2)}) collective-permute-start(bf16[576,1152]{1,0:T(8,128)(2,1)S(1)} %bitcast.540), channel_id=1, source_target_pairs={{0,16},{16,0},{1,17},{17,1},{2,18},{18,2},{3,19},{19,3},{4,20},{20... | collective-permute-start | bytes 3981320 | tf_op jit(solution)/shard_map/ppermute | solution.py:69
  201.7 143.6 %collective-permute-start.24 = (bf16[576,1152]{1,0:T(8,128)(2,1)S(1)}, bf16[576,1152]{1,0:T(8,128)(2,1)S(1)}, u32[]{:S(2)}, u32[]{:S(2)}) collective-permute-start(bf16[576,1152]{1,0:T(8,128)(2,1)S(1)} %bitcast.541), channel_id=1, source_target_pairs={{0,4},{4,0},{1,5},{5,1},{2,6},{6,2},{3,7},{7,3},{8,12},{12,8},{9,1... | collective-permute-start | bytes 3981320 | tf_op jit(solution)/shard_map/ppermute | solution.py:65
  253.7 90.1 %collective-permute-start.21 = (bf16[384,2304]{1,0:T(8,128)(2,1)S(1)}, bf16[384,2304]{1,0:T(8,128)(2,1)S(1)}, u32[]{:S(2)}, u32[]{:S(2)}) collective-permute-start(bf16[384,2304]{1,0:T(8,128)(2,1)S(1)} %pad_maximum_fusion.11), channel_id=1, source_target_pairs={{0,1},{1,0},{2,3},{3,2},{4,5},{5,4},{6,7},{7,6},{8,9},{9,8},{10,11... | collective-permute-start | bytes 5308424 | tf_op jit(solution)/shard_map/ppermute | solution.py:65
  254.9 88.7 %collective-permute-start.27 = (bf16[576,1152]{1,0:T(8,128)(2,1)S(1)}, bf16[576,1152]{1,0:T(8,128)(2,1)S(1)}, u32[]{:S(2)}, u32[]{:S(2)}) collective-permute-start(bf16[576,1152]{1,0:T(8,128)(2,1)S(1)} %bitcast.544), channel_id=1, source_target_pairs={{0,16},{16,0},{1,17},{17,1},{2,18},{18,2},{3,19},{19,3},{4,20},{20... | collective-permute-start | bytes 3981320 | tf_op jit(solution)/shard_map/ppermute | solution.py:69
  258.8 123.5 %collective-permute-start.28 = (bf16[576,1152]{1,0:T(8,128)(2,1)S(1)}, bf16[576,1152]{1,0:T(8,128)(2,1)S(1)}, u32[]{:S(2)}, u32[]{:S(2)}) collective-permute-start(bf16[576,1152]{1,0:T(8,128)(2,1)S(1)} %bitcast.545), channel_id=1, source_target_pairs={{0,4},{4,0},{1,5},{5,1},{2,6},{6,2},{3,7},{7,3},{8,12},{12,8},{9,1... | collective-permute-start | bytes 3981320 | tf_op jit(solution)/shard_map/ppermute | solution.py:65
  259.1 112.9 %collective-permute-start.31 = (bf16[576,1152]{1,0:T(8,128)(2,1)S(1)}, bf16[576,1152]{1,0:T(8,128)(2,1)S(1)}, u32[]{:S(2)}, u32[]{:S(2)}) collective-permute-start(bf16[576,1152]{1,0:T(8,128)(2,1)S(1)} %bitcast.548), channel_id=1, source_target_pairs={{0,16},{16,0},{1,17},{17,1},{2,18},{18,2},{3,19},{19,3},{4,20},{20... | collective-permute-start | bytes 3981320 | tf_op jit(solution)/shard_map/ppermute | solution.py:69
  343.6 30.2 %collective-permute-start.25 = (bf16[576,1152]{1,0:T(8,128)(2,1)S(1)}, bf16[576,1152]{1,0:T(8,128)(2,1)S(1)}, u32[]{:S(2)}, u32[]{:S(2)}) collective-permute-start(bf16[576,1152]{1,0:T(8,128)(2,1)S(1)} %collective-permute-done.23), channel_id=1, source_target_pairs={{0,4},{4,0},{1,5},{5,1},{2,6},{6,2},{3,7},{7,3},{8,12},{12,8},{9,1... | collective-permute-start | bytes 3981320 | tf_op jit(solution)/shard_map/ppermute | solution.py:65
  343.8 58.5 %collective-permute-start.29 = (bf16[576,1152]{1,0:T(8,128)(2,1)S(1)}, bf16[576,1152]{1,0:T(8,128)(2,1)S(1)}, u32[]{:S(2)}, u32[]{:S(2)}) collective-permute-start(bf16[576,1152]{1,0:T(8,128)(2,1)S(1)} %collective-permute-done.27), channel_id=1, source_target_pairs={{0,4},{4,0},{1,5},{5,1},{2,6},{6,2},{3,7},{7,3},{8,12},{12,8},{9,1... | collective-permute-start | bytes 3981320 | tf_op jit(solution)/shard_map/ppermute | solution.py:65
  345.3 85.4 %collective-permute-start.32 = (bf16[576,1152]{1,0:T(8,128)(2,1)S(1)}, bf16[576,1152]{1,0:T(8,128)(2,1)S(1)}, u32[]{:S(2)}, u32[]{:S(2)}) collective-permute-start(bf16[576,1152]{1,0:T(8,128)(2,1)S(1)} %bitcast.549), channel_id=1, source_target_pairs={{0,4},{4,0},{1,5},{5,1},{2,6},{6,2},{3,7},{7,3},{8,12},{12,8},{9,1... | collective-permute-start | bytes 3981320 | tf_op jit(solution)/shard_map/ppermute | solution.py:65
  372.0 87.1 %collective-permute-start.33 = (bf16[576,1152]{1,0:T(8,128)(2,1)S(1)}, bf16[576,1152]{1,0:T(8,128)(2,1)S(1)}, u32[]{:S(2)}, u32[]{:S(2)}) collective-permute-start(bf16[576,1152]{1,0:T(8,128)(2,1)S(1)} %collective-permute-done.31), channel_id=1, source_target_pairs={{0,4},{4,0},{1,5},{5,1},{2,6},{6,2},{3,7},{7,3},{8,12},{12,8},{9,1... | collective-permute-start | bytes 3981320 | tf_op jit(solution)/shard_map/ppermute | solution.py:65
  479.2 28.1 %collective-permute-start.37 = (bf16[128,2304]{1,0:T(8,128)(2,1)}, bf16[128,2304]{1,0:T(8,128)(2,1)}, u32[]{:S(2)}, u32[]{:S(2)}) collective-permute-start(bf16[128,2304]{1,0:T(8,128)(2,1)} %get-tuple-element.124), channel_id=1, source_target_pairs={{0,10},{10,0},{2,8},{8,2},{1,11},{11,1},{3,9},{9,3},{4,14},{14,4},... | collective-permute-start | bytes 1769480 | tf_op jit(solution)/shard_map/ppermute | solution.py:73
  511.9 26.5 %collective-permute-start.41 = (bf16[128,2304]{1,0:T(8,128)(2,1)}, bf16[128,2304]{1,0:T(8,128)(2,1)S(1)}, u32[]{:S(2)}, u32[]{:S(2)}) collective-permute-start(bf16[128,2304]{1,0:T(8,128)(2,1)} %get-tuple-element.103), channel_id=1, source_target_pairs={{0,10},{10,0},{2,8},{8,2},{1,11},{11,1},{3,9},{9,3},{4,14},{14,4},... | collective-permute-start | bytes 1769480 | tf_op jit(solution)/shard_map/ppermute | solution.py:73
  514.5 31.5 %collective-permute-start.38 = (bf16[128,2304]{1,0:T(8,128)(2,1)}, bf16[128,2304]{1,0:T(8,128)(2,1)}, u32[]{:S(2)}, u32[]{:S(2)}) collective-permute-start(bf16[128,2304]{1,0:T(8,128)(2,1)} %get-tuple-element.103), channel_id=1, source_target_pairs={{0,1},{1,0},{2,3},{3,2},{4,5},{5,4},{6,7},{7,6},{8,9},{9,8},{10,11... | collective-permute-start | bytes 1769480 | tf_op jit(solution)/shard_map/ppermute | solution.py:65
  604.9 26.2 %collective-permute-start.43 = (bf16[2,2,128,2304]{3,2,1,0:T(8,128)(2,1)}, bf16[2,2,128,2304]{3,2,1,0:T(8,128)(2,1)}, u32[]{:S(2)}, u32[]{:S(2)}) collective-permute-start(bf16[2,2,128,2304]{3,2,1,0:T(8,128)(2,1)} %fusion.24), channel_id=1, source_target_pairs={{0,1},{1,0},{2,3},{3,2},{4,5},{5,4},{6,7},{7,6},{8,9},{9,8},{10,11... | collective-permute-start | bytes 7077896 | tf_op jit(solution)/shard_map/ppermute | solution.py:65
  618.0 58.9 %collective-permute-start.66 = (bf16[1152,1152]{1,0:T(8,128)(2,1)}, bf16[1152,1152]{1,0:T(8,128)(2,1)}, u32[]{:S(2)}, u32[]{:S(2)}) collective-permute-start(bf16[1152,1152]{1,0:T(8,128)(2,1)} %convolution_convert_fusion), channel_id=1, source_target_pairs={{0,4},{4,0},{1,5},{5,1},{2,6},{6,2},{3,7},{7,3},{8,12},{12,8},{9,1... | collective-permute-start | bytes 7962632 | tf_op jit(solution)/shard_map/ppermute | solution.py:65
  624.8 109.0 %collective-permute-start.60 = (bf16[1152,1152]{1,0:T(8,128)(2,1)}, bf16[1152,1152]{1,0:T(8,128)(2,1)}, u32[]{:S(2)}, u32[]{:S(2)}) collective-permute-start(bf16[1152,1152]{1,0:T(8,128)(2,1)} %convolution_convert_fusion.2), channel_id=1, source_target_pairs={{0,4},{4,0},{1,5},{5,1},{2,6},{6,2},{3,7},{7,3},{8,12},{12,8},{9,1... | collective-permute-start | bytes 7962632 | tf_op jit(solution)/shard_map/ppermute | solution.py:65
  630.9 159.7 %collective-permute-start.63 = (bf16[1152,1152]{1,0:T(8,128)(2,1)}, bf16[1152,1152]{1,0:T(8,128)(2,1)S(1)}, u32[]{:S(2)}, u32[]{:S(2)}) collective-permute-start(bf16[1152,1152]{1,0:T(8,128)(2,1)} %convolution_convert_fusion.1), channel_id=1, source_target_pairs={{0,4},{4,0},{1,5},{5,1},{2,6},{6,2},{3,7},{7,3},{8,12},{12,8},{9,1... | collective-permute-start | bytes 7962632 | tf_op jit(solution)/shard_map/ppermute | solution.py:65
  633.6 107.6 %collective-permute-start.44 = (bf16[128,2304]{1,0:T(8,128)(2,1)S(1)}, bf16[128,2304]{1,0:T(8,128)(2,1)S(1)}, u32[]{:S(2)}, u32[]{:S(2)}) collective-permute-start(bf16[128,2304]{1,0:T(8,128)(2,1)S(1)} %get-tuple-element.120), channel_id=1, source_target_pairs={{0,2},{2,0},{1,3},{3,1},{4,6},{6,4},{5,7},{7,5},{8,10},{10,8},{9,1... | collective-permute-start | bytes 1769480 | tf_op jit(solution)/shard_map/ppermute | solution.py:65
  633.9 109.5 %collective-permute-start.45 = (bf16[128,2304]{1,0:T(8,128)(2,1)S(1)}, bf16[128,2304]{1,0:T(8,128)(2,1)S(1)}, u32[]{:S(2)}, u32[]{:S(2)}) collective-permute-start(bf16[128,2304]{1,0:T(8,128)(2,1)S(1)} %get-tuple-element.122), channel_id=1, source_target_pairs={{0,8},{8,0},{1,9},{9,1},{2,10},{10,2},{3,11},{11,3},{4,12},{12,4},... | collective-permute-start | bytes 1769480 | tf_op jit(solution)/shard_map/ppermute | solution.py:65
  676.9 66.5 %collective-permute-start.46 = (bf16[128,2304]{1,0:T(8,128)(2,1)S(1)}, bf16[128,2304]{1,0:T(8,128)(2,1)S(1)}, u32[]{:S(2)}, u32[]{:S(2)}) collective-permute-start(bf16[128,2304]{1,0:T(8,128)(2,1)S(1)} %get-tuple-element.121), channel_id=1, source_target_pairs={{0,10},{10,0},{2,8},{8,2},{1,11},{11,1},{3,9},{9,3},{4,14},{14,4},... | collective-permute-start | bytes 1769480 | tf_op jit(solution)/shard_map/ppermute | solution.py:73
  733.8 117.5 %collective-permute-start.67 = (bf16[576,1152]{1,0:T(8,128)(2,1)}, bf16[576,1152]{1,0:T(8,128)(2,1)}, u32[]{:S(2)}, u32[]{:S(2)}) collective-permute-start(bf16[576,1152]{1,0:T(8,128)(2,1)} %slice.881), channel_id=1, source_target_pairs={{0,16},{16,0},{1,17},{17,1},{2,18},{18,2},{3,19},{19,3},{4,20},{20... | collective-permute-start | bytes 3981320 | tf_op jit(solution)/shard_map/ppermute | solution.py:69
  741.3 138.5 %collective-permute-start.61 = (bf16[576,1152]{1,0:T(8,128)(2,1)}, bf16[576,1152]{1,0:T(8,128)(2,1)}, u32[]{:S(2)}, u32[]{:S(2)}) collective-permute-start(bf16[576,1152]{1,0:T(8,128)(2,1)} %slice.883), channel_id=1, source_target_pairs={{0,16},{16,0},{1,17},{17,1},{2,18},{18,2},{3,19},{19,3},{4,20},{20... | collective-permute-start | bytes 3981320 | tf_op jit(solution)/shard_map/ppermute | solution.py:69
  746.4 53.2 %collective-permute-start.48 = (bf16[128,2304]{1,0:T(8,128)(2,1)S(1)}, bf16[128,2304]{1,0:T(8,128)(2,1)S(1)}, u32[]{:S(2)}, u32[]{:S(2)}) collective-permute-start(bf16[128,2304]{1,0:T(8,128)(2,1)S(1)} %multiply_convert_fusion.2), channel_id=1, source_target_pairs={{0,2},{2,0},{1,3},{3,1},{4,6},{6,4},{5,7},{7,5},{8,10},{10,8},{9,1... | collective-permute-start | bytes 1769480 | tf_op jit(solution)/shard_map/ppermute | solution.py:65
  796.3 112.0 %collective-permute-start.64 = (bf16[576,1152]{1,0:T(8,128)(2,1)S(1)}, bf16[576,1152]{1,0:T(8,128)(2,1)}, u32[]{:S(2)}, u32[]{:S(2)}) collective-permute-start(bf16[576,1152]{1,0:T(8,128)(2,1)S(1)} %slice.882), channel_id=1, source_target_pairs={{0,16},{16,0},{1,17},{17,1},{2,18},{18,2},{3,19},{19,3},{4,20},{20... | collective-permute-start | bytes 3981320 | tf_op jit(solution)/shard_map/ppermute | solution.py:69
  796.6 115.3 %collective-permute-start.47 = (bf16[128,2304]{1,0:T(8,128)(2,1)S(1)}, bf16[128,2304]{1,0:T(8,128)(2,1)S(1)}, u32[]{:S(2)}, u32[]{:S(2)}) collective-permute-start(bf16[128,2304]{1,0:T(8,128)(2,1)S(1)} %multiply_convert_fusion.2), channel_id=1, source_target_pairs={{0,1},{1,0},{2,3},{3,2},{4,5},{5,4},{6,7},{7,6},{8,9},{9,8},{10,11... | collective-permute-start | bytes 1769480 | tf_op jit(solution)/shard_map/ppermute | solution.py:65
  799.6 112.4 %collective-permute-start.49 = (bf16[128,2304]{1,0:T(8,128)(2,1)S(1)}, bf16[128,2304]{1,0:T(8,128)(2,1)S(1)}, u32[]{:S(2)}, u32[]{:S(2)}) collective-permute-start(bf16[128,2304]{1,0:T(8,128)(2,1)S(1)} %collective-permute-done.48), channel_id=1, source_target_pairs={{0,1},{1,0},{2,3},{3,2},{4,5},{5,4},{6,7},{7,6},{8,9},{9,8},{10,11... | collective-permute-start | bytes 1769480 | tf_op jit(solution)/shard_map/ppermute | solution.py:65
  854.7 112.4 %collective-permute-start.68 = (bf16[288,1152]{1,0:T(8,128)(2,1)}, bf16[288,1152]{1,0:T(8,128)(2,1)}, u32[]{:S(2)}, u32[]{:S(2)}) collective-permute-start(bf16[288,1152]{1,0:T(8,128)(2,1)} %broadcast_select_fusion.2), channel_id=1, source_target_pairs={{0,8},{8,0},{1,9},{9,1},{2,10},{10,2},{3,11},{11,3},{4,12},{12,4},... | collective-permute-start | bytes 1990664 | tf_op jit(solution)/shard_map/ppermute | solution.py:65
  883.5 69.7 %collective-permute-start.62 = (bf16[288,1152]{1,0:T(8,128)(2,1)}, bf16[288,1152]{1,0:T(8,128)(2,1)}, u32[]{:S(2)}, u32[]{:S(2)}) collective-permute-start(bf16[288,1152]{1,0:T(8,128)(2,1)} %broadcast_select_fusion.6), channel_id=1, source_target_pairs={{0,8},{8,0},{1,9},{9,1},{2,10},{10,2},{3,11},{11,3},{4,12},{12,4},... | collective-permute-start | bytes 1990664 | tf_op jit(solution)/shard_map/ppermute | solution.py:65
  911.9 42.7 %collective-permute-start.65 = (bf16[288,1152]{1,0:T(8,128)(2,1)}, bf16[288,1152]{1,0:T(8,128)(2,1)}, u32[]{:S(2)}, u32[]{:S(2)}) collective-permute-start(bf16[288,1152]{1,0:T(8,128)(2,1)} %broadcast_select_fusion.4), channel_id=1, source_target_pairs={{0,8},{8,0},{1,9},{9,1},{2,10},{10,2},{3,11},{11,3},{4,12},{12,4},... | collective-permute-start | bytes 1990664 | tf_op jit(solution)/shard_map/ppermute | solution.py:65
  930.6 84.6 %collective-permute-start.50 = (bf16[2,128,2304]{2,1,0:T(8,128)(2,1)}, bf16[2,128,2304]{2,1,0:T(8,128)(2,1)}, u32[]{:S(2)}, u32[]{:S(2)}) collective-permute-start(bf16[2,128,2304]{2,1,0:T(8,128)(2,1)} %fusion.57), channel_id=1, source_target_pairs={{0,1},{1,0},{2,3},{3,2},{4,5},{5,4},{6,7},{7,6},{8,9},{9,8},{10,11... | collective-permute-start | bytes 3538952 | tf_op jit(solution)/shard_map/ppermute | solution.py:65
  937.5 76.0 %collective-permute-start.56 = (bf16[2,288,512]{2,1,0:T(8,128)(2,1)}, bf16[2,288,512]{2,1,0:T(8,128)(2,1)}, u32[]{:S(2)}, u32[]{:S(2)}) collective-permute-start(bf16[2,288,512]{2,1,0:T(8,128)(2,1)} %fusion.88), channel_id=1, source_target_pairs={{0,8},{8,0},{1,9},{9,1},{2,10},{10,2},{3,11},{11,3},{4,12},{12,4},... | collective-permute-start | bytes 1769480 | tf_op jit(solution)/shard_map/ppermute | solution.py:65
  953.2 23.0 %collective-permute-start.57 = (bf16[2,288,512]{2,1,0:T(8,128)(2,1)}, bf16[2,288,512]{2,1,0:T(8,128)(2,1)}, u32[]{:S(2)}, u32[]{:S(2)}) collective-permute-start(bf16[2,288,512]{2,1,0:T(8,128)(2,1)} %fusion.89), channel_id=1, source_target_pairs={{0,8},{8,0},{1,9},{9,1},{2,10},{10,2},{3,11},{11,3},{4,12},{12,4},... | collective-permute-start | bytes 1769480 | tf_op jit(solution)/shard_map/ppermute | solution.py:65
  954.6 62.6 %collective-permute-start.53 = (bf16[2,288,1024]{2,1,0:T(8,128)(2,1)}, bf16[2,288,1024]{2,1,0:T(8,128)(2,1)}, u32[]{:S(2)}, u32[]{:S(2)}) collective-permute-start(bf16[2,288,1024]{2,1,0:T(8,128)(2,1)} %fusion.55), channel_id=1, source_target_pairs={{0,8},{8,0},{1,9},{9,1},{2,10},{10,2},{3,11},{11,3},{4,12},{12,4},... | collective-permute-start | bytes 3538952 | tf_op jit(solution)/shard_map/ppermute | solution.py:65
  967.1 90.3 %collective-permute-start.52 = (bf16[2,288,1024]{2,1,0:T(8,128)(2,1)}, bf16[2,288,1024]{2,1,0:T(8,128)(2,1)}, u32[]{:S(2)}, u32[]{:S(2)}) collective-permute-start(bf16[2,288,1024]{2,1,0:T(8,128)(2,1)} %fusion.54), channel_id=1, source_target_pairs={{0,8},{8,0},{1,9},{9,1},{2,10},{10,2},{3,11},{11,3},{4,12},{12,4},... | collective-permute-start | bytes 3538952 | tf_op jit(solution)/shard_map/ppermute | solution.py:65
  977.7 35.8 %collective-permute-start.58 = (bf16[2,288,512]{2,1,0:T(8,128)(2,1)S(1)}, bf16[2,288,512]{2,1,0:T(8,128)(2,1)S(1)}, u32[]{:S(2)}, u32[]{:S(2)}) collective-permute-start(bf16[2,288,512]{2,1,0:T(8,128)(2,1)S(1)} %fusion.70), channel_id=1, source_target_pairs={{0,4},{4,0},{1,5},{5,1},{2,6},{6,2},{3,7},{7,3},{8,12},{12,8},{9,1... | collective-permute-start | bytes 1769480 | tf_op jit(solution)/shard_map/ppermute | solution.py:65
  1020.4 37.1 %collective-permute-start.54 = (bf16[2,288,1024]{2,1,0:T(8,128)(2,1)}, bf16[2,288,1024]{2,1,0:T(8,128)(2,1)}, u32[]{:S(2)}, u32[]{:S(2)}) collective-permute-start(bf16[2,288,1024]{2,1,0:T(8,128)(2,1)} %fusion.34), channel_id=1, source_target_pairs={{0,4},{4,0},{1,5},{5,1},{2,6},{6,2},{3,7},{7,3},{8,12},{12,8},{9,1... | collective-permute-start | bytes 3538952 | tf_op jit(solution)/shard_map/ppermute | solution.py:65
  1060.9 27.6 %collective-permute-start.55 = (bf16[288,1024]{1,0:T(8,128)(2,1)}, bf16[288,1024]{1,0:T(8,128)(2,1)}, u32[]{:S(2)}, u32[]{:S(2)}) collective-permute-start(bf16[288,1024]{1,0:T(8,128)(2,1)} %fusion.92), channel_id=1, source_target_pairs={{0,16},{16,0},{1,17},{17,1},{2,18},{18,2},{3,19},{19,3},{4,20},{20... | collective-permute-start | bytes 1769480 | tf_op jit(solution)/shard_map/ppermute | solution.py:69
  (187 other events, 3261.2 us)

commit v2 on v1

v2 whole, which is shorter than its diff:
```python
import functools

import jax
import jax.numpy as jnp
from jax import lax
from jax.experimental import pallas as pl
from jax.experimental.pallas import tpu as pltpu
from jax.sharding import Mesh
from jax.sharding import PartitionSpec as P

SEQ = 512
DEPTH = 4

norm_eps = 1e-06
soft_cap = 50.0
rope_base = 10000.0
beta_first = 0.9
beta_second = 0.95
learn_rate = 0.02
decay_rate = 0.1
adam_eps = 1e-08
step_number = 3.0

F32 = jnp.float32
BF16 = jnp.bfloat16


def norm_forward(values, gain_vec):
    factor = lax.rsqrt(jnp.mean(values * values, axis=-1, keepdims=True) + norm_eps)
    return (values * factor * gain_vec, factor)


def norm_backward(values, factor, gain_vec, incoming):
    unit_rows = values * factor
    gain_part = jnp.sum(incoming * unit_rows, axis=0)
    scaled = incoming * gain_vec
    return (
        factor * (scaled - unit_rows * jnp.mean(scaled * unit_rows, axis=-1, keepdims=True)),
        gain_part,
    )


def rotate(values, cosine_table, sine_table):
    half_width = values.shape[-1] // 2
    first_half = values[:, :half_width]
    second_half = values[:, half_width:]
    return jnp.concatenate(
        [
            first_half * cosine_table - second_half * sine_table,
            second_half * cosine_table + first_half * sine_table,
        ],
        axis=-1,
    )


def adam_step(weight, gradient, mean_old, power_old):
    mean_new = beta_first * mean_old + (1.0 - beta_first) * gradient
    power_new = beta_second * power_old + (1.0 - beta_second) * gradient * gradient
    mean_hat = mean_new / (1.0 - beta_first**step_number)
    power_hat = power_new / (1.0 - beta_second**step_number)
    change = -learn_rate * (mean_hat / (jnp.sqrt(power_hat) + adam_eps) + decay_rate * weight)
    return (weight + change, mean_new, power_new, change)


def swap(value, axis):
    return lax.ppermute(value, axis, [(0, 1), (1, 0)])


def from_ahead(value, axis, size, step):
    return lax.ppermute(value, axis, [(j, (j - step) % size) for j in range(size)])


def after(value, *others):
    return lax.optimization_barrier((value,) + others)[0]


def gated(values, *others):
    values = list(values)
    return list(lax.optimization_barrier(tuple(values) + others)[: len(values)])


def ordered(own, other, place):
    straight = jnp.stack([own, other])
    return jnp.where(place == 0, straight, straight[::-1])


def rolled(value, place, axis):
    count = value.shape[axis]
    result = value
    for step in range(1, count):
        result = jnp.where(place == step, jnp.roll(value, -step, axis), result)
    return result


def transposed(left, right):
    return lax.dot_general(left, right, (((0,), (0,)), ((), ())), preferred_element_type=F32)


def times_transposed(left, right):
    return lax.dot_general(left, right, (((1,), (1,)), ((), ())), preferred_element_type=F32)


VMEM_LIMIT = 60 * 1024 * 1024
params = pltpu.CompilerParams(vmem_limit_bytes=VMEM_LIMIT)


def whole(count):
    return [pl.BlockSpec(memory_space=pltpu.VMEM)] * count


def shape(dims, dtype=BF16):
    return jax.ShapeDtypeStruct(dims, dtype)


def dot(left, right):
    return jnp.dot(left, right, preferred_element_type=F32)


def visible(place_col, place_row, seg_col, seg_row):
    return (seg_col[...] == seg_row[...]) & (place_row[...] <= place_col[...])


def attend_kernel(
    group_size,
    head_width,
    rows,
    gain,
    weights,
    cosine,
    sine,
    place_col,
    place_row,
    seg_col,
    seg_row,
    normed_out,
    queries_out,
    keys_out,
    values_out,
    logsum_out,
    context_out,
    mine_out,
    other_out,
):
    mix_width = (group_size + 2) * head_width
    values = rows[...].astype(F32)
    normed_out[...] = norm_forward(values, gain[...])[0].astype(BF16)
    mixed = dot(normed_out[...], weights[:, :mix_width])
    cos_table, sin_table = cosine[...], sine[...]
    scale = head_width ** (-0.5)
    width = group_size * head_width
    for head in range(group_size):
        part = slice(head * head_width, (head + 1) * head_width)
        queries_out[:, part] = (rotate(mixed[:, part], cos_table, sin_table) * scale).astype(BF16)
    keys_out[...] = rotate(mixed[:, width : width + head_width], cos_table, sin_table).astype(BF16)
    values_out[...] = mixed[:, width + head_width :].astype(BF16)
    allowed = visible(place_col, place_row, seg_col, seg_row)
    for head in range(group_size):
        part = slice(head * head_width, (head + 1) * head_width)
        scores = times_transposed(queries_out[:, part], keys_out[...])
        capped = jnp.where(allowed, soft_cap * jnp.tanh(scores / soft_cap), -jnp.inf)
        row_max = jnp.max(capped, axis=-1, keepdims=True)
        exp_scores = jnp.exp(capped - row_max)
        row_total = jnp.sum(exp_scores, axis=-1, keepdims=True)
        logsum_out[head] = row_max + jnp.log(row_total)
        context_out[:, part] = dot((exp_scores / row_total).astype(BF16), values_out[...]).astype(BF16)
    half = rows.shape[0] // 2
    other_out[...] = times_transposed(context_out[half:], weights[:, mix_width:]).astype(BF16)
    mine_out[...] = times_transposed(context_out[:half], weights[:, mix_width:])


def attend_back_kernel(
    group_size,
    head_width,
    slopes,
    weights,
    queries,
    keys,
    values,
    logsum,
    cosine,
    sine,
    place_col,
    place_row,
    seg_col,
    seg_row,
    mixed_out,
    mine_out,
    other_out,
):
    mix_width = (group_size + 2) * head_width
    width = group_size * head_width
    scale = head_width ** (-0.5)
    context_slope = dot(slopes[...], weights[:, mix_width:]).astype(BF16)
    cos_table, sin_table = cosine[...], -sine[...]
    allowed = visible(place_col, place_row, seg_col, seg_row)
    key_slope = jnp.zeros(keys.shape, F32)
    value_slope = jnp.zeros(values.shape, F32)
    for head in range(group_size):
        part = slice(head * head_width, (head + 1) * head_width)
        tanh_value = jnp.tanh(times_transposed(queries[:, part], keys[...]) / soft_cap)
        probs = jnp.where(allowed, jnp.exp(soft_cap * tanh_value - logsum[head]), 0.0)
        slope = context_slope[:, part]
        prob_slope = times_transposed(slope, values[...])
        value_slope += transposed(probs.astype(BF16), slope)
        inner_sum = jnp.sum(probs * prob_slope, axis=-1, keepdims=True)
        score_slope = (probs * (prob_slope - inner_sum) * (1.0 - tanh_value * tanh_value)).astype(BF16)
        query_slope = dot(score_slope, keys[...])
        key_slope += transposed(score_slope, queries[:, part])
        mixed_out[:, part] = rotate(query_slope * scale, cos_table, sin_table).astype(BF16)
    mixed_out[:, width : width + head_width] = rotate(key_slope, cos_table, sin_table).astype(BF16)
    mixed_out[:, width + head_width :] = value_slope.astype(BF16)
    half = slopes.shape[0] // 2
    other_out[...] = times_transposed(mixed_out[half:], weights[:, :mix_width]).astype(BF16)
    mine_out[...] = times_transposed(mixed_out[:half], weights[:, :mix_width])


root_two_pi = 0.7978845608028654
cubic = 0.044715


def gate_up_kernel(main, rows, weights, active_out, gate_out, up_out):
    result = dot(rows[...], weights[0])
    quarter = weights.shape[2] // 2
    bounds = [
        (slice(0, main), slice(main, 2 * main), slice(0, main)),
        (slice(2 * main, main + quarter), slice(main + quarter, 2 * quarter), slice(main, quarter)),
    ]
    for gate_part, up_part, part in bounds:
        gate, up = result[:, gate_part], result[:, up_part]
        square = gate * gate
        tanh_value = jnp.tanh(root_two_pi * gate * (1.0 + cubic * square))
        near = 0.5 * (1.0 + tanh_value)
        gelu = gate * near
        slope = near + 0.5 * gate * (1.0 - tanh_value * tanh_value) * root_two_pi * (
            1.0 + 3.0 * cubic * square
        )
        active_out[0, :, part] = (gelu * up).astype(BF16)
        gate_out[0, :, part] = (slope * up).astype(BF16)
        up_out[0, :, part] = gelu.astype(BF16)


def gate_up_call(rows, weights, main):
    count, width, columns = weights.shape
    height = rows.shape[0]
    quarter = columns // 2
    out_block = pl.BlockSpec((1, height, quarter), lambda i: (i, 0, 0))
    return pl.pallas_call(
        functools.partial(gate_up_kernel, main),
        grid=(count,),
        in_specs=[
            pl.BlockSpec((height, width), lambda i: (0, 0)),
            pl.BlockSpec((1, width, columns), lambda i: (i, 0, 0)),
        ],
        out_specs=[out_block] * 3,
        out_shape=[shape((count, height, quarter))] * 3,
        compiler_params=params,
    )(rows, weights)


def down_kernel(active, weights, *refs):
    out = refs[-1]
    total = times_transposed(active[0], weights[0])
    for place in range(1, active.shape[0]):
        total += times_transposed(active[place], weights[place])
    if len(refs) > 1:
        total += refs[0][...].astype(F32)
    out[...] = total.astype(out.dtype)


def down_call(active, weights, out_type, *received):
    count, height, quarter = active.shape
    width = weights.shape[1]
    tile = width // 3
    block = pl.BlockSpec((height, tile), lambda i: (0, i))
    return pl.pallas_call(
        down_kernel,
        grid=(3,),
        in_specs=[
            pl.BlockSpec((count, height, quarter), lambda i: (0, 0, 0)),
            pl.BlockSpec((count, tile, quarter), lambda i: (0, i, 0)),
        ]
        + [block] * len(received),
        out_specs=block,
        out_shape=shape((height, width), out_type),
        compiler_params=params,
    )(active, weights, *received)


def feed_back_kernel(main, slopes, down, gate_up, gate_factor, up_factor, slope_out, out, total):
    step = pl.program_id(0)
    active_slope = dot(slopes[...], down[0])
    quarter = active_slope.shape[1]
    gate_slope = (active_slope * gate_factor[0].astype(F32)).astype(BF16)
    up_slope = (active_slope * up_factor[0].astype(F32)).astype(BF16)
    slope_out[0] = jnp.concatenate(
        [gate_slope[:, :main], up_slope[:, :main], gate_slope[:, main:], up_slope[:, main:]], axis=1
    )
    product = times_transposed(slope_out[0], gate_up[0])

    @pl.when(step == 0)
    def _():
        total[...] = product

    @pl.when(step > 0)
    def _():
        total[...] += product

    @pl.when(step == pl.num_programs(0) - 1)
    def _():
        out[...] = total[...].astype(out.dtype)


def feed_back_call(slopes, down, gate_up, gate_factor, up_factor, main, out_type):
    height, width = slopes.shape
    count, _, columns = gate_up.shape
    quarter = columns // 2
    whole_block = pl.BlockSpec((height, width), lambda i: (0, 0))

    def each(rows, wide):
        return pl.BlockSpec((1, rows, wide), lambda i: (i, 0, 0))

    return pl.pallas_call(
        functools.partial(feed_back_kernel, main),
        grid=(count,),
        in_specs=[
            whole_block,
            each(width, quarter),
            each(width, columns),
            each(height, quarter),
            each(height, quarter),
        ],
        out_specs=[each(height, columns), whole_block],
        out_shape=[shape((count, height, columns)), shape((height, width), out_type)],
        scratch_shapes=[pltpu.VMEM((height, width), F32)],
        compiler_params=params,
    )(slopes, down, gate_up, gate_factor, up_factor)


def weight_slope_kernel(left_mine, left_other, right_mine, right_other, out):
    total = transposed(left_mine[...], right_mine[0]) + transposed(left_other[...], right_other[0])
    out[0] = total.astype(BF16)


def weight_slope_call(lefts, rights):
    height, width = lefts[0].shape
    count, _, columns = rights[0].shape
    tile = width // 3
    left_block = pl.BlockSpec((height, tile), lambda i, j: (0, j))
    right_block = pl.BlockSpec((1, height, columns), lambda i, j: (i, 0, 0))
    return pl.pallas_call(
        weight_slope_kernel,
        grid=(count, 3),
        in_specs=[left_block] * 2 + [right_block] * 2,
        out_specs=pl.BlockSpec((1, tile, columns), lambda i, j: (i, j, 0)),
        out_shape=shape((count, width, columns)),
        compiler_params=params,
    )(*lefts, *rights)


def gate_up_adam_kernel(main, depth, *refs):
    pieces, (weight, mean, power), outs = refs[:DEPTH], refs[DEPTH : DEPTH + 3], refs[DEPTH + 3 :]
    rest = pieces[0].shape[1] // 2 - main
    quarters = []
    for place in range(DEPTH):
        step = (place - depth[0]) % DEPTH
        value = pieces[0][...]
        for ahead in range(1, DEPTH):
            value = jnp.where(step == ahead, pieces[ahead][...], value)
        quarters.append(value.astype(F32))
    for slot in range(2):
        begin = 2 * main + slot * rest
        gradient = jnp.concatenate(
            [value[:, slot * main : (slot + 1) * main] for value in quarters]
            + [value[:, begin : begin + rest] for value in quarters],
            axis=1,
        )
        result = adam_step(weight[:, slot], gradient, mean[:, slot], power[:, slot])
        for out, value in zip(outs, (gradient,) + result[:3]):
            out[:, slot] = value


def gate_up_adam_call(depth, pieces, weight, mean, power, main):
    block, columns = pieces[0].shape
    tile = 24 if block % 32 else 32
    piece_block = pl.BlockSpec((tile, columns), lambda i, depth: (i, 0))
    weight_block = pl.BlockSpec((tile,) + weight.shape[1:], lambda i, depth: (i, 0, 0))
    return pl.pallas_call(
        functools.partial(gate_up_adam_kernel, main),
        grid_spec=pltpu.PrefetchScalarGridSpec(
            num_scalar_prefetch=1,
            grid=(block // tile,),
            in_specs=[piece_block] * DEPTH + [weight_block] * 3,
            out_specs=[weight_block] * 4,
        ),
        out_shape=[shape(weight.shape, F32)] * 4,
        compiler_params=params,
    )(depth.reshape(1), *pieces, weight, mean, power)


def make_device(side_size):
    def per_device(
        inputs,
        segments,
        cotangent,
        project_weight,
        output_weight,
        gate_up_weight,
        down_weight,
        norm_gains,
        project_mean,
        project_power,
        output_mean,
        output_power,
        gate_up_mean,
        gate_up_power,
        down_mean,
        down_power,
        gains_mean,
        gains_power,
    ):
        depth, side, row, core = (lax.axis_index(name) for name in ("z", "x", "y", "c"))
        own_rows, width = inputs.shape
        block = project_weight.shape[0]
        head_width = project_weight.shape[3]
        slots = project_weight.shape[2]
        group_size = slots - 2
        kv_local = project_weight.shape[1]
        mix_width = kv_local * slots * head_width
        context_width = output_weight.shape[0]
        hidden = down_weight.shape[0]
        quarter = hidden // DEPTH
        main = quarter // 128 * 128
        total_rows = 4 * own_rows
        seq_count = total_rows // SEQ

        def arrange(value):
            lead = value.shape[0]
            value = value.reshape(lead, DEPTH, side_size, block).transpose(0, 2, 1, 3)
            return value.reshape(lead, width)

        def unarrange(value):
            lead = value.shape[0]
            value = value.reshape(lead, side_size, DEPTH, block).transpose(0, 2, 1, 3)
            return value.reshape(lead, width)

        attend_own = jnp.concatenate(
            [project_weight.astype(BF16).reshape(block, mix_width), output_weight.astype(BF16).T],
            axis=1,
        )
        rows_own = arrange(inputs)

        def gather_sequence(value):
            mine = jnp.concatenate([value, swap(value, "y")], axis=0)
            return jnp.concatenate([mine, swap(mine, "c")], axis=0)

        def scatter_sequence(mine, other, *earlier):
            mine = mine + swap(other, "c").astype(F32)
            if earlier:
                mine = after(mine, *earlier)
            return mine[:own_rows] + swap(mine[own_rows:].astype(BF16), "y").astype(F32)

        def gather_group(value):
            mine = jnp.concatenate(
                [value] + [from_ahead(value, "z", DEPTH, step) for step in range(1, DEPTH)], axis=0
            )
            return mine, swap(mine, "c")

        def scatter_group(mine):
            total = mine[:own_rows]
            received = []
            for step in range(1, DEPTH):
                part = mine[step * own_rows : (step + 1) * own_rows].astype(BF16)
                received.append(from_ahead(part, "z", DEPTH, DEPTH - step))
                total = total + received[-1].astype(F32)
            return total, received[0]

        gains_parts = ordered(norm_gains, swap(norm_gains, "y"), row)
        gains_parts = ordered(gains_parts, swap(gains_parts, "c"), core)
        gains_own = gains_parts.transpose(2, 1, 0, 3).reshape(1, 4 * block).astype(BF16)
        attend_width = mix_width + context_width
        extra = 8
        attend_own = jnp.concatenate(
            [attend_own, jnp.pad(gains_own, ((0, extra - 1), (0, attend_width - 4 * block)))], axis=0
        )

        def quartered(weight):
            whole = weight[:, : DEPTH * main].reshape(-1, DEPTH, main).transpose(1, 0, 2)
            rest = weight[:, DEPTH * main :].reshape(-1, DEPTH, quarter - main).transpose(1, 0, 2)
            return whole, rest

        def unquartered(whole, rest):
            return jnp.concatenate(
                [
                    whole.transpose(1, 0, 2).reshape(-1, DEPTH * main),
                    rest.transpose(1, 0, 2).reshape(-1, DEPTH * (quarter - main)),
                ],
                axis=1,
            )

        def over_z(pieces):
            return [from_ahead(piece, "z", DEPTH, step + 1) for step, piece in enumerate(pieces)]

        def quarter_pieces(pieces):
            return [
                lax.dynamic_index_in_dim(pieces, (depth - step) % DEPTH, 0, keepdims=False)
                for step in range(DEPTH)
            ]

        def by_depth(received):
            result = jnp.zeros((DEPTH * block, received[0].shape[1]), BF16)
            for step in range(DEPTH):
                result = lax.dynamic_update_slice(
                    result, received[step], ((depth + step) % DEPTH * block, 0)
                )
            return result

        def over_x(piece):
            return [from_ahead(piece, "x", side_size, ahead) for ahead in range(1, side_size)]

        gate_whole, gate_rest = quartered(gate_up_weight[:, 0].astype(BF16))
        up_whole, up_rest = quartered(gate_up_weight[:, 1].astype(BF16))
        gate_up_pieces = quarter_pieces(
            jnp.concatenate([gate_whole, up_whole, gate_rest, up_rest], axis=2)
        )
        down_pieces = quarter_pieces(jnp.concatenate(quartered(down_weight.astype(BF16).T), axis=2))

        attend_sent, rows_sent, *gate_up_sent = gated([attend_own, rows_own, *gate_up_pieces[1:]])
        gate_up_own = over_z(gate_up_sent)
        attend_across = [[attend_sent] + over_x(attend_sent)]
        rows_row = swap(rows_sent, "y")

        rows_half = jnp.concatenate([rows_own, rows_row], axis=0)
        rows_half, *attend_sent = gated(
            [rows_half, attend_own, attend_own, attend_own], *attend_across[0][1:], *gate_up_own
        )
        rows_in = jnp.concatenate([rows_half, swap(rows_half, "c")], axis=0)
        gate_up_own = by_depth(gate_up_pieces[:1] + gate_up_own)
        gate_up_own = after(gate_up_own, rows_row, *attend_across[0][1:])
        full_gate_up = lax.all_gather(gate_up_own, ("y", "x"), axis=0, tiled=True)
        full_gate_up = full_gate_up.reshape(2, width, 2 * quarter)
        near_pieces = [
            from_ahead(attend_sent[0], "z", DEPTH, 1),
            from_ahead(attend_sent[2], "z", DEPTH, 3),
        ]

        far_sent, *near_sent = gated([attend_sent[1], *near_pieces], rows_in)
        far_piece = from_ahead(far_sent, "z", DEPTH, 2)
        near_across = [[piece] + over_x(piece) for piece in near_sent]

        far_sent, *down_sent = gated(
            [far_piece, *down_pieces[1:]], *near_across[0][1:], *near_across[1][1:]
        )
        attend_across += [near_across[0], [far_sent] + over_x(far_sent), near_across[1]]
        down_received = over_z(down_sent)
        down_own = after(by_depth(down_pieces[:1] + down_received), full_gate_up)
        full_down = lax.all_gather(down_own, ("y", "x"), axis=0, tiled=True).reshape(2, width, quarter)

        full_attend = jnp.zeros((side_size, DEPTH, block, attend_width), BF16)
        gains_all = jnp.zeros((side_size, DEPTH, 4, block), BF16)
        for step in range(DEPTH):
            for ahead in range(side_size):
                piece = attend_across[step][ahead]
                place = ((side + ahead) % side_size, (depth + step) % DEPTH, 0, 0)
                full_attend = lax.dynamic_update_slice(full_attend, piece[None, None, :block], place)
                gains_piece = piece[block : block + 1, : 4 * block].reshape(1, 1, 4, block)
                gains_all = lax.dynamic_update_slice(gains_all, gains_piece, place)
        full_attend = full_attend.reshape(width, attend_width)
        gains_all = gains_all.astype(F32).transpose(2, 0, 1, 3).reshape(4, width)

        residual_in = rows_own.astype(F32)
        factor_one = lax.rsqrt(jnp.mean(residual_in * residual_in, axis=-1, keepdims=True) + norm_eps)
        start = jnp.stack(
            [
                ((row ^ dr) * 2 + (core ^ dc)) * own_rows
                for dc in range(2)
                for dr in range(2)
            ]
        )
        order = (start[:, None] + jnp.arange(own_rows)[None, :]).reshape(total_rows)
        seg_parts = segments.reshape(2, 2, own_rows)
        seg_parts = rolled(rolled(seg_parts, row, 0), core, 1)
        seg_rows = seg_parts.transpose(1, 0, 2).reshape(total_rows)
        places = order
        half_width = head_width // 2
        frequency = rope_base ** (-2.0 * jnp.arange(half_width, dtype=F32) / head_width)
        angles = places.astype(F32)[:, None] * frequency[None, :]
        cosine_table, sine_table = jnp.cos(angles), jnp.sin(angles)
        tables = (
            cosine_table,
            sine_table,
            order[:, None],
            order[None, :],
            seg_rows[:, None],
            seg_rows[None, :],
        )
        rows_one, queries, key_vectors, value_rows, logsum, context_flat, mine, other = pl.pallas_call(
            functools.partial(attend_kernel, group_size, head_width),
            in_specs=whole(9),
            out_specs=whole(8),
            out_shape=[
                shape((total_rows, width)),
                shape((total_rows, context_width)),
                shape((total_rows, head_width)),
                shape((total_rows, head_width)),
                shape((group_size, total_rows, 1), F32),
                shape((total_rows, context_width)),
                shape((total_rows // 2, width), F32),
                shape((total_rows // 2, width)),
            ],
            compiler_params=params,
        )(rows_in, gains_all[:1], full_attend, *tables)
        attend_sum = scatter_sequence(mine, after(other, *down_received))
        post_one, factor_two = norm_forward(attend_sum, gains_all[1])
        hidden_state = residual_in + post_one
        normed_two, factor_three = norm_forward(hidden_state, gains_all[2])

        rows_two = gather_group(normed_two.astype(BF16))
        activated, gate_factor, up_factor = zip(
            *[gate_up_call(rows, full_gate_up, main) for rows in rows_two]
        )
        received = swap(down_call(activated[1], full_down, BF16), "c")
        feed_sum = scatter_group(down_call(activated[0], full_down, F32, received))[0]
        post_two, factor_four = norm_forward(feed_sum, gains_all[3])
        layer_output = unarrange((hidden_state + post_two).astype(BF16))

        upstream = arrange(cotangent).astype(F32)
        feed_slope, gain_four = norm_backward(feed_sum, factor_four, gains_all[3], upstream)
        feed_slope_rows = gather_group(feed_slope.astype(BF16))
        def ffn_total(left, right):
            return weight_slope_call(left, right).reshape(2 * width, -1)

        def reduce_ffn(total):
            return lax.psum_scatter(total, ("y", "x"), scatter_dimension=0, tiled=True)

        down_total = ffn_total(feed_slope_rows, activated)
        later_rows = gated(feed_slope_rows, down_total)
        backs = [
            feed_back_call(
                later_rows[place],
                full_down,
                full_gate_up,
                gate_factor[place],
                up_factor[place],
                main,
                (F32, BF16)[place],
            )
            for place in range(2)
        ]
        received = swap(backs[1][1], "c")
        normed_two_slope, first_received = scatter_group(backs[0][1] + received.astype(F32))

        def owned(pieces):
            return rolled(jnp.stack(pieces), (DEPTH - depth) % DEPTH, 0)

        down_pieces = quarter_pieces(reduce_ffn(down_total).reshape(DEPTH, block, quarter))
        gate_up_total = ffn_total(rows_two, gated([back[0] for back in backs], first_received))
        gate_up_mine = reduce_ffn(gate_up_total)

        hidden_part, gain_three = norm_backward(
            hidden_state, factor_three, gains_all[2], normed_two_slope
        )
        hidden_slope = upstream + hidden_part
        attend_slope, gain_two = norm_backward(attend_sum, factor_two, gains_all[1], hidden_slope)

        attend_slope = after(attend_slope, gate_up_total)

        slope_sent, *down_sent = gated([attend_slope.astype(BF16), *down_pieces[1:]])
        attend_slope_rows = gather_sequence(slope_sent)
        down_received = over_z(down_sent)
        down_parts = owned(down_pieces[:1] + down_received)
        down_grad = unquartered(down_parts[:, :, :main], down_parts[:, :, main:]).T.astype(F32)
        mixed_slope, mine, other = pl.pallas_call(
            functools.partial(attend_back_kernel, group_size, head_width),
            in_specs=whole(12),
            out_specs=whole(3),
            out_shape=[
                shape((total_rows, mix_width)),
                shape((total_rows // 2, width), F32),
                shape((total_rows // 2, width)),
            ],
            compiler_params=params,
        )(attend_slope_rows, full_attend, queries, key_vectors, value_rows, logsum, *tables)
        def gradient(left, right):
            total = transposed(left, right).astype(BF16)
            return total.reshape(side_size, DEPTH, block, right.shape[1])

        def side_parts(total):
            return [
                lax.dynamic_index_in_dim(total, (side + ahead) % side_size, 0, keepdims=False)
                for ahead in range(side_size)
            ]

        def over_side(parts):
            across = parts[0].astype(F32)
            for ahead in range(1, side_size):
                across = across + from_ahead(parts[ahead], "x", side_size, side_size - ahead).astype(F32)
            return across

        gate_up_pieces = quarter_pieces(gate_up_mine.reshape(DEPTH, block, 2 * quarter))
        project_parts = side_parts(gradient(rows_one, mixed_slope))
        sent = gated([*project_parts[1:], *gate_up_pieces[1:]], *down_received)
        gate_up_received = over_z(sent[side_size - 1 :])
        project_here = after(project_parts[0], *gate_up_received)
        project_across = over_side([project_here] + sent[: side_size - 1])
        normed_one_slope = scatter_sequence(mine, other)

        input_part, gain_one = norm_backward(residual_in, factor_one, gains_all[0], normed_one_slope)
        input_grad = unarrange(hidden_slope + input_part)

        gain_sum = jnp.stack([gain_one, gain_two, gain_three, gain_four], axis=0)
        lines = -(-4 * block // context_width)
        gain_sum = gain_sum.reshape(4, side_size, DEPTH, block).transpose(1, 2, 0, 3)
        gain_sum = gain_sum.reshape(side_size, DEPTH, 4 * block).astype(BF16)
        gain_sum = jnp.pad(gain_sum, ((0, 0), (0, 0), (0, lines * context_width - 4 * block)))
        gain_sum = jnp.pad(
            gain_sum.reshape(side_size, DEPTH, lines, context_width),
            ((0, 0), (0, 0), (0, extra - lines), (0, 0)),
        )
        output_total = jnp.concatenate(
            [gradient(attend_slope_rows, context_flat), gain_sum], axis=2
        )

        output_parts = side_parts(output_total)
        project_pieces = quarter_pieces(project_across.astype(BF16))
        project_received = over_z(gated(project_pieces[1:], *gate_up_received))
        output_sent = gated(output_parts[1:], project_across)
        output_across = over_side(output_parts[:1] + output_sent)
        output_pieces = quarter_pieces(output_across.astype(BF16))
        output_received = over_z(gated(output_pieces[1:], *project_received))
        gate_up_sent = gated([gate_up_pieces[0], *gate_up_received], project_received[0])
        gate_up_grad, gate_up_new, gate_up_mean_new, gate_up_power_new = gate_up_adam_call(
            depth, gate_up_sent, gate_up_weight, gate_up_mean, gate_up_power, main
        )
        output_received = gated(output_received, gate_up_grad)

        def own_sum(across, received):
            mine = lax.dynamic_index_in_dim(across, depth, 0, keepdims=False)
            for part in received:
                mine = mine + part.astype(F32)
            return mine

        project_grad = own_sum(project_across, project_received).reshape(project_weight.shape)
        output_mine = own_sum(output_across, output_received)
        output_grad = output_mine[:block].T
        gain_part = output_mine[block : block + lines].reshape(1, -1)[:, : 4 * block]
        gain_part = gain_part.reshape(4, 2, 2, norm_gains.shape[1]).transpose(1, 2, 0, 3)
        for axis, place in (("y", row), ("c", core)):
            parts = rolled(gain_part, place, 0)
            gain_part = parts[0] + swap(parts[1], axis)
        gains_grad = gain_part

        project_new, project_mean_new, project_power_new, unused_one = adam_step(
            project_weight, project_grad, project_mean, project_power
        )
        output_new, output_mean_new, output_power_new, unused_two = adam_step(
            output_weight, output_grad, output_mean, output_power
        )
        down_new, down_mean_new, down_power_new, unused_four = adam_step(
            down_weight, down_grad, down_mean, down_power
        )
        unused_five, gains_mean_new, gains_power_new, gains_step = adam_step(
            norm_gains, gains_grad, gains_mean, gains_power
        )
        return (
            layer_output,
            input_grad,
            project_grad,
            project_new,
            project_mean_new,
            project_power_new,
            output_grad,
            output_new,
            output_mean_new,
            output_power_new,
            gate_up_grad,
            gate_up_new,
            gate_up_mean_new,
            gate_up_power_new,
            down_grad,
            down_new,
            down_mean_new,
            down_power_new,
            gains_grad,
            gains_step,
            gains_mean_new,
            gains_power_new,
        )

    return per_device


def solution(mesh):
    side_size = mesh.shape["fsdp"] // DEPTH
    fine = Mesh(mesh.devices.reshape(DEPTH, side_size, 2, 2), ("z", "x", "y", "c"))
    fsdp = ("z", "x")
    tp = ("y", "c")
    both = fsdp + tp
    rows = P(both, None)
    project = P(fsdp, tp, None, None)
    across = P(tp, fsdp)
    gate_up = P(fsdp, None, tp)
    gains = P(None, both)
    in_specs = (
        (rows, P(fsdp), rows, project, across, gate_up, across, gains)
        + (project,) * 2
        + (across,) * 2
        + (gate_up,) * 2
        + (across,) * 2
        + (gains,) * 2
    )
    out_specs = (
        (rows, rows)
        + (project,) * 4
        + (across,) * 4
        + (gate_up,) * 4
        + (across,) * 4
        + (gains,) * 4
    )
    return jax.shard_map(
        make_device(side_size), mesh=fine, in_specs=in_specs, out_specs=out_specs, check_vma=False
    )
```

time: 1100 us -> 940 us (0.85)
  waiting for transfers between devices: 667 us -> 501 us
  Pallas kernels: 0 us -> 155 us
  matrix products: 132 us -> 9.14 us
  other arithmetic: 111 us -> 62.2 us
  starting transfers between devices: 69.3 us -> 82.1 us
  between operations: 3.55 us -> 15.1 us
    ppermute x59 -> x16, waiting for transfers between devices: 384 us -> 53.5 us  [swap(): return lax.ppermute(value, axis, [(0, 1), (1, 0)])]
    ppermute x11 -> x39, waiting for transfers between devices: 242 us -> 440 us  [from_ahead(): lax.ppermute(value, axis, [(j, (j - step) % size) for j in range(size)])]
    pallas_call x0 -> x11, Pallas kernels: none -> 155 us  [the longest x2 42.1 us: feed_back_call(): pl.pallas_call(functools.partial(feed_back_kernel, main), grid=(count,),...]
    dot_general x16 -> x0, matrix products: 91.4 us -> none  [the longest x1 15.1 us: per_device(): jnp.dot(feed_slope_rows, full_down, preferred_element_type=F32)]
    ppermute x11 -> x39, starting transfers between devices: 12.9 us -> 66.5 us  [from_ahead(): lax.ppermute(value, axis, [(j, (j - step) % size) for j in range(size)])]
    unnamed x346 -> x129, local copies, waits for them, and re-layouts: 67.7 us -> 22.4 us
    ppermute x4 -> x0, waiting for transfers between devices: 40.6 us -> none  [swap_two(): lax.ppermute(value, (first, second), [(0, 3), (3, 0), (1, 2), (2, 1)])]
    ppermute x59 -> x16, starting transfers between devices: 50.6 us -> 15.2 us  [swap(): return lax.ppermute(value, axis, [(0, 1), (1, 0)])]
  transfers between devices with their start and end apart: 74 -> 59, of which waited for: 37 -> 31; matrix products, arithmetic and copies ran while one was open for 23% -> 16% of each run, Pallas kernels for 0% -> 14%
where the time goes in v2:
time: 940 us; the launch traced here: 930 us
  waiting for transfers between devices  501 us (53%)
  Pallas kernels  155 us (16%)
  local copies, waits for them, and re-layouts  106 us (11%)
  starting transfers between devices  82.1 us (9%)
  other arithmetic  62.2 us (7%)
  between operations  15.1 us (2%)
    ppermute x39, waiting for transfers between devices, from_ahead(): lax.ppermute(value, axis, [(j, (j - step) % size) for j in range(size)])  440 us
    ppermute x39, starting transfers between devices, from_ahead(): lax.ppermute(value, axis, [(j, (j - step) % size) for j in range(size)])  66.5 us
    ppermute x16, waiting for transfers between devices, swap(): return lax.ppermute(value, axis, [(0, 1), (1, 0)])  53.5 us
    pallas_call x2, Pallas kernels, feed_back_call(): pl.pallas_call(functools.partial(feed_back_kernel, main), grid=(count,),...  42.1 us
    pallas_call x2, Pallas kernels, weight_slope_call(): pl.pallas_call(weight_slope_kernel, grid=(count, 3), in_specs=[left_block...  29.7 us
    pallas_call x2, Pallas kernels, gate_up_call(): pl.pallas_call(functools.partial(gate_up_kernel, main), grid=(count,), in...  22.8 us
    unnamed x129, local copies, waits for them, and re-layouts  22.4 us
    pallas_call x1, Pallas kernels, gate_up_adam_call(): pl.pallas_call(functools.partial(gate_up_adam_kernel, main), grid_spec=pl...  19.7 us
  transfers between devices with their start and end apart: 59, of which 31 were waited for; matrix products, arithmetic and copies ran while one was open for 16% of the time, Pallas kernels for 14%

profile of v2, /device:TPU:1, one launch (start us, length us, event | category | flops | bytes accessed | tf_op | source)
XLA Modules:
  0.0 930.0 jit_solution(15031706573896269163)
XLA Ops:
  16.7 3.7 concatenate.76
  36.6 9.6 %collective-permute-done.4 = bf16[288,1152]{1,0:T(8,128)(2,1)} collective-permute-done((bf16[288,1152]{1,0:T(8,128)(2,1)}, bf16[288,1152]{1,0:T(8,128)(2,1)}, u32[]{:S(2)}, u32[]{:S(2)}) %collective-permute-start.4) | collective-permute-done | bytes 663584 | tf_op jit(solution)/shard_map/ppermute | solution.py:70
  48.1 40.5 %collective-permute-done.5 = bf16[288,1152]{1,0:T(8,128)(2,1)} collective-permute-done((bf16[288,1152]{1,0:T(8,128)(2,1)}, bf16[288,1152]{1,0:T(8,128)(2,1)}, u32[]{:S(2)}, u32[]{:S(2)}) %collective-permute-start.5) | collective-permute-done | bytes 663584 | tf_op jit(solution)/shard_map/ppermute | solution.py:70
  106.3 3.5 broadcast_in_dim.49
  117.5 9.4 %collective-permute-done.8 = bf16[296,1536]{1,0:T(8,128)(2,1)} collective-permute-done((bf16[296,1536]{1,0:T(8,128)(2,1)}, bf16[296,1536]{1,0:T(8,128)(2,1)}, u32[]{:S(2)}, u32[]{:S(2)}) %collective-permute-start.8) | collective-permute-done | bytes 909344 | tf_op jit(solution)/shard_map/ppermute | solution.py:70
  126.9 19.6 %collective-permute-done.9 = bf16[296,1536]{1,0:T(8,128)(2,1)S(1)} collective-permute-done((bf16[296,1536]{1,0:T(8,128)(2,1)}, bf16[296,1536]{1,0:T(8,128)(2,1)S(1)}, u32[]{:S(2)}, u32[]{:S(2)}) %collective-permute-start.9) | collective-permute-done | bytes 909344 | tf_op jit(solution)/shard_map/ppermute | solution.py:70
  155.4 33.8 %collective-permute-done.11 = bf16[296,1536]{1,0:T(8,128)(2,1)} collective-permute-done((bf16[296,1536]{1,0:T(8,128)(2,1)}, bf16[296,1536]{1,0:T(8,128)(2,1)}, u32[]{:S(2)}, u32[]{:S(2)}) %collective-permute-start.11) | collective-permute-done | bytes 909344 | tf_op jit(solution)/shard_map/ppermute | solution.py:70
  189.3 39.0 %collective-permute-done.12 = bf16[296,1536]{1,0:T(8,128)(2,1)} collective-permute-done((bf16[296,1536]{1,0:T(8,128)(2,1)S(1)}, bf16[296,1536]{1,0:T(8,128)(2,1)}, u32[]{:S(2)}, u32[]{:S(2)}) %collective-permute-start.12) | collective-permute-done | bytes 909344 | tf_op jit(solution)/shard_map/ppermute | solution.py:70
  239.0 23.9 %collective-permute-done.15 = bf16[288,576]{1,0:T(8,128)(2,1)} collective-permute-done((bf16[288,576]{1,0:T(8,128)(2,1)}, bf16[288,576]{1,0:T(8,128)(2,1)}, u32[]{:S(2)}, u32[]{:S(2)}) %collective-permute-start.15) | collective-permute-done | bytes 331808 | tf_op jit(solution)/shard_map/ppermute | solution.py:70
  272.0 12.1 %shard_map.345 = (bf16[512,2304]{1,0:T(8,128)(2,1)}, bf16[512,512]{1,0:T(8,128)(2,1)}, bf16[512,256]{1,0:T(8,128)(2,1)}, bf16[512,256]{1,0:T(8,128)(2,1)}, f32[2...) custom-call(bf16[512,2304]{1,0:T(8,128)(2,1)} %constant_dynamic-update-slice_fusion, ...), custom_call_target="tpu_custom_call" | custom-call | tf_op jit(solution)/shard_map/pallas_call | solution.py:596
  291.3 15.8 %collective-permute-done.18 = bf16[128,2304]{1,0:T(8,128)(2,1)S(1)} collective-permute-done((bf16[128,2304]{1,0:T(8,128)(2,1)S(1)}, bf16[128,2304]{1,0:T(8,128)(2,1)S(1)}, u32[]{:S(2)}, u32[]{:S(2)}) %collective-permute-start.18) | collective-permute-done | bytes 589856 | tf_op jit(solution)/shard_map/ppermute | solution.py:66
  314.8 11.2 %collective-permute-done.21 = bf16[128,2304]{1,0:T(8,128)(2,1)S(1)} collective-permute-done((bf16[128,2304]{1,0:T(8,128)(2,1)S(1)}, bf16[128,2304]{1,0:T(8,128)(2,1)S(1)}, u32[]{:S(2)}, u32[]{:S(2)}) %collective-permute-start.21) | collective-permute-done | bytes 589856 | tf_op jit(solution)/shard_map/ppermute | solution.py:70
  326.0 26.3 %collective-permute-done.20 = bf16[128,2304]{1,0:T(8,128)(2,1)S(1)} collective-permute-done((bf16[128,2304]{1,0:T(8,128)(2,1)S(1)}, bf16[128,2304]{1,0:T(8,128)(2,1)S(1)}, u32[]{:S(2)}, u32[]{:S(2)}) %collective-permute-start.20) | collective-permute-done | bytes 589856 | tf_op jit(solution)/shard_map/ppermute | solution.py:70
  354.5 4.3 collective-permute-done.22.rows.left_other
  358.7 11.4 %shard_map.347 = (bf16[2,512,576]{2,1,0:T(8,128)(2,1)}, bf16[2,512,576]{2,1,0:T(8,128)(2,1)}, bf16[2,512,576]{2,1,0:T(8,128)(2,1)}) custom-call(bf16[512,2304]{1,0:T(8,128)(2,1)} %collective-permute-done.22.rows.left_other, bf16[2,2304,1152]{2,1,0:T(8,128)(2,1)} %bitcast.221), custom_call_target="tpu_custom_call" | custom-call | tf_op jit(solution)/shard_map/pallas_call | solution.py:247
  370.2 7.4 shard_map.348
  378.0 11.4 %shard_map.346 = (bf16[2,512,576]{2,1,0:T(8,128)(2,1)}, bf16[2,512,576]{2,1,0:T(8,128)(2,1)}, bf16[2,512,576]{2,1,0:T(8,128)(2,1)}) custom-call(bf16[512,2304]{1,0:T(8,128)(2,1)} %copy-done, bf16[2,2304,1152]{2,1,0:T(8,128)(2,1)} %bitcast.222), custom_call_target="tpu_custom_call" | custom-call | tf_op jit(solution)/shard_map/pallas_call | solution.py:247
  389.4 8.4 shard_map.349
  401.6 12.8 %collective-permute-start.24 = (bf16[128,2304]{1,0:T(8,128)(2,1)}, bf16[128,2304]{1,0:T(8,128)(2,1)}, u32[]{:S(2)}, u32[]{:S(2)}) collective-permute-start(bf16[128,2304]{1,0:T(8,128)(2,1)} %get-tuple-element.284), channel_id=1, source_target_pairs={{0,8},{8,16},{16,24},{24,0},{1,9},{9,17},{17,25},{25,1},{2,10},{10... | collective-permute-start | bytes 1769480 | tf_op jit(solution)/shard_map/ppermute | solution.py:70
  424.0 5.3 collective-permute-done.24
  429.3 12.8 %collective-permute-done.26 = bf16[128,2304]{1,0:T(8,128)(2,1)} collective-permute-done((bf16[128,2304]{1,0:T(8,128)(2,1)}, bf16[128,2304]{1,0:T(8,128)(2,1)}, u32[]{:S(2)}, u32[]{:S(2)}) %collective-permute-start.26) | collective-permute-done | bytes 589856 | tf_op jit(solution)/shard_map/ppermute | solution.py:70
  442.1 25.3 %collective-permute-done.25 = bf16[128,2304]{1,0:T(8,128)(2,1)} collective-permute-done((bf16[128,2304]{1,0:T(8,128)(2,1)}, bf16[128,2304]{1,0:T(8,128)(2,1)}, u32[]{:S(2)}, u32[]{:S(2)}) %collective-permute-start.25) | collective-permute-done | bytes 589856 | tf_op jit(solution)/shard_map/ppermute | solution.py:70
  475.2 12.9 %collective-permute-done.29 = bf16[128,2304]{1,0:T(8,128)(2,1)S(1)} collective-permute-done((bf16[128,2304]{1,0:T(8,128)(2,1)S(1)}, bf16[128,2304]{1,0:T(8,128)(2,1)S(1)}, u32[]{:S(2)}, u32[]{:S(2)}) %collective-permute-start.29) | collective-permute-done | bytes 589856 | tf_op jit(solution)/shard_map/ppermute | solution.py:70
  488.1 24.3 %collective-permute-done.28 = bf16[128,2304]{1,0:T(8,128)(2,1)S(1)} collective-permute-done((bf16[128,2304]{1,0:T(8,128)(2,1)S(1)}, bf16[128,2304]{1,0:T(8,128)(2,1)S(1)}, u32[]{:S(2)}, u32[]{:S(2)}) %collective-permute-start.28) | collective-permute-done | bytes 589856 | tf_op jit(solution)/shard_map/ppermute | solution.py:70
  516.2 4.3 collective-permute-done.30.left_other.slopes
  520.5 12.4 %shard_map.350 = bf16[2,2304,576]{2,1,0:T(8,128)(2,1)} custom-call(bf16[512,2304]{1,0:T(8,128)(2,1)} %copy-done.1, bf16[512,2304]{1,0:T(8,128)(2,1)} %collective-permute-done.30.left_other.slopes, bf16[2,512,576]{2,1,0:T(8,128)(2,1)} %get-tuple-element.114.active.right_mine, bf16[2,512,576]{2,1,0:T(8,128)(2,1)} %get-tuple-element.116.active.right_other), custom_call_target="tpu_custom_call" | custom-call | tf_op jit(solution)/shard_map/pallas_call | solution.py:350
  532.9 20.3 %shard_map.352 = (bf16[2,512,1152]{2,1,0:T(8,128)(2,1)}, bf16[512,2304]{1,0:T(8,128)(2,1)}) custom-call(bf16[512,2304]{1,0:T(8,128)(2,1)} %collective-permute-done.30.left_other.slopes, bf16[2,2304,576]{2,1,0:T(8,128)(2,1)} %bitcast.227, bf16[2,2304,1152]{2,1,0:T(8,128)(2,1)} %bitcast.223, bf16[2,512,576]{2,1,0:T(8,128)(2,1)} %get-tuple-element.122.gate_factor, ...), custom_call_target="tpu_custom_call" | custom-call | tf_op jit(solution)/shard_map/pallas_call | solution.py:322
  553.6 21.8 %shard_map.351 = (bf16[2,512,1152]{2,1,0:T(8,128)(2,1)}, f32[512,2304]{1,0:T(8,128)}) custom-call(bf16[512,2304]{1,0:T(8,128)(2,1)} %copy-done.1, bf16[2,2304,576]{2,1,0:T(8,128)(2,1)} %bitcast.228, bf16[2,2304,1152]{2,1,0:T(8,128)(2,1)} %bitcast.224, bf16[2,512,576]{2,1,0:T(8,128)(2,1)} %get-tuple-element.118.gate_factor, ...), custom_call_target="tpu_custom_call" | custom-call | tf_op jit(solution)/shard_map/pallas_call | solution.py:322
  575.4 5.8 fusion.48
  582.4 13.4 %collective-permute-start.32 = (bf16[128,2304]{1,0:T(8,128)(2,1)S(1)}, bf16[128,2304]{1,0:T(8,128)(2,1)S(1)}, u32[]{:S(2)}, u32[]{:S(2)}) collective-permute-start(bf16[128,2304]{1,0:T(8,128)(2,1)S(1)} %get-tuple-element.281), channel_id=1, source_target_pairs={{0,8},{8,16},{16,24},{24,0},{1,9},{9,17},{17,25},{25,1},{2,10},{10... | collective-permute-start | bytes 1769480 | tf_op jit(solution)/shard_map/ppermute | solution.py:70
  595.7 12.9 %collective-permute-done.32 = bf16[128,2304]{1,0:T(8,128)(2,1)S(1)} collective-permute-done((bf16[128,2304]{1,0:T(8,128)(2,1)S(1)}, bf16[128,2304]{1,0:T(8,128)(2,1)S(1)}, u32[]{:S(2)}, u32[]{:S(2)}) %collective-permute-start.32) | collective-permute-done | bytes 589856 | tf_op jit(solution)/shard_map/ppermute | solution.py:70
  609.5 17.4 %shard_map.353 = bf16[2,2304,1152]{2,1,0:T(8,128)(2,1)} custom-call(bf16[512,2304]{1,0:T(8,128)(2,1)} %copy-done, bf16[512,2304]{1,0:T(8,128)(2,1)} %collective-permute-done.22.rows.left_other, bf16[2,512,1152]{2,1,0:T(8,128)(2,1)} %get-tuple-element.127.right_mine, bf16[2,512,1152]{2,1,0:T(8,128)(2,1)} %get-tuple-element.128.right_other), custom_call_target="tpu_custom_call" | custom-call | tf_op jit(solution)/shard_map/pallas_call | solution.py:350
  630.3 12.3 %collective-permute-done.34 = bf16[128,2304]{1,0:T(8,128)(2,1)S(1)} collective-permute-done((bf16[128,2304]{1,0:T(8,128)(2,1)}, bf16[128,2304]{1,0:T(8,128)(2,1)S(1)}, u32[]{:S(2)}, u32[]{:S(2)}) %collective-permute-start.34) | collective-permute-done | bytes 589856 | tf_op jit(solution)/shard_map/ppermute | solution.py:70
  642.6 26.0 %collective-permute-done.33 = bf16[128,2304]{1,0:T(8,128)(2,1)S(1)} collective-permute-done((bf16[128,2304]{1,0:T(8,128)(2,1)}, bf16[128,2304]{1,0:T(8,128)(2,1)S(1)}, u32[]{:S(2)}, u32[]{:S(2)}) %collective-permute-start.33) | collective-permute-done | bytes 589856 | tf_op jit(solution)/shard_map/ppermute | solution.py:70
  682.3 21.6 %collective-permute-done.35 = bf16[128,2304]{1,0:T(8,128)(2,1)S(1)} collective-permute-done((bf16[128,2304]{1,0:T(8,128)(2,1)S(1)}, bf16[128,2304]{1,0:T(8,128)(2,1)S(1)}, u32[]{:S(2)}, u32[]{:S(2)}) %collective-permute-start.35) | collective-permute-done | bytes 589856 | tf_op jit(solution)/shard_map/ppermute | solution.py:66
  705.9 6.2 collective-permute-done.40
  714.9 12.7 %shard_map.354 = (bf16[512,1024]{1,0:T(8,128)(2,1)}, f32[256,2304]{1,0:T(8,128)}, bf16[256,2304]{1,0:T(8,128)(2,1)}) custom-call(bf16[512,2304]{1,0:T(8,128)(2,1)} %constant_dynamic-update-slice_fusion.8.slopes, bf16[2304,1536]{1,0:T(8,128)(2,1)} %bitcast.36.weights, bf16[512,512]{1,0:T(8,128)(2,1)} %get-tuple-element.131.queries, ...), custom_call_target="tpu_custom_call" | custom-call | tf_op jit(solution)/shard_map/pallas_call | solution.py:672
  729.4 4.6 convolution_convert_fusion
  736.7 6.6 reduce-scatter.5.cloned.1.call-done
  753.7 4.6 convolution_convert_fusion.1
  762.0 4.0 collective-permute-done.38
  774.7 42.6 %collective-permute-done.43.refs_2_ = bf16[288,1152]{1,0:T(8,128)(2,1)} collective-permute-done((bf16[288,1152]{1,0:T(8,128)(2,1)}, bf16[288,1152]{1,0:T(8,128)(2,1)}, u32[]{:S(2)}, u32[]{:S(2)}) %collective-permute-start.43) | collective-permute-done | bytes 663584 | tf_op jit(solution)/shard_map/ppermute | solution.py:70
  817.4 5.2 convert_add_fusion
  823.8 4.8 multiply_add_fusion
  833.7 15.0 %collective-permute-done.49 = bf16[4,296,512]{2,1,0:T(8,128)(2,1)S(1)} collective-permute-done((bf16[4,296,512]{2,1,0:T(8,128)(2,1)S(1)}, bf16[4,296,512]{2,1,0:T(8,128)(2,1)S(1)}, u32[]{:S(2)}, u32[]{:S(2)}) %collective-permute-start.49) | collective-permute-done | bytes 1212448 | tf_op jit(solution)/shard_map/ppermute | solution.py:70
  851.5 30.8 %collective-permute-done.47 = bf16[288,1024]{1,0:T(8,128)(2,1)S(1)} collective-permute-done((bf16[288,1024]{1,0:T(8,128)(2,1)S(1)}, bf16[288,1024]{1,0:T(8,128)(2,1)S(1)}, u32[]{:S(2)}, u32[]{:S(2)}) %collective-permute-start.47) | collective-permute-done | bytes 589856 | tf_op jit(solution)/shard_map/ppermute | solution.py:70
  891.4 19.7 %shard_map.355 = (f32[288,2,2304]{2,1,0:T(2,128)}, f32[288,2,2304]{2,1,0:T(2,128)}, f32[288,2,2304]{2,1,0:T(2,128)}, f32[288,2,2304]{2,1,0:T(2,128)}) custom-call(s32[1]{0:T(128)} %bitcast.90.depth, bf16[288,1152]{1,0:T(8,128)(2,1)} %get-tuple-element.155.refs_0_, bf16[288,1152]{1,0:T(8,128)(2,1)} %collective-permute-done.42.refs_1_, ...), custom_call_target="tpu_custom_call" | custom-call | tf_op jit(solution)/shard_map/pallas_call | solution.py:387
  913.4 5.2 multiply_add_fusion.2
  (390 shorter events, 200.1 us)
Async XLA Ops:
  7.2 262.4 %all-gather.3.cloned.1.call-start = ((), (), s32[]{:S(2)}) async-start(), calls=%async_computation.2 | async-start | bytes 13271040 | tf_op jit(solution)/shard_map/all_gather | solution.py:539
  7.9 17.2 %collective-permute-start = (bf16[4,72]{1,0:T(4,128)(2,1)S(1)}, bf16[4,72]{1,0:T(4,128)(2,1)S(1)}, u32[]{:S(2)}, u32[]{:S(2)}) collective-permute-start(bf16[4,72]{1,0:T(4,128)(2,1)S(1)} %convert.58), channel_id=1, source_target_pairs={{0,2},{2,0},{1,3},{3,1},{4,6},{6,4},{5,7},{7,5},{8,10},{10,8},{9,1... | collective-permute-start | bytes 1736 | tf_op jit(solution)/shard_map/ppermute | solution.py:66
  28.4 17.7 %collective-permute-start.4 = (bf16[288,1152]{1,0:T(8,128)(2,1)}, bf16[288,1152]{1,0:T(8,128)(2,1)}, u32[]{:S(2)}, u32[]{:S(2)}) collective-permute-start(bf16[288,1152]{1,0:T(8,128)(2,1)} %get-tuple-element.96), channel_id=1, source_target_pairs={{0,24},{8,0},{16,8},{24,16},{1,25},{9,1},{17,9},{25,17},{2,26},{10... | collective-permute-start | bytes 1990664 | tf_op jit(solution)/shard_map/ppermute | solution.py:70
  31.8 56.8 %collective-permute-start.5 = (bf16[288,1152]{1,0:T(8,128)(2,1)}, bf16[288,1152]{1,0:T(8,128)(2,1)}, u32[]{:S(2)}, u32[]{:S(2)}) collective-permute-start(bf16[288,1152]{1,0:T(8,128)(2,1)} %get-tuple-element.97), channel_id=1, source_target_pairs={{0,16},{8,24},{16,0},{24,8},{1,17},{9,25},{17,1},{25,9},{2,18},{10... | collective-permute-start | bytes 1990664 | tf_op jit(solution)/shard_map/ppermute | solution.py:70
  31.8 58.8 %collective-permute-start.6 = (bf16[288,1152]{1,0:T(8,128)(2,1)}, bf16[288,1152]{1,0:T(8,128)(2,1)}, u32[]{:S(2)}, u32[]{:S(2)}) collective-permute-start(bf16[288,1152]{1,0:T(8,128)(2,1)} %get-tuple-element.98), channel_id=1, source_target_pairs={{0,8},{8,16},{16,24},{24,0},{1,9},{9,17},{17,25},{25,1},{2,10},{10... | collective-permute-start | bytes 1990664 | tf_op jit(solution)/shard_map/ppermute | solution.py:70
  32.2 60.3 %collective-permute-start.3 = (bf16[296,1536]{1,0:T(8,128)(2,1)}, bf16[296,1536]{1,0:T(8,128)(2,1)}, u32[]{:S(2)}, u32[]{:S(2)}) collective-permute-start(bf16[296,1536]{1,0:T(8,128)(2,1)} %fusion.19), channel_id=1, source_target_pairs={{0,4},{4,0},{1,5},{5,1},{2,6},{6,2},{3,7},{7,3},{8,12},{12,8},{9,1... | collective-permute-start | bytes 2727944 | tf_op jit(solution)/shard_map/ppermute | solution.py:70
  36.3 56.3 %collective-permute-start.2 = (bf16[128,2304]{1,0:T(8,128)(2,1)S(1)}, bf16[128,2304]{1,0:T(8,128)(2,1)}, u32[]{:S(2)}, u32[]{:S(2)}) collective-permute-start(bf16[128,2304]{1,0:T(8,128)(2,1)S(1)} %copy.158), channel_id=1, source_target_pairs={{0,2},{2,0},{1,3},{3,1},{4,6},{6,4},{5,7},{7,5},{8,10},{10,8},{9,1... | collective-permute-start | bytes 1769480 | tf_op jit(solution)/shard_map/ppermute | solution.py:66
  92.6 277.6 %all-gather.5.cloned.1.call-start = ((), (), s32[]{:S(2)}) async-start(), calls=%async_computation.3 | async-start | bytes 7372800 | tf_op jit(solution)/shard_map/all_gather | solution.py:556
  104.8 22.1 %collective-permute-start.8 = (bf16[296,1536]{1,0:T(8,128)(2,1)}, bf16[296,1536]{1,0:T(8,128)(2,1)}, u32[]{:S(2)}, u32[]{:S(2)}) collective-permute-start(bf16[296,1536]{1,0:T(8,128)(2,1)} %fusion.19), channel_id=1, source_target_pairs={{0,24},{8,0},{16,8},{24,16},{1,25},{9,1},{17,9},{25,17},{2,26},{10... | collective-permute-start | bytes 2727944 | tf_op jit(solution)/shard_map/ppermute | solution.py:70
  104.8 41.7 %collective-permute-start.9 = (bf16[296,1536]{1,0:T(8,128)(2,1)}, bf16[296,1536]{1,0:T(8,128)(2,1)S(1)}, u32[]{:S(2)}, u32[]{:S(2)}) collective-permute-start(bf16[296,1536]{1,0:T(8,128)(2,1)} %fusion.19), channel_id=1, source_target_pairs={{0,8},{8,16},{16,24},{24,0},{1,9},{9,17},{17,25},{25,1},{2,10},{10... | collective-permute-start | bytes 2727944 | tf_op jit(solution)/shard_map/ppermute | solution.py:70
  146.5 42.7 %collective-permute-start.11 = (bf16[296,1536]{1,0:T(8,128)(2,1)}, bf16[296,1536]{1,0:T(8,128)(2,1)}, u32[]{:S(2)}, u32[]{:S(2)}) collective-permute-start(bf16[296,1536]{1,0:T(8,128)(2,1)} %fusion.19), channel_id=1, source_target_pairs={{0,16},{8,24},{16,0},{24,8},{1,17},{9,25},{17,1},{25,9},{2,18},{10... | collective-permute-start | bytes 2727944 | tf_op jit(solution)/shard_map/ppermute | solution.py:70
  147.7 41.6 %collective-permute-start.10 = (bf16[296,1536]{1,0:T(8,128)(2,1)}, bf16[296,1536]{1,0:T(8,128)(2,1)}, u32[]{:S(2)}, u32[]{:S(2)}) collective-permute-start(bf16[296,1536]{1,0:T(8,128)(2,1)} %collective-permute-done.8), channel_id=1, source_target_pairs={{0,4},{4,0},{1,5},{5,1},{2,6},{6,2},{3,7},{7,3},{8,12},{12,8},{9,1... | collective-permute-start | bytes 2727944 | tf_op jit(solution)/shard_map/ppermute | solution.py:70
  148.8 79.4 %collective-permute-start.12 = (bf16[296,1536]{1,0:T(8,128)(2,1)S(1)}, bf16[296,1536]{1,0:T(8,128)(2,1)}, u32[]{:S(2)}, u32[]{:S(2)}) collective-permute-start(bf16[296,1536]{1,0:T(8,128)(2,1)S(1)} %collective-permute-done.9), channel_id=1, source_target_pairs={{0,4},{4,0},{1,5},{5,1},{2,6},{6,2},{3,7},{7,3},{8,12},{12,8},{9,1... | collective-permute-start | bytes 2727944 | tf_op jit(solution)/shard_map/ppermute | solution.py:70
  229.3 34.8 %collective-permute-start.13 = (bf16[296,1536]{1,0:T(8,128)(2,1)}, bf16[296,1536]{1,0:T(8,128)(2,1)}, u32[]{:S(2)}, u32[]{:S(2)}) collective-permute-start(bf16[296,1536]{1,0:T(8,128)(2,1)} %collective-permute-done.11), channel_id=1, source_target_pairs={{0,4},{4,0},{1,5},{5,1},{2,6},{6,2},{3,7},{7,3},{8,12},{12,8},{9,1... | collective-permute-start | bytes 2727944 | tf_op jit(solution)/shard_map/ppermute | solution.py:70
  235.6 27.4 %collective-permute-start.15 = (bf16[288,576]{1,0:T(8,128)(2,1)}, bf16[288,576]{1,0:T(8,128)(2,1)}, u32[]{:S(2)}, u32[]{:S(2)}) collective-permute-start(bf16[288,576]{1,0:T(8,128)(2,1)} %get-tuple-element.110), channel_id=1, source_target_pairs={{0,16},{8,24},{16,0},{24,8},{1,17},{9,25},{17,1},{25,9},{2,18},{10... | collective-permute-start | bytes 995336 | tf_op jit(solution)/shard_map/ppermute | solution.py:70
  237.5 26.5 %collective-permute-start.16 = (bf16[288,576]{1,0:T(8,128)(2,1)}, bf16[288,576]{1,0:T(8,128)(2,1)S(1)}, u32[]{:S(2)}, u32[]{:S(2)}) collective-permute-start(bf16[288,576]{1,0:T(8,128)(2,1)} %get-tuple-element.111), channel_id=1, source_target_pairs={{0,8},{8,16},{16,24},{24,0},{1,9},{9,17},{17,25},{25,1},{2,10},{10... | collective-permute-start | bytes 995336 | tf_op jit(solution)/shard_map/ppermute | solution.py:70
  269.6 404.6 %reduce-scatter.3.cloned.1.call-start = ((), (), s32[]{:S(2)}) async-start(), calls=%async_computation.4 | async-start | bytes 7372800 | tf_op jit(solution)/shard_map/reduce_scatter | solution.py:633
  289.8 17.4 %collective-permute-start.18 = (bf16[128,2304]{1,0:T(8,128)(2,1)S(1)}, bf16[128,2304]{1,0:T(8,128)(2,1)S(1)}, u32[]{:S(2)}, u32[]{:S(2)}) collective-permute-start(bf16[128,2304]{1,0:T(8,128)(2,1)S(1)} %slice.412), channel_id=1, source_target_pairs={{0,2},{2,0},{1,3},{3,1},{4,6},{6,4},{5,7},{7,5},{8,10},{10,8},{9,1... | collective-permute-start | bytes 1769480 | tf_op jit(solution)/shard_map/ppermute | solution.py:66
  309.9 16.1 %collective-permute-start.21 = (bf16[128,2304]{1,0:T(8,128)(2,1)S(1)}, bf16[128,2304]{1,0:T(8,128)(2,1)S(1)}, u32[]{:S(2)}, u32[]{:S(2)}) collective-permute-start(bf16[128,2304]{1,0:T(8,128)(2,1)S(1)} %multiply_convert_fusion.1), channel_id=1, source_target_pairs={{0,8},{8,16},{16,24},{24,0},{1,9},{9,17},{17,25},{25,1},{2,10},{10... | collective-permute-start | bytes 1769480 | tf_op jit(solution)/shard_map/ppermute | solution.py:70
  311.1 41.2 %collective-permute-start.20 = (bf16[128,2304]{1,0:T(8,128)(2,1)S(1)}, bf16[128,2304]{1,0:T(8,128)(2,1)S(1)}, u32[]{:S(2)}, u32[]{:S(2)}) collective-permute-start(bf16[128,2304]{1,0:T(8,128)(2,1)S(1)} %multiply_convert_fusion.1), channel_id=1, source_target_pairs={{0,16},{8,24},{16,0},{24,8},{1,17},{9,25},{17,1},{25,9},{2,18},{10... | collective-permute-start | bytes 1769480 | tf_op jit(solution)/shard_map/ppermute | solution.py:70
  313.2 39.0 %collective-permute-start.19 = (bf16[128,2304]{1,0:T(8,128)(2,1)S(1)}, bf16[128,2304]{1,0:T(8,128)(2,1)S(1)}, u32[]{:S(2)}, u32[]{:S(2)}) collective-permute-start(bf16[128,2304]{1,0:T(8,128)(2,1)S(1)} %multiply_convert_fusion.1), channel_id=1, source_target_pairs={{0,24},{8,0},{16,8},{24,16},{1,25},{9,1},{17,9},{25,17},{2,26},{10... | collective-permute-start | bytes 1769480 | tf_op jit(solution)/shard_map/ppermute | solution.py:70
  401.6 27.7 %collective-permute-start.24 = (bf16[128,2304]{1,0:T(8,128)(2,1)}, bf16[128,2304]{1,0:T(8,128)(2,1)}, u32[]{:S(2)}, u32[]{:S(2)}) collective-permute-start(bf16[128,2304]{1,0:T(8,128)(2,1)} %get-tuple-element.284), channel_id=1, source_target_pairs={{0,8},{8,16},{16,24},{24,0},{1,9},{9,17},{17,25},{25,1},{2,10},{10... | collective-permute-start | bytes 1769480 | tf_op jit(solution)/shard_map/ppermute | solution.py:70
  414.4 27.7 %collective-permute-start.26 = (bf16[128,2304]{1,0:T(8,128)(2,1)}, bf16[128,2304]{1,0:T(8,128)(2,1)}, u32[]{:S(2)}, u32[]{:S(2)}) collective-permute-start(bf16[128,2304]{1,0:T(8,128)(2,1)} %get-tuple-element.285), channel_id=1, source_target_pairs={{0,24},{8,0},{16,8},{24,16},{1,25},{9,1},{17,9},{25,17},{2,26},{10... | collective-permute-start | bytes 1769480 | tf_op jit(solution)/shard_map/ppermute | solution.py:70
  415.3 52.1 %collective-permute-start.25 = (bf16[128,2304]{1,0:T(8,128)(2,1)}, bf16[128,2304]{1,0:T(8,128)(2,1)}, u32[]{:S(2)}, u32[]{:S(2)}) collective-permute-start(bf16[128,2304]{1,0:T(8,128)(2,1)} %get-tuple-element.286), channel_id=1, source_target_pairs={{0,16},{8,24},{16,0},{24,8},{1,17},{9,25},{17,1},{25,9},{2,18},{10... | collective-permute-start | bytes 1769480 | tf_op jit(solution)/shard_map/ppermute | solution.py:70
  471.8 16.3 %collective-permute-start.29 = (bf16[128,2304]{1,0:T(8,128)(2,1)S(1)}, bf16[128,2304]{1,0:T(8,128)(2,1)S(1)}, u32[]{:S(2)}, u32[]{:S(2)}) collective-permute-start(bf16[128,2304]{1,0:T(8,128)(2,1)S(1)} %get-tuple-element.297), channel_id=1, source_target_pairs={{0,8},{8,16},{16,24},{24,0},{1,9},{9,17},{17,25},{25,1},{2,10},{10... | collective-permute-start | bytes 1769480 | tf_op jit(solution)/shard_map/ppermute | solution.py:70
  471.8 40.7 %collective-permute-start.28 = (bf16[128,2304]{1,0:T(8,128)(2,1)S(1)}, bf16[128,2304]{1,0:T(8,128)(2,1)S(1)}, u32[]{:S(2)}, u32[]{:S(2)}) collective-permute-start(bf16[128,2304]{1,0:T(8,128)(2,1)S(1)} %get-tuple-element.297), channel_id=1, source_target_pairs={{0,16},{8,24},{16,0},{24,8},{1,17},{9,25},{17,1},{25,9},{2,18},{10... | collective-permute-start | bytes 1769480 | tf_op jit(solution)/shard_map/ppermute | solution.py:70
  473.0 39.5 %collective-permute-start.27 = (bf16[128,2304]{1,0:T(8,128)(2,1)S(1)}, bf16[128,2304]{1,0:T(8,128)(2,1)S(1)}, u32[]{:S(2)}, u32[]{:S(2)}) collective-permute-start(bf16[128,2304]{1,0:T(8,128)(2,1)S(1)} %get-tuple-element.297), channel_id=1, source_target_pairs={{0,24},{8,0},{16,8},{24,16},{1,25},{9,1},{17,9},{25,17},{2,26},{10... | collective-permute-start | bytes 1769480 | tf_op jit(solution)/shard_map/ppermute | solution.py:70
  532.9 210.4 %reduce-scatter.5.cloned.1.call-start = ((), (), s32[]{:S(2)}) async-start(), calls=%async_computation.5 | async-start | bytes 13271040 | tf_op jit(solution)/shard_map/reduce_scatter | solution.py:633
  553.2 22.2 %collective-permute-start.31 = (bf16[512,2304]{1,0:T(8,128)(2,1)}, bf16[512,2304]{1,0:T(8,128)(2,1)}, u32[]{:S(2)}, u32[]{:S(2)}) collective-permute-start(bf16[512,2304]{1,0:T(8,128)(2,1)} %get-tuple-element.124), channel_id=1, source_target_pairs={{0,1},{1,0},{2,3},{3,2},{4,5},{5,4},{6,7},{7,6},{8,9},{9,8},{10,11... | collective-permute-start | bytes 7077896 | tf_op jit(solution)/shard_map/ppermute | solution.py:66
  582.4 26.3 %collective-permute-start.32 = (bf16[128,2304]{1,0:T(8,128)(2,1)S(1)}, bf16[128,2304]{1,0:T(8,128)(2,1)S(1)}, u32[]{:S(2)}, u32[]{:S(2)}) collective-permute-start(bf16[128,2304]{1,0:T(8,128)(2,1)S(1)} %get-tuple-element.281), channel_id=1, source_target_pairs={{0,8},{8,16},{16,24},{24,0},{1,9},{9,17},{17,25},{25,1},{2,10},{10... | collective-permute-start | bytes 1769480 | tf_op jit(solution)/shard_map/ppermute | solution.py:70
  626.9 15.7 %collective-permute-start.34 = (bf16[128,2304]{1,0:T(8,128)(2,1)}, bf16[128,2304]{1,0:T(8,128)(2,1)S(1)}, u32[]{:S(2)}, u32[]{:S(2)}) collective-permute-start(bf16[128,2304]{1,0:T(8,128)(2,1)} %get-tuple-element.282), channel_id=1, source_target_pairs={{0,24},{8,0},{16,8},{24,16},{1,25},{9,1},{17,9},{25,17},{2,26},{10... | collective-permute-start | bytes 1769480 | tf_op jit(solution)/shard_map/ppermute | solution.py:70
  627.2 41.4 %collective-permute-start.33 = (bf16[128,2304]{1,0:T(8,128)(2,1)}, bf16[128,2304]{1,0:T(8,128)(2,1)S(1)}, u32[]{:S(2)}, u32[]{:S(2)}) collective-permute-start(bf16[128,2304]{1,0:T(8,128)(2,1)} %get-tuple-element.283), channel_id=1, source_target_pairs={{0,16},{8,24},{16,0},{24,8},{1,17},{9,25},{17,1},{25,9},{2,18},{10... | collective-permute-start | bytes 1769480 | tf_op jit(solution)/shard_map/ppermute | solution.py:70
  676.9 27.0 %collective-permute-start.35 = (bf16[128,2304]{1,0:T(8,128)(2,1)S(1)}, bf16[128,2304]{1,0:T(8,128)(2,1)S(1)}, u32[]{:S(2)}, u32[]{:S(2)}) collective-permute-start(bf16[128,2304]{1,0:T(8,128)(2,1)S(1)} %subtract_multiply_fusion), channel_id=1, source_target_pairs={{0,2},{2,0},{1,3},{3,1},{4,6},{6,4},{5,7},{7,5},{8,10},{10,8},{9,1... | collective-permute-start | bytes 1769480 | tf_op jit(solution)/shard_map/ppermute | solution.py:66
  680.8 25.1 %collective-permute-start.39 = (bf16[288,576]{1,0:T(8,128)(2,1)}, bf16[288,576]{1,0:T(8,128)(2,1)S(1)}, u32[]{:S(2)}, u32[]{:S(2)}) collective-permute-start(bf16[288,576]{1,0:T(8,128)(2,1)} %get-tuple-element.139), channel_id=1, source_target_pairs={{0,24},{8,0},{16,8},{24,16},{1,25},{9,1},{17,9},{25,17},{2,26},{10... | collective-permute-start | bytes 995336 | tf_op jit(solution)/shard_map/ppermute | solution.py:70
  681.8 30.2 %collective-permute-start.40 = (bf16[288,576]{1,0:T(8,128)(2,1)}, bf16[288,576]{1,0:T(8,128)(2,1)S(1)}, u32[]{:S(2)}, u32[]{:S(2)}) collective-permute-start(bf16[288,576]{1,0:T(8,128)(2,1)} %get-tuple-element.140), channel_id=1, source_target_pairs={{0,16},{8,24},{16,0},{24,8},{1,17},{9,25},{17,1},{25,9},{2,18},{10... | collective-permute-start | bytes 995336 | tf_op jit(solution)/shard_map/ppermute | solution.py:70
  681.9 30.2 %collective-permute-start.41 = (bf16[288,576]{1,0:T(8,128)(2,1)}, bf16[288,576]{1,0:T(8,128)(2,1)S(1)}, u32[]{:S(2)}, u32[]{:S(2)}) collective-permute-start(bf16[288,576]{1,0:T(8,128)(2,1)} %get-tuple-element.141), channel_id=1, source_target_pairs={{0,8},{8,16},{16,24},{24,0},{1,9},{9,17},{17,25},{25,1},{2,10},{10... | collective-permute-start | bytes 995336 | tf_op jit(solution)/shard_map/ppermute | solution.py:70
  727.7 21.0 %collective-permute-start.37 = (bf16[256,2304]{1,0:T(8,128)(2,1)}, bf16[256,2304]{1,0:T(8,128)(2,1)S(1)}, u32[]{:S(2)}, u32[]{:S(2)}) collective-permute-start(bf16[256,2304]{1,0:T(8,128)(2,1)} %get-tuple-element.136), channel_id=1, source_target_pairs={{0,1},{1,0},{2,3},{3,2},{4,5},{5,4},{6,7},{7,6},{8,9},{9,8},{10,11... | collective-permute-start | bytes 3538952 | tf_op jit(solution)/shard_map/ppermute | solution.py:66
  746.5 70.8 %collective-permute-start.45 = (bf16[4,288,1024]{2,1,0:T(8,128)(2,1)}, bf16[4,288,1024]{2,1,0:T(8,128)(2,1)}, u32[]{:S(2)}, u32[]{:S(2)}) collective-permute-start(bf16[4,288,1024]{2,1,0:T(8,128)(2,1)} %get-tuple-element.146), channel_id=1, source_target_pairs={{0,4},{4,0},{1,5},{5,1},{2,6},{6,2},{3,7},{7,3},{8,12},{12,8},{9,1... | collective-permute-start | bytes 7077896 | tf_op jit(solution)/shard_map/ppermute | solution.py:70
  758.3 16.4 %collective-permute-start.42 = (bf16[288,1152]{1,0:T(8,128)(2,1)}, bf16[288,1152]{1,0:T(8,128)(2,1)}, u32[]{:S(2)}, u32[]{:S(2)}) collective-permute-start(bf16[288,1152]{1,0:T(8,128)(2,1)} %get-tuple-element.142), channel_id=1, source_target_pairs={{0,24},{8,0},{16,8},{24,16},{1,25},{9,1},{17,9},{25,17},{2,26},{10... | collective-permute-start | bytes 1990664 | tf_op jit(solution)/shard_map/ppermute | solution.py:70
  761.3 56.0 %collective-permute-start.43 = (bf16[288,1152]{1,0:T(8,128)(2,1)}, bf16[288,1152]{1,0:T(8,128)(2,1)}, u32[]{:S(2)}, u32[]{:S(2)}) collective-permute-start(bf16[288,1152]{1,0:T(8,128)(2,1)} %get-tuple-element.143), channel_id=1, source_target_pairs={{0,16},{8,24},{16,0},{24,8},{1,17},{9,25},{17,1},{25,9},{2,18},{10... | collective-permute-start | bytes 1990664 | tf_op jit(solution)/shard_map/ppermute | solution.py:70
  761.3 56.0 %collective-permute-start.44 = (bf16[288,1152]{1,0:T(8,128)(2,1)}, bf16[288,1152]{1,0:T(8,128)(2,1)}, u32[]{:S(2)}, u32[]{:S(2)}) collective-permute-start(bf16[288,1152]{1,0:T(8,128)(2,1)} %get-tuple-element.144), channel_id=1, source_target_pairs={{0,8},{8,16},{16,24},{24,0},{1,9},{9,17},{17,25},{25,1},{2,10},{10... | collective-permute-start | bytes 1990664 | tf_op jit(solution)/shard_map/ppermute | solution.py:70
  822.7 26.0 %collective-permute-start.49 = (bf16[4,296,512]{2,1,0:T(8,128)(2,1)S(1)}, bf16[4,296,512]{2,1,0:T(8,128)(2,1)S(1)}, u32[]{:S(2)}, u32[]{:S(2)}) collective-permute-start(bf16[4,296,512]{2,1,0:T(8,128)(2,1)S(1)} %dynamic-slice_bitcast_fusion.2), channel_id=1, source_target_pairs={{0,4},{4,0},{1,5},{5,1},{2,6},{6,2},{3,7},{7,3},{8,12},{12,8},{9,1... | collective-permute-start | bytes 3637256 | tf_op jit(solution)/shard_map/ppermute | solution.py:70
  828.8 22.7 %collective-permute-start.46 = (bf16[288,1024]{1,0:T(8,128)(2,1)S(1)}, bf16[288,1024]{1,0:T(8,128)(2,1)S(1)}, u32[]{:S(2)}, u32[]{:S(2)}) collective-permute-start(bf16[288,1024]{1,0:T(8,128)(2,1)S(1)} %get-tuple-element.147), channel_id=1, source_target_pairs={{0,24},{8,0},{16,8},{24,16},{1,25},{9,1},{17,9},{25,17},{2,26},{10... | collective-permute-start | bytes 1769480 | tf_op jit(solution)/shard_map/ppermute | solution.py:70
  828.9 53.4 %collective-permute-start.47 = (bf16[288,1024]{1,0:T(8,128)(2,1)S(1)}, bf16[288,1024]{1,0:T(8,128)(2,1)S(1)}, u32[]{:S(2)}, u32[]{:S(2)}) collective-permute-start(bf16[288,1024]{1,0:T(8,128)(2,1)S(1)} %get-tuple-element.148), channel_id=1, source_target_pairs={{0,16},{8,24},{16,0},{24,8},{1,17},{9,25},{17,1},{25,9},{2,18},{10... | collective-permute-start | bytes 1769480 | tf_op jit(solution)/shard_map/ppermute | solution.py:70
  832.3 50.0 %collective-permute-start.48 = (bf16[288,1024]{1,0:T(8,128)(2,1)S(1)}, bf16[288,1024]{1,0:T(8,128)(2,1)S(1)}, u32[]{:S(2)}, u32[]{:S(2)}) collective-permute-start(bf16[288,1024]{1,0:T(8,128)(2,1)S(1)} %get-tuple-element.149), channel_id=1, source_target_pairs={{0,8},{8,16},{16,24},{24,0},{1,9},{9,17},{17,25},{25,1},{2,10},{10... | collective-permute-start | bytes 1769480 | tf_op jit(solution)/shard_map/ppermute | solution.py:70
  882.3 28.9 %collective-permute-start.50 = (bf16[296,512]{1,0:T(8,128)(2,1)}, bf16[296,512]{1,0:T(8,128)(2,1)}, u32[]{:S(2)}, u32[]{:S(2)}) collective-permute-start(bf16[296,512]{1,0:T(8,128)(2,1)} %get-tuple-element.152), channel_id=1, source_target_pairs={{0,24},{8,0},{16,8},{24,16},{1,25},{9,1},{17,9},{25,17},{2,26},{10... | collective-permute-start | bytes 909320 | tf_op jit(solution)/shard_map/ppermute | solution.py:70
  882.3 28.8 %collective-permute-start.51 = (bf16[296,512]{1,0:T(8,128)(2,1)}, bf16[296,512]{1,0:T(8,128)(2,1)}, u32[]{:S(2)}, u32[]{:S(2)}) collective-permute-start(bf16[296,512]{1,0:T(8,128)(2,1)} %get-tuple-element.153), channel_id=1, source_target_pairs={{0,16},{8,24},{16,0},{24,8},{1,17},{9,25},{17,1},{25,9},{2,18},{10... | collective-permute-start | bytes 909320 | tf_op jit(solution)/shard_map/ppermute | solution.py:70
  883.0 28.2 %collective-permute-start.52 = (bf16[296,512]{1,0:T(8,128)(2,1)}, bf16[296,512]{1,0:T(8,128)(2,1)}, u32[]{:S(2)}, u32[]{:S(2)}) collective-permute-start(bf16[296,512]{1,0:T(8,128)(2,1)} %get-tuple-element.154), channel_id=1, source_target_pairs={{0,8},{8,16},{16,24},{24,0},{1,9},{9,17},{17,25},{25,1},{2,10},{10... | collective-permute-start | bytes 909320 | tf_op jit(solution)/shard_map/ppermute | solution.py:70
  (69 other events, 557.7 us)
Sparse Core Ops, SparseCore 0:
  92.7 145.7 all-gather.2
  269.7 76.0 all-gather.4
  533.0 75.6 reduce-scatter.2
  627.0 116.2 reduce-scatter.4

commit v3 on v2

--- a/solution.py
+++ b/solution.py
@@ -467,20 +467,27 @@
 
         def scatter_group(mine):
             total = mine[:own_rows]
-            received = []
             for step in range(1, DEPTH):
                 part = mine[step * own_rows : (step + 1) * own_rows].astype(BF16)
-                received.append(from_ahead(part, "z", DEPTH, DEPTH - step))
-                total = total + received[-1].astype(F32)
-            return total, received[0]
+                total = total + from_ahead(part, "z", DEPTH, DEPTH - step).astype(F32)
+            return total
 
         gains_parts = ordered(norm_gains, swap(norm_gains, "y"), row)
         gains_parts = ordered(gains_parts, swap(gains_parts, "c"), core)
-        gains_own = gains_parts.transpose(2, 1, 0, 3).reshape(1, 4 * block).astype(BF16)
+        gains_parts = gains_parts.transpose(2, 1, 0, 3).reshape(1, 4 * block)
+        gains_high = lax.optimization_barrier(gains_parts.astype(BF16))
+        gains_low = (gains_parts - gains_high.astype(F32)).astype(BF16)
         attend_width = mix_width + context_width
         extra = 8
         attend_own = jnp.concatenate(
-            [attend_own, jnp.pad(gains_own, ((0, extra - 1), (0, attend_width - 4 * block)))], axis=0
+            [
+                attend_own,
+                jnp.pad(
+                    jnp.concatenate([gains_high, gains_low], axis=0),
+                    ((0, extra - 2), (0, attend_width - 4 * block)),
+                ),
+            ],
+            axis=0,
         )
 
         def quartered(weight):
@@ -524,20 +531,19 @@
         )
         down_pieces = quarter_pieces(jnp.concatenate(quartered(down_weight.astype(BF16).T), axis=2))
 
-        attend_sent, rows_sent, *gate_up_sent = gated([attend_own, rows_own, *gate_up_pieces[1:]])
-        gate_up_own = over_z(gate_up_sent)
+        attend_sent, rows_sent, *down_sent = gated([attend_own, rows_own, *down_pieces[1:]])
+        down_received = over_z(down_sent)
         attend_across = [[attend_sent] + over_x(attend_sent)]
         rows_row = swap(rows_sent, "y")
 
         rows_half = jnp.concatenate([rows_own, rows_row], axis=0)
         rows_half, *attend_sent = gated(
-            [rows_half, attend_own, attend_own, attend_own], *attend_across[0][1:], *gate_up_own
+            [rows_half, attend_own, attend_own, attend_own], *attend_across[0][1:], *down_received
         )
         rows_in = jnp.concatenate([rows_half, swap(rows_half, "c")], axis=0)
-        gate_up_own = by_depth(gate_up_pieces[:1] + gate_up_own)
-        gate_up_own = after(gate_up_own, rows_row, *attend_across[0][1:])
-        full_gate_up = lax.all_gather(gate_up_own, ("y", "x"), axis=0, tiled=True)
-        full_gate_up = full_gate_up.reshape(2, width, 2 * quarter)
+        down_own = by_depth(down_pieces[:1] + down_received)
+        down_own = after(down_own, rows_row, *attend_across[0][1:])
+        full_down = lax.all_gather(down_own, ("y", "x"), axis=0, tiled=True).reshape(2, width, quarter)
         near_pieces = [
             from_ahead(attend_sent[0], "z", DEPTH, 1),
             from_ahead(attend_sent[2], "z", DEPTH, 3),
@@ -547,25 +553,28 @@
         far_piece = from_ahead(far_sent, "z", DEPTH, 2)
         near_across = [[piece] + over_x(piece) for piece in near_sent]
 
-        far_sent, *down_sent = gated(
-            [far_piece, *down_pieces[1:]], *near_across[0][1:], *near_across[1][1:]
+        far_sent, *gate_up_sent = gated(
+            [far_piece, *gate_up_pieces[1:]], *near_across[0][1:], *near_across[1][1:]
         )
         attend_across += [near_across[0], [far_sent] + over_x(far_sent), near_across[1]]
-        down_received = over_z(down_sent)
-        down_own = after(by_depth(down_pieces[:1] + down_received), full_gate_up)
-        full_down = lax.all_gather(down_own, ("y", "x"), axis=0, tiled=True).reshape(2, width, quarter)
+        gate_up_received = over_z(gate_up_sent)
+        gate_up_own = by_depth(gate_up_pieces[:1] + gate_up_received)
+        gate_up_own = after(gate_up_own, full_down, *attend_across[2][1:])
+        full_gate_up = lax.all_gather(gate_up_own, ("y", "x"), axis=0, tiled=True)
+        full_gate_up = full_gate_up.reshape(2, width, 2 * quarter)
 
         full_attend = jnp.zeros((side_size, DEPTH, block, attend_width), BF16)
-        gains_all = jnp.zeros((side_size, DEPTH, 4, block), BF16)
+        gains_all = jnp.zeros((side_size, DEPTH, 4, block), F32)
         for step in range(DEPTH):
             for ahead in range(side_size):
                 piece = attend_across[step][ahead]
                 place = ((side + ahead) % side_size, (depth + step) % DEPTH, 0, 0)
                 full_attend = lax.dynamic_update_slice(full_attend, piece[None, None, :block], place)
-                gains_piece = piece[block : block + 1, : 4 * block].reshape(1, 1, 4, block)
+                gains_pair = piece[block : block + 2, : 4 * block].astype(F32)
+                gains_piece = (gains_pair[0] + gains_pair[1]).reshape(1, 1, 4, block)
                 gains_all = lax.dynamic_update_slice(gains_all, gains_piece, place)
         full_attend = full_attend.reshape(width, attend_width)
-        gains_all = gains_all.astype(F32).transpose(2, 0, 1, 3).reshape(4, width)
+        gains_all = gains_all.transpose(2, 0, 1, 3).reshape(4, width)
 
         residual_in = rows_own.astype(F32)
         factor_one = lax.rsqrt(jnp.mean(residual_in * residual_in, axis=-1, keepdims=True) + norm_eps)
@@ -609,17 +618,17 @@
             ],
             compiler_params=params,
         )(rows_in, gains_all[:1], full_attend, *tables)
-        attend_sum = scatter_sequence(mine, after(other, *down_received))
+        attend_sum = scatter_sequence(mine, other)
         post_one, factor_two = norm_forward(attend_sum, gains_all[1])
         hidden_state = residual_in + post_one
         normed_two, factor_three = norm_forward(hidden_state, gains_all[2])
 
-        rows_two = gather_group(normed_two.astype(BF16))
+        rows_two = gather_group(after(normed_two.astype(BF16), *gate_up_received))
         activated, gate_factor, up_factor = zip(
             *[gate_up_call(rows, full_gate_up, main) for rows in rows_two]
         )
         received = swap(down_call(activated[1], full_down, BF16), "c")
-        feed_sum = scatter_group(down_call(activated[0], full_down, F32, received))[0]
+        feed_sum = scatter_group(down_call(activated[0], full_down, F32, received))
         post_two, factor_four = norm_forward(feed_sum, gains_all[3])
         layer_output = unarrange((hidden_state + post_two).astype(BF16))
 
@@ -647,13 +656,13 @@
             for place in range(2)
         ]
         received = swap(backs[1][1], "c")
-        normed_two_slope, first_received = scatter_group(backs[0][1] + received.astype(F32))
+        normed_two_slope = scatter_group(backs[0][1] + received.astype(F32))
 
         def owned(pieces):
             return rolled(jnp.stack(pieces), (DEPTH - depth) % DEPTH, 0)
 
         down_pieces = quarter_pieces(reduce_ffn(down_total).reshape(DEPTH, block, quarter))
-        gate_up_total = ffn_total(rows_two, gated([back[0] for back in backs], first_received))
+        gate_up_total = ffn_total(rows_two, gated([back[0] for back in backs], received))
         gate_up_mine = reduce_ffn(gate_up_total)
 
         hidden_part, gain_three = norm_backward(
@@ -716,8 +725,9 @@
             gain_sum.reshape(side_size, DEPTH, lines, context_width),
             ((0, 0), (0, 0), (0, extra - lines), (0, 0)),
         )
+        context_later = after(context_flat, gate_up_received[0])
         output_total = jnp.concatenate(
-            [gradient(attend_slope_rows, context_flat), gain_sum], axis=2
+            [gradient(attend_slope_rows, context_later), gain_sum], axis=2
         )
 
         output_parts = side_parts(output_total)
@@ -755,6 +765,7 @@
         output_new, output_mean_new, output_power_new, unused_two = adam_step(
             output_weight, output_grad, output_mean, output_power
         )
+        down_grad = after(down_grad, project_received[0])
         down_new, down_mean_new, down_power_new, unused_four = adam_step(
             down_weight, down_grad, down_mean, down_power
         )

time: 940 us -> 902 us (0.960)
  waiting for transfers between devices: 501 us -> 474 us
  starting transfers between devices: 82.1 us -> 71.7 us
    ppermute x39, starting transfers between devices: 66.5 us -> 52.6 us  [from_ahead(): lax.ppermute(value, axis, [(j, (j - step) % size) for j in range(size)])]
    ppermute x39, waiting for transfers between devices: 440 us -> 429 us  [from_ahead(): lax.ppermute(value, axis, [(j, (j - step) % size) for j in range(size)])]
    unnamed x129 -> x142, local copies, waits for them, and re-layouts: 22.4 us -> 26.3 us
  transfers between devices with their start and end apart: 59 -> 59, of which waited for: 31 -> 30; matrix products, arithmetic and copies ran while one was open for 16% -> 16% of each run, Pallas kernels for 14% -> 13%
where the time goes in v3:
time: 902 us; the launch traced here: 892 us
  waiting for transfers between devices  474 us (53%)
  Pallas kernels  154 us (17%)
  local copies, waits for them, and re-layouts  102 us (11%)
  starting transfers between devices  71.7 us (8%)
  other arithmetic  67.1 us (7%)
  between operations  15.1 us (2%)
    ppermute x39, waiting for transfers between devices, from_ahead(): lax.ppermute(value, axis, [(j, (j - step) % size) for j in range(size)])  429 us
    ppermute x39, starting transfers between devices, from_ahead(): lax.ppermute(value, axis, [(j, (j - step) % size) for j in range(size)])  52.6 us
    ppermute x16, waiting for transfers between devices, swap(): return lax.ppermute(value, axis, [(0, 1), (1, 0)])  45.1 us
    pallas_call x2, Pallas kernels, feed_back_call(): pl.pallas_call(functools.partial(feed_back_kernel, main), grid=(count,),...  42 us
    pallas_call x2, Pallas kernels, weight_slope_call(): pl.pallas_call(weight_slope_kernel, grid=(count, 3), in_specs=[left_block...  29.9 us
    unnamed x142, local copies, waits for them, and re-layouts  26.3 us
    pallas_call x2, Pallas kernels, gate_up_call(): pl.pallas_call(functools.partial(gate_up_kernel, main), grid=(count,), in...  22.8 us
    pallas_call x1, Pallas kernels, gate_up_adam_call(): pl.pallas_call(functools.partial(gate_up_adam_kernel, main), grid_spec=pl...  19.7 us
  transfers between devices with their start and end apart: 59, of which 30 were waited for; matrix products, arithmetic and copies ran while one was open for 16% of the time, Pallas kernels for 13%

profile of v3, /device:TPU:1, one launch (start us, length us, event | category | flops | bytes accessed | tf_op | source)
XLA Modules:
  0.0 892.0 jit_solution(6755321683308941897)
XLA Ops:
  27.6 5.8 collective-permute-done.4
  34.4 22.5 %collective-permute-done.5 = bf16[288,576]{1,0:T(8,128)(2,1)} collective-permute-done((bf16[288,576]{1,0:T(8,128)(2,1)}, bf16[288,576]{1,0:T(8,128)(2,1)}, u32[]{:S(2)}, u32[]{:S(2)}) %collective-permute-start.5) | collective-permute-done | bytes 331808 | tf_op jit(solution)/shard_map/ppermute | solution.py:70
  69.1 3.7 concatenate.83
  77.3 17.8 %collective-permute-done.8 = bf16[296,1536]{1,0:T(8,128)(2,1)S(1)} collective-permute-done((bf16[296,1536]{1,0:T(8,128)(2,1)}, bf16[296,1536]{1,0:T(8,128)(2,1)S(1)}, u32[]{:S(2)}, u32[]{:S(2)}) %collective-permute-start.8) | collective-permute-done | bytes 909344 | tf_op jit(solution)/shard_map/ppermute | solution.py:70
  95.1 21.0 %collective-permute-done.9 = bf16[296,1536]{1,0:T(8,128)(2,1)S(1)} collective-permute-done((bf16[296,1536]{1,0:T(8,128)(2,1)}, bf16[296,1536]{1,0:T(8,128)(2,1)S(1)}, u32[]{:S(2)}, u32[]{:S(2)}) %collective-permute-start.9) | collective-permute-done | bytes 909344 | tf_op jit(solution)/shard_map/ppermute | solution.py:70
  121.7 35.6 %collective-permute-done.11 = bf16[296,1536]{1,0:T(8,128)(2,1)S(1)} collective-permute-done((bf16[296,1536]{1,0:T(8,128)(2,1)}, bf16[296,1536]{1,0:T(8,128)(2,1)S(1)}, u32[]{:S(2)}, u32[]{:S(2)}) %collective-permute-start.11) | collective-permute-done | bytes 909344 | tf_op jit(solution)/shard_map/ppermute | solution.py:70
  157.3 6.3 collective-permute-done.12
  171.0 10.4 %collective-permute-done.16 = bf16[288,1152]{1,0:T(8,128)(2,1)S(1)} collective-permute-done((bf16[288,1152]{1,0:T(8,128)(2,1)}, bf16[288,1152]{1,0:T(8,128)(2,1)S(1)}, u32[]{:S(2)}, u32[]{:S(2)}) %collective-permute-start.16) | collective-permute-done | bytes 663584 | tf_op jit(solution)/shard_map/ppermute | solution.py:70
  182.3 41.8 %collective-permute-done.17 = bf16[288,1152]{1,0:T(8,128)(2,1)} collective-permute-done((bf16[288,1152]{1,0:T(8,128)(2,1)}, bf16[288,1152]{1,0:T(8,128)(2,1)}, u32[]{:S(2)}, u32[]{:S(2)}) %collective-permute-start.17) | collective-permute-done | bytes 663584 | tf_op jit(solution)/shard_map/ppermute | solution.py:70
  251.4 11.2 %shard_map.345 = (bf16[512,2304]{1,0:T(8,128)(2,1)}, bf16[512,512]{1,0:T(8,128)(2,1)}, bf16[512,256]{1,0:T(8,128)(2,1)}, bf16[512,256]{1,0:T(8,128)(2,1)}, f32[2...) custom-call(bf16[512,2304]{1,0:T(8,128)(2,1)} %copy-done.22, ...), custom_call_target="tpu_custom_call" | custom-call | tf_op jit(solution)/shard_map/pallas_call | solution.py:605
  271.6 11.8 %collective-permute-done.15 = bf16[128,2304]{1,0:T(8,128)(2,1)S(1)} collective-permute-done((bf16[128,2304]{1,0:T(8,128)(2,1)S(1)}, bf16[128,2304]{1,0:T(8,128)(2,1)S(1)}, u32[]{:S(2)}, u32[]{:S(2)}) %collective-permute-start.15) | collective-permute-done | bytes 589856 | tf_op jit(solution)/shard_map/ppermute | solution.py:66
  289.8 10.9 %collective-permute-done.19 = bf16[128,2304]{1,0:T(8,128)(2,1)S(1)} collective-permute-done((bf16[128,2304]{1,0:T(8,128)(2,1)S(1)}, bf16[128,2304]{1,0:T(8,128)(2,1)S(1)}, u32[]{:S(2)}, u32[]{:S(2)}) %collective-permute-start.19) | collective-permute-done | bytes 589856 | tf_op jit(solution)/shard_map/ppermute | solution.py:70
  300.7 37.5 %collective-permute-done.20 = bf16[128,2304]{1,0:T(8,128)(2,1)S(1)} collective-permute-done((bf16[128,2304]{1,0:T(8,128)(2,1)S(1)}, bf16[128,2304]{1,0:T(8,128)(2,1)S(1)}, u32[]{:S(2)}, u32[]{:S(2)}) %collective-permute-start.20) | collective-permute-done | bytes 589856 | tf_op jit(solution)/shard_map/ppermute | solution.py:70
  341.6 4.3 collective-permute-done.22.rows.left_other
  345.9 11.4 %shard_map.347 = (bf16[2,512,576]{2,1,0:T(8,128)(2,1)}, bf16[2,512,576]{2,1,0:T(8,128)(2,1)}, bf16[2,512,576]{2,1,0:T(8,128)(2,1)}) custom-call(bf16[512,2304]{1,0:T(8,128)(2,1)} %collective-permute-done.22.rows.left_other, bf16[2,2304,1152]{2,1,0:T(8,128)(2,1)} %bitcast.219), custom_call_target="tpu_custom_call" | custom-call | tf_op jit(solution)/shard_map/pallas_call | solution.py:247
  357.3 7.4 shard_map.348
  365.1 11.4 %shard_map.346 = (bf16[2,512,576]{2,1,0:T(8,128)(2,1)}, bf16[2,512,576]{2,1,0:T(8,128)(2,1)}, bf16[2,512,576]{2,1,0:T(8,128)(2,1)}) custom-call(bf16[512,2304]{1,0:T(8,128)(2,1)} %copy-done.5, bf16[2,2304,1152]{2,1,0:T(8,128)(2,1)} %bitcast.220), custom_call_target="tpu_custom_call" | custom-call | tf_op jit(solution)/shard_map/pallas_call | solution.py:247
  376.5 8.4 shard_map.349
  400.4 5.3 collective-permute-done.24
  405.7 10.8 %collective-permute-done.26 = bf16[128,2304]{1,0:T(8,128)(2,1)} collective-permute-done((bf16[128,2304]{1,0:T(8,128)(2,1)}, bf16[128,2304]{1,0:T(8,128)(2,1)}, u32[]{:S(2)}, u32[]{:S(2)}) %collective-permute-start.26) | collective-permute-done | bytes 589856 | tf_op jit(solution)/shard_map/ppermute | solution.py:70
  416.5 26.3 %collective-permute-done.25 = bf16[128,2304]{1,0:T(8,128)(2,1)} collective-permute-done((bf16[128,2304]{1,0:T(8,128)(2,1)}, bf16[128,2304]{1,0:T(8,128)(2,1)}, u32[]{:S(2)}, u32[]{:S(2)}) %collective-permute-start.25) | collective-permute-done | bytes 589856 | tf_op jit(solution)/shard_map/ppermute | solution.py:70
  450.4 12.5 %collective-permute-done.29 = bf16[128,2304]{1,0:T(8,128)(2,1)S(1)} collective-permute-done((bf16[128,2304]{1,0:T(8,128)(2,1)S(1)}, bf16[128,2304]{1,0:T(8,128)(2,1)S(1)}, u32[]{:S(2)}, u32[]{:S(2)}) %collective-permute-start.29) | collective-permute-done | bytes 589856 | tf_op jit(solution)/shard_map/ppermute | solution.py:70
  463.0 24.7 %collective-permute-done.28 = bf16[128,2304]{1,0:T(8,128)(2,1)S(1)} collective-permute-done((bf16[128,2304]{1,0:T(8,128)(2,1)S(1)}, bf16[128,2304]{1,0:T(8,128)(2,1)S(1)}, u32[]{:S(2)}, u32[]{:S(2)}) %collective-permute-start.28) | collective-permute-done | bytes 589856 | tf_op jit(solution)/shard_map/ppermute | solution.py:70
  491.7 4.3 collective-permute-done.30.left_other.slopes
  496.0 12.4 %shard_map.350 = bf16[2,2304,576]{2,1,0:T(8,128)(2,1)} custom-call(bf16[512,2304]{1,0:T(8,128)(2,1)} %copy-done, bf16[512,2304]{1,0:T(8,128)(2,1)} %collective-permute-done.30.left_other.slopes, bf16[2,512,576]{2,1,0:T(8,128)(2,1)} %get-tuple-element.117.active.right_mine, bf16[2,512,576]{2,1,0:T(8,128)(2,1)} %get-tuple-element.118.active.right_other), custom_call_target="tpu_custom_call" | custom-call | tf_op jit(solution)/shard_map/pallas_call | solution.py:350
  508.7 20.2 %shard_map.352 = (bf16[2,512,1152]{2,1,0:T(8,128)(2,1)}, bf16[512,2304]{1,0:T(8,128)(2,1)}) custom-call(bf16[512,2304]{1,0:T(8,128)(2,1)} %collective-permute-done.30.left_other.slopes, bf16[2,2304,576]{2,1,0:T(8,128)(2,1)} %bitcast.225, bf16[2,2304,1152]{2,1,0:T(8,128)(2,1)} %bitcast.221, bf16[2,512,576]{2,1,0:T(8,128)(2,1)} %get-tuple-element.124.gate_factor, ...), custom_call_target="tpu_custom_call" | custom-call | tf_op jit(solution)/shard_map/pallas_call | solution.py:322
  529.3 21.8 %shard_map.351 = (bf16[2,512,1152]{2,1,0:T(8,128)(2,1)}, f32[512,2304]{1,0:T(8,128)}) custom-call(bf16[512,2304]{1,0:T(8,128)(2,1)} %copy-done, bf16[2,2304,576]{2,1,0:T(8,128)(2,1)} %bitcast.226, bf16[2,2304,1152]{2,1,0:T(8,128)(2,1)} %bitcast.222, bf16[2,512,576]{2,1,0:T(8,128)(2,1)} %get-tuple-element.120.gate_factor, ...), custom_call_target="tpu_custom_call" | custom-call | tf_op jit(solution)/shard_map/pallas_call | solution.py:322
  551.1 17.5 %shard_map.353 = bf16[2,2304,1152]{2,1,0:T(8,128)(2,1)} custom-call(bf16[512,2304]{1,0:T(8,128)(2,1)} %copy-done.5, bf16[512,2304]{1,0:T(8,128)(2,1)} %collective-permute-done.22.rows.left_other, bf16[2,512,1152]{2,1,0:T(8,128)(2,1)} %get-tuple-element.129.right_mine, bf16[2,512,1152]{2,1,0:T(8,128)(2,1)} %get-tuple-element.130.right_other), custom_call_target="tpu_custom_call" | custom-call | tf_op jit(solution)/shard_map/pallas_call | solution.py:350
  568.6 3.6 fusion.59
  572.4 12.8 %collective-permute-start.32 = (bf16[128,2304]{1,0:T(8,128)(2,1)S(1)}, bf16[128,2304]{1,0:T(8,128)(2,1)S(1)}, u32[]{:S(2)}, u32[]{:S(2)}) collective-permute-start(bf16[128,2304]{1,0:T(8,128)(2,1)S(1)} %get-tuple-element.284), channel_id=1, source_target_pairs={{0,8},{8,16},{16,24},{24,0},{1,9},{9,17},{17,25},{25,1},{2,10},{10... | collective-permute-start | bytes 1769480 | tf_op jit(solution)/shard_map/ppermute | solution.py:70
  586.4 11.3 %collective-permute-done.32 = bf16[128,2304]{1,0:T(8,128)(2,1)S(1)} collective-permute-done((bf16[128,2304]{1,0:T(8,128)(2,1)S(1)}, bf16[128,2304]{1,0:T(8,128)(2,1)S(1)}, u32[]{:S(2)}, u32[]{:S(2)}) %collective-permute-start.32) | collective-permute-done | bytes 589856 | tf_op jit(solution)/shard_map/ppermute | solution.py:70
  597.8 12.7 %collective-permute-done.34 = bf16[128,2304]{1,0:T(8,128)(2,1)S(1)} collective-permute-done((bf16[128,2304]{1,0:T(8,128)(2,1)S(1)}, bf16[128,2304]{1,0:T(8,128)(2,1)S(1)}, u32[]{:S(2)}, u32[]{:S(2)}) %collective-permute-start.34) | collective-permute-done | bytes 589856 | tf_op jit(solution)/shard_map/ppermute | solution.py:70
  610.4 24.7 %collective-permute-done.33 = bf16[128,2304]{1,0:T(8,128)(2,1)S(1)} collective-permute-done((bf16[128,2304]{1,0:T(8,128)(2,1)S(1)}, bf16[128,2304]{1,0:T(8,128)(2,1)S(1)}, u32[]{:S(2)}, u32[]{:S(2)}) %collective-permute-start.33) | collective-permute-done | bytes 589856 | tf_op jit(solution)/shard_map/ppermute | solution.py:70
  647.2 3.6 collective-permute-start.39
  651.1 14.4 %collective-permute-done.35 = bf16[128,2304]{1,0:T(8,128)(2,1)S(1)} collective-permute-done((bf16[128,2304]{1,0:T(8,128)(2,1)S(1)}, bf16[128,2304]{1,0:T(8,128)(2,1)S(1)}, u32[]{:S(2)}, u32[]{:S(2)}) %collective-permute-start.35) | collective-permute-done | bytes 589856 | tf_op jit(solution)/shard_map/ppermute | solution.py:66
  667.1 13.6 %collective-permute-done.40 = bf16[288,576]{1,0:T(8,128)(2,1)S(1)} collective-permute-done((bf16[288,576]{1,0:T(8,128)(2,1)}, bf16[288,576]{1,0:T(8,128)(2,1)S(1)}, u32[]{:S(2)}, u32[]{:S(2)}) %collective-permute-start.40) | collective-permute-done | bytes 331808 | tf_op jit(solution)/shard_map/ppermute | solution.py:70
  683.6 12.8 %shard_map.354 = (bf16[512,1024]{1,0:T(8,128)(2,1)}, f32[256,2304]{1,0:T(8,128)}, bf16[256,2304]{1,0:T(8,128)(2,1)}) custom-call(bf16[512,2304]{1,0:T(8,128)(2,1)} %constant_dynamic-update-slice_fusion.6.slopes, bf16[2304,1536]{1,0:T(8,128)(2,1)} %bitcast.36.weights, bf16[512,512]{1,0:T(8,128)(2,1)} %get-tuple-element.133.queries, ...), custom_call_target="tpu_custom_call" | custom-call | tf_op jit(solution)/shard_map/pallas_call | solution.py:681
  699.2 4.6 convolution_convert_fusion
  718.8 6.7 collective-permute-done.38
  731.5 41.8 %collective-permute-done.43.refs_2_ = bf16[288,1152]{1,0:T(8,128)(2,1)} collective-permute-done((bf16[288,1152]{1,0:T(8,128)(2,1)}, bf16[288,1152]{1,0:T(8,128)(2,1)}, u32[]{:S(2)}, u32[]{:S(2)}) %collective-permute-start.43) | collective-permute-done | bytes 663584 | tf_op jit(solution)/shard_map/ppermute | solution.py:70
  780.2 5.1 convert_add_fusion
  798.3 4.0 collective-permute-done.46
  802.3 10.7 %collective-permute-done.49 = bf16[4,296,512]{2,1,0:T(8,128)(2,1)} collective-permute-done((bf16[4,296,512]{2,1,0:T(8,128)(2,1)}, bf16[4,296,512]{2,1,0:T(8,128)(2,1)}, u32[]{:S(2)}, u32[]{:S(2)}) %collective-permute-start.49) | collective-permute-done | bytes 1212448 | tf_op jit(solution)/shard_map/ppermute | solution.py:70
  817.3 20.9 %collective-permute-done.47 = bf16[288,1024]{1,0:T(8,128)(2,1)} collective-permute-done((bf16[288,1024]{1,0:T(8,128)(2,1)}, bf16[288,1024]{1,0:T(8,128)(2,1)}, u32[]{:S(2)}, u32[]{:S(2)}) %collective-permute-start.47) | collective-permute-done | bytes 589856 | tf_op jit(solution)/shard_map/ppermute | solution.py:70
  838.2 3.7 collective-permute-start.51
  843.6 7.4 multiply_add_fusion
  853.7 19.7 %shard_map.355 = (f32[288,2,2304]{2,1,0:T(2,128)}, f32[288,2,2304]{2,1,0:T(2,128)}, f32[288,2,2304]{2,1,0:T(2,128)}, f32[288,2,2304]{2,1,0:T(2,128)}) custom-call(s32[1]{0:T(128)} %bitcast.90.depth, bf16[288,1152]{1,0:T(8,128)(2,1)} %get-tuple-element.158.refs_0_, bf16[288,1152]{1,0:T(8,128)(2,1)} %collective-permute-done.42.refs_1_, ...), custom_call_target="tpu_custom_call" | custom-call | tf_op jit(solution)/shard_map/pallas_call | solution.py:387
  876.1 5.3 multiply_add_fusion.2
  (413 shorter events, 202.3 us)
Async XLA Ops:
  7.2 219.8 %all-gather.3.cloned.1.call-start = ((), (), s32[]{:S(2)}) async-start(), calls=%async_computation.2 | async-start | bytes 7372800 | tf_op jit(solution)/shard_map/all_gather | solution.py:546
  21.1 36.9 %collective-permute-start.3 = (bf16[296,1536]{1,0:T(8,128)(2,1)}, bf16[296,1536]{1,0:T(8,128)(2,1)}, u32[]{:S(2)}, u32[]{:S(2)}) collective-permute-start(bf16[296,1536]{1,0:T(8,128)(2,1)} %pad_maximum_fusion.3), channel_id=1, source_target_pairs={{0,4},{4,0},{1,5},{5,1},{2,6},{6,2},{3,7},{7,3},{8,12},{12,8},{9,1... | collective-permute-start | bytes 2727944 | tf_op jit(solution)/shard_map/ppermute | solution.py:70
  26.7 31.3 %collective-permute-start.2 = (bf16[128,2304]{1,0:T(8,128)(2,1)}, bf16[128,2304]{1,0:T(8,128)(2,1)}, u32[]{:S(2)}, u32[]{:S(2)}) collective-permute-start(bf16[128,2304]{1,0:T(8,128)(2,1)} %copy.154), channel_id=1, source_target_pairs={{0,2},{2,0},{1,3},{3,1},{4,6},{6,4},{5,7},{7,5},{8,10},{10,8},{9,1... | collective-permute-start | bytes 1769480 | tf_op jit(solution)/shard_map/ppermute | solution.py:66
  26.9 29.9 %collective-permute-start.5 = (bf16[288,576]{1,0:T(8,128)(2,1)}, bf16[288,576]{1,0:T(8,128)(2,1)}, u32[]{:S(2)}, u32[]{:S(2)}) collective-permute-start(bf16[288,576]{1,0:T(8,128)(2,1)} %get-tuple-element.99), channel_id=1, source_target_pairs={{0,16},{8,24},{16,0},{24,8},{1,17},{9,25},{17,1},{25,9},{2,18},{10... | collective-permute-start | bytes 995336 | tf_op jit(solution)/shard_map/ppermute | solution.py:70
  26.9 31.0 %collective-permute-start.6 = (bf16[288,576]{1,0:T(8,128)(2,1)}, bf16[288,576]{1,0:T(8,128)(2,1)S(1)}, u32[]{:S(2)}, u32[]{:S(2)}) collective-permute-start(bf16[288,576]{1,0:T(8,128)(2,1)} %get-tuple-element.100), channel_id=1, source_target_pairs={{0,8},{8,16},{16,24},{24,0},{1,9},{9,17},{17,25},{25,1},{2,10},{10... | collective-permute-start | bytes 995336 | tf_op jit(solution)/shard_map/ppermute | solution.py:70
  59.1 286.8 %all-gather.5.cloned.1.call-start = ((), (), s32[]{:S(2)}) async-start(), calls=%async_computation.3 | async-start | bytes 13271040 | tf_op jit(solution)/shard_map/all_gather | solution.py:563
  72.9 22.2 %collective-permute-start.8 = (bf16[296,1536]{1,0:T(8,128)(2,1)}, bf16[296,1536]{1,0:T(8,128)(2,1)S(1)}, u32[]{:S(2)}, u32[]{:S(2)}) collective-permute-start(bf16[296,1536]{1,0:T(8,128)(2,1)} %pad_maximum_fusion.3), channel_id=1, source_target_pairs={{0,24},{8,0},{16,8},{24,16},{1,25},{9,1},{17,9},{25,17},{2,26},{10... | collective-permute-start | bytes 2727944 | tf_op jit(solution)/shard_map/ppermute | solution.py:70
  73.0 43.1 %collective-permute-start.9 = (bf16[296,1536]{1,0:T(8,128)(2,1)}, bf16[296,1536]{1,0:T(8,128)(2,1)S(1)}, u32[]{:S(2)}, u32[]{:S(2)}) collective-permute-start(bf16[296,1536]{1,0:T(8,128)(2,1)} %pad_maximum_fusion.3), channel_id=1, source_target_pairs={{0,8},{8,16},{16,24},{24,0},{1,9},{9,17},{17,25},{25,1},{2,10},{10... | collective-permute-start | bytes 2727944 | tf_op jit(solution)/shard_map/ppermute | solution.py:70
  116.1 41.1 %collective-permute-start.11 = (bf16[296,1536]{1,0:T(8,128)(2,1)}, bf16[296,1536]{1,0:T(8,128)(2,1)S(1)}, u32[]{:S(2)}, u32[]{:S(2)}) collective-permute-start(bf16[296,1536]{1,0:T(8,128)(2,1)} %pad_maximum_fusion.3), channel_id=1, source_target_pairs={{0,16},{8,24},{16,0},{24,8},{1,17},{9,25},{17,1},{25,9},{2,18},{10... | collective-permute-start | bytes 2727944 | tf_op jit(solution)/shard_map/ppermute | solution.py:70
  116.1 41.1 %collective-permute-start.10 = (bf16[296,1536]{1,0:T(8,128)(2,1)S(1)}, bf16[296,1536]{1,0:T(8,128)(2,1)S(1)}, u32[]{:S(2)}, u32[]{:S(2)}) collective-permute-start(bf16[296,1536]{1,0:T(8,128)(2,1)S(1)} %collective-permute-done.8), channel_id=1, source_target_pairs={{0,4},{4,0},{1,5},{5,1},{2,6},{6,2},{3,7},{7,3},{8,12},{12,8},{9,1... | collective-permute-start | bytes 2727944 | tf_op jit(solution)/shard_map/ppermute | solution.py:70
  116.9 46.7 %collective-permute-start.12 = (bf16[296,1536]{1,0:T(8,128)(2,1)S(1)}, bf16[296,1536]{1,0:T(8,128)(2,1)S(1)}, u32[]{:S(2)}, u32[]{:S(2)}) collective-permute-start(bf16[296,1536]{1,0:T(8,128)(2,1)S(1)} %collective-permute-done.9), channel_id=1, source_target_pairs={{0,4},{4,0},{1,5},{5,1},{2,6},{6,2},{3,7},{7,3},{8,12},{12,8},{9,1... | collective-permute-start | bytes 2727944 | tf_op jit(solution)/shard_map/ppermute | solution.py:70
  164.5 16.9 %collective-permute-start.16 = (bf16[288,1152]{1,0:T(8,128)(2,1)}, bf16[288,1152]{1,0:T(8,128)(2,1)S(1)}, u32[]{:S(2)}, u32[]{:S(2)}) collective-permute-start(bf16[288,1152]{1,0:T(8,128)(2,1)} %get-tuple-element.111), channel_id=1, source_target_pairs={{0,24},{8,0},{16,8},{24,16},{1,25},{9,1},{17,9},{25,17},{2,26},{10... | collective-permute-start | bytes 1990664 | tf_op jit(solution)/shard_map/ppermute | solution.py:70
  169.3 54.8 %collective-permute-start.17 = (bf16[288,1152]{1,0:T(8,128)(2,1)}, bf16[288,1152]{1,0:T(8,128)(2,1)}, u32[]{:S(2)}, u32[]{:S(2)}) collective-permute-start(bf16[288,1152]{1,0:T(8,128)(2,1)} %get-tuple-element.112), channel_id=1, source_target_pairs={{0,16},{8,24},{16,0},{24,8},{1,17},{9,25},{17,1},{25,9},{2,18},{10... | collective-permute-start | bytes 1990664 | tf_op jit(solution)/shard_map/ppermute | solution.py:70
  169.3 56.7 %collective-permute-start.18 = (bf16[288,1152]{1,0:T(8,128)(2,1)S(1)}, bf16[288,1152]{1,0:T(8,128)(2,1)S(1)}, u32[]{:S(2)}, u32[]{:S(2)}) collective-permute-start(bf16[288,1152]{1,0:T(8,128)(2,1)S(1)} %get-tuple-element.113), channel_id=1, source_target_pairs={{0,8},{8,16},{16,24},{24,0},{1,9},{9,17},{17,25},{25,1},{2,10},{10... | collective-permute-start | bytes 1990664 | tf_op jit(solution)/shard_map/ppermute | solution.py:70
  169.7 57.2 %collective-permute-start.13 = (bf16[296,1536]{1,0:T(8,128)(2,1)}, bf16[296,1536]{1,0:T(8,128)(2,1)S(1)}, u32[]{:S(2)}, u32[]{:S(2)}) collective-permute-start(bf16[296,1536]{1,0:T(8,128)(2,1)} %copy-done.34), channel_id=1, source_target_pairs={{0,4},{4,0},{1,5},{5,1},{2,6},{6,2},{3,7},{7,3},{8,12},{12,8},{9,1... | collective-permute-start | bytes 2727944 | tf_op jit(solution)/shard_map/ppermute | solution.py:70
  227.0 412.3 %reduce-scatter.3.cloned.1.call-start = ((), (), s32[]{:S(2)}) async-start(), calls=%async_computation.4 | async-start | bytes 7372800 | tf_op jit(solution)/shard_map/reduce_scatter | solution.py:642
  268.8 14.6 %collective-permute-start.15 = (bf16[128,2304]{1,0:T(8,128)(2,1)S(1)}, bf16[128,2304]{1,0:T(8,128)(2,1)S(1)}, u32[]{:S(2)}, u32[]{:S(2)}) collective-permute-start(bf16[128,2304]{1,0:T(8,128)(2,1)S(1)} %slice.524), channel_id=1, source_target_pairs={{0,2},{2,0},{1,3},{3,1},{4,6},{6,4},{5,7},{7,5},{8,10},{10,8},{9,1... | collective-permute-start | bytes 1769480 | tf_op jit(solution)/shard_map/ppermute | solution.py:66
  286.8 51.5 %collective-permute-start.21 = (bf16[128,2304]{1,0:T(8,128)(2,1)S(1)}, bf16[128,2304]{1,0:T(8,128)(2,1)S(1)}, u32[]{:S(2)}, u32[]{:S(2)}) collective-permute-start(bf16[128,2304]{1,0:T(8,128)(2,1)S(1)} %multiply_convert_fusion.1), channel_id=1, source_target_pairs={{0,8},{8,16},{16,24},{24,0},{1,9},{9,17},{17,25},{25,1},{2,10},{10... | collective-permute-start | bytes 1769480 | tf_op jit(solution)/shard_map/ppermute | solution.py:70
  288.7 49.6 %collective-permute-start.20 = (bf16[128,2304]{1,0:T(8,128)(2,1)S(1)}, bf16[128,2304]{1,0:T(8,128)(2,1)S(1)}, u32[]{:S(2)}, u32[]{:S(2)}) collective-permute-start(bf16[128,2304]{1,0:T(8,128)(2,1)S(1)} %multiply_convert_fusion.1), channel_id=1, source_target_pairs={{0,16},{8,24},{16,0},{24,8},{1,17},{9,25},{17,1},{25,9},{2,18},{10... | collective-permute-start | bytes 1769480 | tf_op jit(solution)/shard_map/ppermute | solution.py:70
  388.8 16.9 %collective-permute-start.24 = (bf16[128,2304]{1,0:T(8,128)(2,1)}, bf16[128,2304]{1,0:T(8,128)(2,1)}, u32[]{:S(2)}, u32[]{:S(2)}) collective-permute-start(bf16[128,2304]{1,0:T(8,128)(2,1)} %get-tuple-element.287), channel_id=1, source_target_pairs={{0,8},{8,16},{16,24},{24,0},{1,9},{9,17},{17,25},{25,1},{2,10},{10... | collective-permute-start | bytes 1769480 | tf_op jit(solution)/shard_map/ppermute | solution.py:70
  388.8 27.7 %collective-permute-start.26 = (bf16[128,2304]{1,0:T(8,128)(2,1)}, bf16[128,2304]{1,0:T(8,128)(2,1)}, u32[]{:S(2)}, u32[]{:S(2)}) collective-permute-start(bf16[128,2304]{1,0:T(8,128)(2,1)} %get-tuple-element.288), channel_id=1, source_target_pairs={{0,24},{8,0},{16,8},{24,16},{1,25},{9,1},{17,9},{25,17},{2,26},{10... | collective-permute-start | bytes 1769480 | tf_op jit(solution)/shard_map/ppermute | solution.py:70
  392.0 50.8 %collective-permute-start.25 = (bf16[128,2304]{1,0:T(8,128)(2,1)}, bf16[128,2304]{1,0:T(8,128)(2,1)}, u32[]{:S(2)}, u32[]{:S(2)}) collective-permute-start(bf16[128,2304]{1,0:T(8,128)(2,1)} %get-tuple-element.289), channel_id=1, source_target_pairs={{0,16},{8,24},{16,0},{24,8},{1,17},{9,25},{17,1},{25,9},{2,18},{10... | collective-permute-start | bytes 1769480 | tf_op jit(solution)/shard_map/ppermute | solution.py:70
  447.2 15.8 %collective-permute-start.29 = (bf16[128,2304]{1,0:T(8,128)(2,1)S(1)}, bf16[128,2304]{1,0:T(8,128)(2,1)S(1)}, u32[]{:S(2)}, u32[]{:S(2)}) collective-permute-start(bf16[128,2304]{1,0:T(8,128)(2,1)S(1)} %get-tuple-element.300), channel_id=1, source_target_pairs={{0,8},{8,16},{16,24},{24,0},{1,9},{9,17},{17,25},{25,1},{2,10},{10... | collective-permute-start | bytes 1769480 | tf_op jit(solution)/shard_map/ppermute | solution.py:70
  447.2 40.5 %collective-permute-start.28 = (bf16[128,2304]{1,0:T(8,128)(2,1)S(1)}, bf16[128,2304]{1,0:T(8,128)(2,1)S(1)}, u32[]{:S(2)}, u32[]{:S(2)}) collective-permute-start(bf16[128,2304]{1,0:T(8,128)(2,1)S(1)} %get-tuple-element.300), channel_id=1, source_target_pairs={{0,16},{8,24},{16,0},{24,8},{1,17},{9,25},{17,1},{25,9},{2,18},{10... | collective-permute-start | bytes 1769480 | tf_op jit(solution)/shard_map/ppermute | solution.py:70
  447.2 40.5 %collective-permute-start.27 = (bf16[128,2304]{1,0:T(8,128)(2,1)S(1)}, bf16[128,2304]{1,0:T(8,128)(2,1)S(1)}, u32[]{:S(2)}, u32[]{:S(2)}) collective-permute-start(bf16[128,2304]{1,0:T(8,128)(2,1)S(1)} %get-tuple-element.300), channel_id=1, source_target_pairs={{0,24},{8,0},{16,8},{24,16},{1,25},{9,1},{17,9},{25,17},{2,26},{10... | collective-permute-start | bytes 1769480 | tf_op jit(solution)/shard_map/ppermute | solution.py:70
  508.4 198.0 %reduce-scatter.5.cloned.1.call-start = ((), (), s32[]{:S(2)}) async-start(), calls=%async_computation.5 | async-start | bytes 13271040 | tf_op jit(solution)/shard_map/reduce_scatter | solution.py:642
  528.9 22.2 %collective-permute-start.31 = (bf16[512,2304]{1,0:T(8,128)(2,1)}, bf16[512,2304]{1,0:T(8,128)(2,1)}, u32[]{:S(2)}, u32[]{:S(2)}) collective-permute-start(bf16[512,2304]{1,0:T(8,128)(2,1)} %get-tuple-element.126), channel_id=1, source_target_pairs={{0,1},{1,0},{2,3},{3,2},{4,5},{5,4},{6,7},{7,6},{8,9},{9,8},{10,11... | collective-permute-start | bytes 7077896 | tf_op jit(solution)/shard_map/ppermute | solution.py:66
  572.4 25.4 %collective-permute-start.32 = (bf16[128,2304]{1,0:T(8,128)(2,1)S(1)}, bf16[128,2304]{1,0:T(8,128)(2,1)S(1)}, u32[]{:S(2)}, u32[]{:S(2)}) collective-permute-start(bf16[128,2304]{1,0:T(8,128)(2,1)S(1)} %get-tuple-element.284), channel_id=1, source_target_pairs={{0,8},{8,16},{16,24},{24,0},{1,9},{9,17},{17,25},{25,1},{2,10},{10... | collective-permute-start | bytes 1769480 | tf_op jit(solution)/shard_map/ppermute | solution.py:70
  585.2 25.3 %collective-permute-start.34 = (bf16[128,2304]{1,0:T(8,128)(2,1)S(1)}, bf16[128,2304]{1,0:T(8,128)(2,1)S(1)}, u32[]{:S(2)}, u32[]{:S(2)}) collective-permute-start(bf16[128,2304]{1,0:T(8,128)(2,1)S(1)} %get-tuple-element.285), channel_id=1, source_target_pairs={{0,24},{8,0},{16,8},{24,16},{1,25},{9,1},{17,9},{25,17},{2,26},{10... | collective-permute-start | bytes 1769480 | tf_op jit(solution)/shard_map/ppermute | solution.py:70
  585.2 50.0 %collective-permute-start.33 = (bf16[128,2304]{1,0:T(8,128)(2,1)S(1)}, bf16[128,2304]{1,0:T(8,128)(2,1)S(1)}, u32[]{:S(2)}, u32[]{:S(2)}) collective-permute-start(bf16[128,2304]{1,0:T(8,128)(2,1)S(1)} %get-tuple-element.286), channel_id=1, source_target_pairs={{0,16},{8,24},{16,0},{24,8},{1,17},{9,25},{17,1},{25,9},{2,18},{10... | collective-permute-start | bytes 1769480 | tf_op jit(solution)/shard_map/ppermute | solution.py:70
  642.0 23.5 %collective-permute-start.35 = (bf16[128,2304]{1,0:T(8,128)(2,1)S(1)}, bf16[128,2304]{1,0:T(8,128)(2,1)S(1)}, u32[]{:S(2)}, u32[]{:S(2)}) collective-permute-start(bf16[128,2304]{1,0:T(8,128)(2,1)S(1)} %subtract_multiply_fusion), channel_id=1, source_target_pairs={{0,2},{2,0},{1,3},{3,1},{4,6},{6,4},{5,7},{7,5},{8,10},{10,8},{9,1... | collective-permute-start | bytes 1769480 | tf_op jit(solution)/shard_map/ppermute | solution.py:66
  647.2 20.0 %collective-permute-start.39 = (bf16[288,576]{1,0:T(8,128)(2,1)}, bf16[288,576]{1,0:T(8,128)(2,1)S(1)}, u32[]{:S(2)}, u32[]{:S(2)}) collective-permute-start(bf16[288,576]{1,0:T(8,128)(2,1)} %get-tuple-element.141), channel_id=1, source_target_pairs={{0,24},{8,0},{16,8},{24,16},{1,25},{9,1},{17,9},{25,17},{2,26},{10... | collective-permute-start | bytes 995336 | tf_op jit(solution)/shard_map/ppermute | solution.py:70
  650.8 29.9 %collective-permute-start.40 = (bf16[288,576]{1,0:T(8,128)(2,1)}, bf16[288,576]{1,0:T(8,128)(2,1)S(1)}, u32[]{:S(2)}, u32[]{:S(2)}) collective-permute-start(bf16[288,576]{1,0:T(8,128)(2,1)} %get-tuple-element.142), channel_id=1, source_target_pairs={{0,16},{8,24},{16,0},{24,8},{1,17},{9,25},{17,1},{25,9},{2,18},{10... | collective-permute-start | bytes 995336 | tf_op jit(solution)/shard_map/ppermute | solution.py:70
  650.8 29.9 %collective-permute-start.41 = (bf16[288,576]{1,0:T(8,128)(2,1)S(1)}, bf16[288,576]{1,0:T(8,128)(2,1)S(1)}, u32[]{:S(2)}, u32[]{:S(2)}) collective-permute-start(bf16[288,576]{1,0:T(8,128)(2,1)S(1)} %get-tuple-element.143), channel_id=1, source_target_pairs={{0,8},{8,16},{16,24},{24,0},{1,9},{9,17},{17,25},{25,1},{2,10},{10... | collective-permute-start | bytes 995336 | tf_op jit(solution)/shard_map/ppermute | solution.py:70
  665.6 16.9 %collective-permute-start.36 = (bf16[256,2304]{1,0:T(8,128)(2,1)S(1)}, bf16[256,2304]{1,0:T(8,128)(2,1)S(1)}, u32[]{:S(2)}, u32[]{:S(2)}) collective-permute-start(bf16[256,2304]{1,0:T(8,128)(2,1)S(1)} %pad_maximum_fusion.2), channel_id=1, source_target_pairs={{0,1},{1,0},{2,3},{3,2},{4,5},{5,4},{6,7},{7,6},{8,9},{9,8},{10,11... | collective-permute-start | bytes 3538952 | tf_op jit(solution)/shard_map/ppermute | solution.py:66
  696.4 14.1 %collective-permute-start.37 = (bf16[256,2304]{1,0:T(8,128)(2,1)}, bf16[256,2304]{1,0:T(8,128)(2,1)S(1)}, u32[]{:S(2)}, u32[]{:S(2)}) collective-permute-start(bf16[256,2304]{1,0:T(8,128)(2,1)} %get-tuple-element.138), channel_id=1, source_target_pairs={{0,1},{1,0},{2,3},{3,2},{4,5},{5,4},{6,7},{7,6},{8,9},{9,8},{10,11... | collective-permute-start | bytes 3538952 | tf_op jit(solution)/shard_map/ppermute | solution.py:66
  709.9 69.4 %collective-permute-start.45 = (bf16[4,288,1024]{2,1,0:T(8,128)(2,1)}, bf16[4,288,1024]{2,1,0:T(8,128)(2,1)}, u32[]{:S(2)}, u32[]{:S(2)}) collective-permute-start(bf16[4,288,1024]{2,1,0:T(8,128)(2,1)} %get-tuple-element.148), channel_id=1, source_target_pairs={{0,4},{4,0},{1,5},{5,1},{2,6},{6,2},{3,7},{7,3},{8,12},{12,8},{9,1... | collective-permute-start | bytes 7077896 | tf_op jit(solution)/shard_map/ppermute | solution.py:70
  710.9 14.6 %collective-permute-start.38 = (bf16[128,2304]{1,0:T(8,128)(2,1)S(1)}, bf16[128,2304]{1,0:T(8,128)(2,1)S(1)}, u32[]{:S(2)}, u32[]{:S(2)}) collective-permute-start(bf16[128,2304]{1,0:T(8,128)(2,1)S(1)} %slice.523), channel_id=1, source_target_pairs={{0,2},{2,0},{1,3},{3,1},{4,6},{6,4},{5,7},{7,5},{8,10},{10,8},{9,1... | collective-permute-start | bytes 1769480 | tf_op jit(solution)/shard_map/ppermute | solution.py:66
  712.1 19.3 %collective-permute-start.42 = (bf16[288,1152]{1,0:T(8,128)(2,1)}, bf16[288,1152]{1,0:T(8,128)(2,1)}, u32[]{:S(2)}, u32[]{:S(2)}) collective-permute-start(bf16[288,1152]{1,0:T(8,128)(2,1)} %get-tuple-element.144), channel_id=1, source_target_pairs={{0,24},{8,0},{16,8},{24,16},{1,25},{9,1},{17,9},{25,17},{2,26},{10... | collective-permute-start | bytes 1990664 | tf_op jit(solution)/shard_map/ppermute | solution.py:70
  712.2 61.1 %collective-permute-start.43 = (bf16[288,1152]{1,0:T(8,128)(2,1)}, bf16[288,1152]{1,0:T(8,128)(2,1)}, u32[]{:S(2)}, u32[]{:S(2)}) collective-permute-start(bf16[288,1152]{1,0:T(8,128)(2,1)} %get-tuple-element.145), channel_id=1, source_target_pairs={{0,16},{8,24},{16,0},{24,8},{1,17},{9,25},{17,1},{25,9},{2,18},{10... | collective-permute-start | bytes 1990664 | tf_op jit(solution)/shard_map/ppermute | solution.py:70
  715.3 58.0 %collective-permute-start.44 = (bf16[288,1152]{1,0:T(8,128)(2,1)}, bf16[288,1152]{1,0:T(8,128)(2,1)}, u32[]{:S(2)}, u32[]{:S(2)}) collective-permute-start(bf16[288,1152]{1,0:T(8,128)(2,1)} %get-tuple-element.146), channel_id=1, source_target_pairs={{0,8},{8,16},{16,24},{24,0},{1,9},{9,17},{17,25},{25,1},{2,10},{10... | collective-permute-start | bytes 1990664 | tf_op jit(solution)/shard_map/ppermute | solution.py:70
  785.3 27.7 %collective-permute-start.49 = (bf16[4,296,512]{2,1,0:T(8,128)(2,1)}, bf16[4,296,512]{2,1,0:T(8,128)(2,1)}, u32[]{:S(2)}, u32[]{:S(2)}) collective-permute-start(bf16[4,296,512]{2,1,0:T(8,128)(2,1)} %dynamic-slice_bitcast_fusion.2), channel_id=1, source_target_pairs={{0,4},{4,0},{1,5},{5,1},{2,6},{6,2},{3,7},{7,3},{8,12},{12,8},{9,1... | collective-permute-start | bytes 3637256 | tf_op jit(solution)/shard_map/ppermute | solution.py:70
  787.5 14.8 %collective-permute-start.46 = (bf16[288,1024]{1,0:T(8,128)(2,1)}, bf16[288,1024]{1,0:T(8,128)(2,1)}, u32[]{:S(2)}, u32[]{:S(2)}) collective-permute-start(bf16[288,1024]{1,0:T(8,128)(2,1)} %get-tuple-element.149), channel_id=1, source_target_pairs={{0,24},{8,0},{16,8},{24,16},{1,25},{9,1},{17,9},{25,17},{2,26},{10... | collective-permute-start | bytes 1769480 | tf_op jit(solution)/shard_map/ppermute | solution.py:70
  787.5 50.7 %collective-permute-start.47 = (bf16[288,1024]{1,0:T(8,128)(2,1)}, bf16[288,1024]{1,0:T(8,128)(2,1)}, u32[]{:S(2)}, u32[]{:S(2)}) collective-permute-start(bf16[288,1024]{1,0:T(8,128)(2,1)} %get-tuple-element.150), channel_id=1, source_target_pairs={{0,16},{8,24},{16,0},{24,8},{1,17},{9,25},{17,1},{25,9},{2,18},{10... | collective-permute-start | bytes 1769480 | tf_op jit(solution)/shard_map/ppermute | solution.py:70
  787.5 50.7 %collective-permute-start.48 = (bf16[288,1024]{1,0:T(8,128)(2,1)}, bf16[288,1024]{1,0:T(8,128)(2,1)}, u32[]{:S(2)}, u32[]{:S(2)}) collective-permute-start(bf16[288,1024]{1,0:T(8,128)(2,1)} %get-tuple-element.151), channel_id=1, source_target_pairs={{0,8},{8,16},{16,24},{24,0},{1,9},{9,17},{17,25},{25,1},{2,10},{10... | collective-permute-start | bytes 1769480 | tf_op jit(solution)/shard_map/ppermute | solution.py:70
  838.2 35.2 %collective-permute-start.50 = (bf16[296,512]{1,0:T(8,128)(2,1)}, bf16[296,512]{1,0:T(8,128)(2,1)S(1)}, u32[]{:S(2)}, u32[]{:S(2)}) collective-permute-start(bf16[296,512]{1,0:T(8,128)(2,1)} %get-tuple-element.155), channel_id=1, source_target_pairs={{0,24},{8,0},{16,8},{24,16},{1,25},{9,1},{17,9},{25,17},{2,26},{10... | collective-permute-start | bytes 909320 | tf_op jit(solution)/shard_map/ppermute | solution.py:70
  838.2 35.2 %collective-permute-start.51 = (bf16[296,512]{1,0:T(8,128)(2,1)}, bf16[296,512]{1,0:T(8,128)(2,1)S(1)}, u32[]{:S(2)}, u32[]{:S(2)}) collective-permute-start(bf16[296,512]{1,0:T(8,128)(2,1)} %get-tuple-element.156), channel_id=1, source_target_pairs={{0,16},{8,24},{16,0},{24,8},{1,17},{9,25},{17,1},{25,9},{2,18},{10... | collective-permute-start | bytes 909320 | tf_op jit(solution)/shard_map/ppermute | solution.py:70
  841.9 31.5 %collective-permute-start.52 = (bf16[296,512]{1,0:T(8,128)(2,1)}, bf16[296,512]{1,0:T(8,128)(2,1)S(1)}, u32[]{:S(2)}, u32[]{:S(2)}) collective-permute-start(bf16[296,512]{1,0:T(8,128)(2,1)} %get-tuple-element.157), channel_id=1, source_target_pairs={{0,8},{8,16},{16,24},{24,0},{1,9},{9,17},{17,25},{25,1},{2,10},{10... | collective-permute-start | bytes 909320 | tf_op jit(solution)/shard_map/ppermute | solution.py:70
  (75 other events, 801.9 us)
Sparse Core Ops, SparseCore 0:
  59.2 71.3 all-gather.2
  227.1 114.9 all-gather.4
  508.6 75.7 reduce-scatter.2
  587.4 115.0 reduce-scatter.4

commit v4 on v3

--- a/solution.py
+++ b/solution.py
@@ -286,35 +286,39 @@
     )(active, weights, *received)
 
 
-def feed_back_kernel(main, slopes, down, gate_up, gate_factor, up_factor, slope_out, out, total):
+def feed_back_kernel(main, *refs):
+    slopes, (down, gate_up), factors = refs[:2], refs[2:4], refs[4:8]
+    slope_outs, mine_out, other_out, total = refs[8:10], refs[10], refs[11], refs[12]
     step = pl.program_id(0)
-    active_slope = dot(slopes[...], down[0])
-    quarter = active_slope.shape[1]
-    gate_slope = (active_slope * gate_factor[0].astype(F32)).astype(BF16)
-    up_slope = (active_slope * up_factor[0].astype(F32)).astype(BF16)
-    slope_out[0] = jnp.concatenate(
-        [gate_slope[:, :main], up_slope[:, :main], gate_slope[:, main:], up_slope[:, main:]], axis=1
-    )
-    product = times_transposed(slope_out[0], gate_up[0])
-
-    @pl.when(step == 0)
-    def _():
-        total[...] = product
-
-    @pl.when(step > 0)
-    def _():
-        total[...] += product
+    for place, sums in ((1, total), (0, mine_out)):
+        active_slope = dot(slopes[place][...], down[0])
+        gate_slope = (active_slope * factors[place][0].astype(F32)).astype(BF16)
+        up_slope = (active_slope * factors[2 + place][0].astype(F32)).astype(BF16)
+        slope_outs[place][0] = jnp.concatenate(
+            [gate_slope[:, :main], up_slope[:, :main], gate_slope[:, main:], up_slope[:, main:]],
+            axis=1,
+        )
+        product = times_transposed(slope_outs[place][0], gate_up[0])
+
+        @pl.when(step == 0)
+        def _():
+            sums[...] = product
+
+        @pl.when(step > 0)
+        def _():
+            sums[...] += product
 
     @pl.when(step == pl.num_programs(0) - 1)
     def _():
-        out[...] = total[...].astype(out.dtype)
-
-
-def feed_back_call(slopes, down, gate_up, gate_factor, up_factor, main, out_type):
-    height, width = slopes.shape
+        other_out[...] = total[...].astype(BF16)
+
+
+def feed_back_call(slopes, down, gate_up, gate_factors, up_factors, main):
+    height, width = slopes[0].shape
     count, _, columns = gate_up.shape
     quarter = columns // 2
     whole_block = pl.BlockSpec((height, width), lambda i: (0, 0))
+    once = pl.BlockSpec((height, width), lambda i: (0, 0), pipeline_mode=pl.Buffered(1))
 
     def each(rows, wide):
         return pl.BlockSpec((1, rows, wide), lambda i: (i, 0, 0))
@@ -322,18 +326,15 @@
     return pl.pallas_call(
         functools.partial(feed_back_kernel, main),
         grid=(count,),
-        in_specs=[
-            whole_block,
-            each(width, quarter),
-            each(width, columns),
-            each(height, quarter),
-            each(height, quarter),
-        ],
-        out_specs=[each(height, columns), whole_block],
-        out_shape=[shape((count, height, columns)), shape((height, width), out_type)],
+        in_specs=[once] * 2
+        + [each(width, quarter), each(width, columns)]
+        + [each(height, quarter)] * 4,
+        out_specs=[each(height, columns)] * 2 + [whole_block] * 2,
+        out_shape=[shape((count, height, columns))] * 2
+        + [shape((height, width), F32), shape((height, width))],
         scratch_shapes=[pltpu.VMEM((height, width), F32)],
         compiler_params=params,
-    )(slopes, down, gate_up, gate_factor, up_factor)
+    )(*slopes, down, gate_up, *gate_factors, *up_factors)
 
 
 def weight_slope_kernel(left_mine, left_other, right_mine, right_other, out):
@@ -643,26 +644,17 @@
 
         down_total = ffn_total(feed_slope_rows, activated)
         later_rows = gated(feed_slope_rows, down_total)
-        backs = [
-            feed_back_call(
-                later_rows[place],
-                full_down,
-                full_gate_up,
-                gate_factor[place],
-                up_factor[place],
-                main,
-                (F32, BF16)[place],
-            )
-            for place in range(2)
-        ]
-        received = swap(backs[1][1], "c")
-        normed_two_slope = scatter_group(backs[0][1] + received.astype(F32))
+        slope_mine, slope_other, mine, other = feed_back_call(
+            later_rows, full_down, full_gate_up, gate_factor, up_factor, main
+        )
+        received = swap(other, "c")
+        normed_two_slope = scatter_group(mine + received.astype(F32))
 
         def owned(pieces):
             return rolled(jnp.stack(pieces), (DEPTH - depth) % DEPTH, 0)
 
         down_pieces = quarter_pieces(reduce_ffn(down_total).reshape(DEPTH, block, quarter))
-        gate_up_total = ffn_total(rows_two, gated([back[0] for back in backs], received))
+        gate_up_total = ffn_total(rows_two, gated([slope_mine, slope_other], received))
         gate_up_mine = reduce_ffn(gate_up_total)
 
         hidden_part, gain_three = norm_backward(

time: 902 us -> 900 us (level)
    pallas_call x2 -> x1, Pallas kernels: 42 us -> 35.1 us  [feed_back_call(): pl.pallas_call(functools.partial(feed_back_kernel, main), grid=(count,),...]
  transfers between devices with their start and end apart: 59 -> 59, of which waited for: 30 -> 31; matrix products, arithmetic and copies ran while one was open for 16% -> 16% of each run, Pallas kernels for 13% -> 12%
where the time goes in v4:
time: 900 us; the launch traced here: 890 us
  waiting for transfers between devices  479 us (53%)
  Pallas kernels  147 us (16%)
  local copies, waits for them, and re-layouts  101 us (11%)
  starting transfers between devices  72.6 us (8%)
  other arithmetic  67.1 us (7%)
  between operations  15.1 us (2%)
    ppermute x39, waiting for transfers between devices, from_ahead(): lax.ppermute(value, axis, [(j, (j - step) % size) for j in range(size)])  427 us
    ppermute x39, starting transfers between devices, from_ahead(): lax.ppermute(value, axis, [(j, (j - step) % size) for j in range(size)])  51.9 us
    ppermute x16, waiting for transfers between devices, swap(): return lax.ppermute(value, axis, [(0, 1), (1, 0)])  51.7 us
    pallas_call x1, Pallas kernels, feed_back_call(): pl.pallas_call(functools.partial(feed_back_kernel, main), grid=(count,),...  35.1 us
    pallas_call x2, Pallas kernels, weight_slope_call(): pl.pallas_call(weight_slope_kernel, grid=(count, 3), in_specs=[left_block...  29.7 us
    unnamed x142, local copies, waits for them, and re-layouts  26.1 us
    pallas_call x2, Pallas kernels, gate_up_call(): pl.pallas_call(functools.partial(gate_up_kernel, main), grid=(count,), in...  22.8 us
    ppermute x16, starting transfers between devices, swap(): return lax.ppermute(value, axis, [(0, 1), (1, 0)])  20.3 us
  transfers between devices with their start and end apart: 59, of which 31 were waited for; matrix products, arithmetic and copies ran while one was open for 16% of the time, Pallas kernels for 12%

profile of v4, /device:TPU:1, one launch (start us, length us, event | category | flops | bytes accessed | tf_op | source)
XLA Modules:
  0.0 889.9 jit_solution(10758137365961797859)
XLA Ops:
  22.3 3.3 collective-permute-start.4
  27.6 5.8 collective-permute-done.4
  34.4 22.5 %collective-permute-done.5 = bf16[288,576]{1,0:T(8,128)(2,1)} collective-permute-done((bf16[288,576]{1,0:T(8,128)(2,1)}, bf16[288,576]{1,0:T(8,128)(2,1)}, u32[]{:S(2)}, u32[]{:S(2)}) %collective-permute-start.5) | collective-permute-done | bytes 331808 | tf_op jit(solution)/shard_map/ppermute | solution.py:70
  69.1 3.7 concatenate.83
  77.3 17.8 %collective-permute-done.8 = bf16[296,1536]{1,0:T(8,128)(2,1)S(1)} collective-permute-done((bf16[296,1536]{1,0:T(8,128)(2,1)}, bf16[296,1536]{1,0:T(8,128)(2,1)S(1)}, u32[]{:S(2)}, u32[]{:S(2)}) %collective-permute-start.8) | collective-permute-done | bytes 909344 | tf_op jit(solution)/shard_map/ppermute | solution.py:70
  95.1 21.0 %collective-permute-done.9 = bf16[296,1536]{1,0:T(8,128)(2,1)S(1)} collective-permute-done((bf16[296,1536]{1,0:T(8,128)(2,1)}, bf16[296,1536]{1,0:T(8,128)(2,1)S(1)}, u32[]{:S(2)}, u32[]{:S(2)}) %collective-permute-start.9) | collective-permute-done | bytes 909344 | tf_op jit(solution)/shard_map/ppermute | solution.py:70
  121.7 35.6 %collective-permute-done.11 = bf16[296,1536]{1,0:T(8,128)(2,1)S(1)} collective-permute-done((bf16[296,1536]{1,0:T(8,128)(2,1)}, bf16[296,1536]{1,0:T(8,128)(2,1)S(1)}, u32[]{:S(2)}, u32[]{:S(2)}) %collective-permute-start.11) | collective-permute-done | bytes 909344 | tf_op jit(solution)/shard_map/ppermute | solution.py:70
  157.3 6.3 collective-permute-done.12
  171.0 10.4 %collective-permute-done.16 = bf16[288,1152]{1,0:T(8,128)(2,1)S(1)} collective-permute-done((bf16[288,1152]{1,0:T(8,128)(2,1)}, bf16[288,1152]{1,0:T(8,128)(2,1)S(1)}, u32[]{:S(2)}, u32[]{:S(2)}) %collective-permute-start.16) | collective-permute-done | bytes 663584 | tf_op jit(solution)/shard_map/ppermute | solution.py:70
  182.3 41.8 %collective-permute-done.17 = bf16[288,1152]{1,0:T(8,128)(2,1)} collective-permute-done((bf16[288,1152]{1,0:T(8,128)(2,1)}, bf16[288,1152]{1,0:T(8,128)(2,1)}, u32[]{:S(2)}, u32[]{:S(2)}) %collective-permute-start.17) | collective-permute-done | bytes 663584 | tf_op jit(solution)/shard_map/ppermute | solution.py:70
  227.9 3.4 broadcast_in_dim.49
  251.4 11.2 %shard_map.345 = (bf16[512,2304]{1,0:T(8,128)(2,1)}, bf16[512,512]{1,0:T(8,128)(2,1)}, bf16[512,256]{1,0:T(8,128)(2,1)}, bf16[512,256]{1,0:T(8,128)(2,1)}, f32[2...) custom-call(bf16[512,2304]{1,0:T(8,128)(2,1)} %copy-done.22, ...), custom_call_target="tpu_custom_call" | custom-call | tf_op jit(solution)/shard_map/pallas_call | solution.py:606
  271.6 11.8 %collective-permute-done.15 = bf16[128,2304]{1,0:T(8,128)(2,1)S(1)} collective-permute-done((bf16[128,2304]{1,0:T(8,128)(2,1)S(1)}, bf16[128,2304]{1,0:T(8,128)(2,1)S(1)}, u32[]{:S(2)}, u32[]{:S(2)}) %collective-permute-start.15) | collective-permute-done | bytes 589856 | tf_op jit(solution)/shard_map/ppermute | solution.py:66
  289.8 10.8 %collective-permute-done.19 = bf16[128,2304]{1,0:T(8,128)(2,1)S(1)} collective-permute-done((bf16[128,2304]{1,0:T(8,128)(2,1)S(1)}, bf16[128,2304]{1,0:T(8,128)(2,1)S(1)}, u32[]{:S(2)}, u32[]{:S(2)}) %collective-permute-start.19) | collective-permute-done | bytes 589856 | tf_op jit(solution)/shard_map/ppermute | solution.py:70
  300.7 37.6 %collective-permute-done.20 = bf16[128,2304]{1,0:T(8,128)(2,1)S(1)} collective-permute-done((bf16[128,2304]{1,0:T(8,128)(2,1)S(1)}, bf16[128,2304]{1,0:T(8,128)(2,1)S(1)}, u32[]{:S(2)}, u32[]{:S(2)}) %collective-permute-start.20) | collective-permute-done | bytes 589856 | tf_op jit(solution)/shard_map/ppermute | solution.py:70
  341.6 4.3 collective-permute-done.22.rows.left_other
  345.9 11.4 %shard_map.347 = (bf16[2,512,576]{2,1,0:T(8,128)(2,1)}, bf16[2,512,576]{2,1,0:T(8,128)(2,1)}, bf16[2,512,576]{2,1,0:T(8,128)(2,1)}) custom-call(bf16[512,2304]{1,0:T(8,128)(2,1)} %collective-permute-done.22.rows.left_other, bf16[2,2304,1152]{2,1,0:T(8,128)(2,1)} %bitcast.219), custom_call_target="tpu_custom_call" | custom-call | tf_op jit(solution)/shard_map/pallas_call | solution.py:247
  357.3 7.4 shard_map.348
  365.1 11.4 %shard_map.346 = (bf16[2,512,576]{2,1,0:T(8,128)(2,1)}, bf16[2,512,576]{2,1,0:T(8,128)(2,1)}, bf16[2,512,576]{2,1,0:T(8,128)(2,1)}) custom-call(bf16[512,2304]{1,0:T(8,128)(2,1)} %copy-done.5, bf16[2,2304,1152]{2,1,0:T(8,128)(2,1)} %bitcast.220), custom_call_target="tpu_custom_call" | custom-call | tf_op jit(solution)/shard_map/pallas_call | solution.py:247
  376.5 8.4 shard_map.349
  400.4 5.3 collective-permute-done.24
  405.7 10.8 %collective-permute-done.26 = bf16[128,2304]{1,0:T(8,128)(2,1)} collective-permute-done((bf16[128,2304]{1,0:T(8,128)(2,1)}, bf16[128,2304]{1,0:T(8,128)(2,1)}, u32[]{:S(2)}, u32[]{:S(2)}) %collective-permute-start.26) | collective-permute-done | bytes 589856 | tf_op jit(solution)/shard_map/ppermute | solution.py:70
  416.5 26.3 %collective-permute-done.25 = bf16[128,2304]{1,0:T(8,128)(2,1)} collective-permute-done((bf16[128,2304]{1,0:T(8,128)(2,1)}, bf16[128,2304]{1,0:T(8,128)(2,1)}, u32[]{:S(2)}, u32[]{:S(2)}) %collective-permute-start.25) | collective-permute-done | bytes 589856 | tf_op jit(solution)/shard_map/ppermute | solution.py:70
  450.4 12.5 %collective-permute-done.29 = bf16[128,2304]{1,0:T(8,128)(2,1)S(1)} collective-permute-done((bf16[128,2304]{1,0:T(8,128)(2,1)S(1)}, bf16[128,2304]{1,0:T(8,128)(2,1)S(1)}, u32[]{:S(2)}, u32[]{:S(2)}) %collective-permute-start.29) | collective-permute-done | bytes 589856 | tf_op jit(solution)/shard_map/ppermute | solution.py:70
  463.0 24.7 %collective-permute-done.28 = bf16[128,2304]{1,0:T(8,128)(2,1)S(1)} collective-permute-done((bf16[128,2304]{1,0:T(8,128)(2,1)S(1)}, bf16[128,2304]{1,0:T(8,128)(2,1)S(1)}, u32[]{:S(2)}, u32[]{:S(2)}) %collective-permute-start.28) | collective-permute-done | bytes 589856 | tf_op jit(solution)/shard_map/ppermute | solution.py:70
  491.8 4.3 collective-permute-done.30.left_other.refs_1_
  496.0 12.4 %shard_map.350 = bf16[2,2304,576]{2,1,0:T(8,128)(2,1)} custom-call(bf16[512,2304]{1,0:T(8,128)(2,1)} %copy-done, bf16[512,2304]{1,0:T(8,128)(2,1)} %collective-permute-done.30.left_other.refs_1_, bf16[2,512,576]{2,1,0:T(8,128)(2,1)} %get-tuple-element.117.active.right_mine, bf16[2,512,576]{2,1,0:T(8,128)(2,1)} %get-tuple-element.118.active.right_other), custom_call_target="tpu_custom_call" | custom-call | tf_op jit(solution)/shard_map/pallas_call | solution.py:351
  508.7 35.1 %shard_map.351 = (bf16[2,512,1152]{2,1,0:T(8,128)(2,1)}, bf16[2,512,1152]{2,1,0:T(8,128)(2,1)}, f32[512,2304]{1,0:T(8,128)}, bf16[512,2304]{1,0:T(8,128)(2,1)}) custom-call(bf16[512,2304]{1,0:T(8,128)(2,1)} %copy-done, bf16[512,2304]{1,0:T(8,128)(2,1)} %collective-permute-done.30.left_other.refs_1_, bf16[2,2304,576]{2,1,0:T(8,128)(2,1)} %bitcast.224, ...), custom_call_target="tpu_custom_call" | custom-call | tf_op jit(solution)/shard_map/pallas_call | solution.py:326
  544.2 4.5 collective-permute-done.31
  548.7 17.4 %shard_map.352 = bf16[2,2304,1152]{2,1,0:T(8,128)(2,1)} custom-call(bf16[512,2304]{1,0:T(8,128)(2,1)} %copy-done.5, bf16[512,2304]{1,0:T(8,128)(2,1)} %collective-permute-done.22.rows.left_other, bf16[2,512,1152]{2,1,0:T(8,128)(2,1)} %get-tuple-element.129.right_mine, bf16[2,512,1152]{2,1,0:T(8,128)(2,1)} %get-tuple-element.130.right_other), custom_call_target="tpu_custom_call" | custom-call | tf_op jit(solution)/shard_map/pallas_call | solution.py:351
  566.1 3.6 fusion.59
  569.9 13.0 %collective-permute-start.32 = (bf16[128,2304]{1,0:T(8,128)(2,1)S(1)}, bf16[128,2304]{1,0:T(8,128)(2,1)S(1)}, u32[]{:S(2)}, u32[]{:S(2)}) collective-permute-start(bf16[128,2304]{1,0:T(8,128)(2,1)S(1)} %get-tuple-element.284), channel_id=1, source_target_pairs={{0,8},{8,16},{16,24},{24,0},{1,9},{9,17},{17,25},{25,1},{2,10},{10... | collective-permute-start | bytes 1769480 | tf_op jit(solution)/shard_map/ppermute | solution.py:70
  584.4 11.0 %collective-permute-done.32 = bf16[128,2304]{1,0:T(8,128)(2,1)S(1)} collective-permute-done((bf16[128,2304]{1,0:T(8,128)(2,1)S(1)}, bf16[128,2304]{1,0:T(8,128)(2,1)S(1)}, u32[]{:S(2)}, u32[]{:S(2)}) %collective-permute-start.32) | collective-permute-done | bytes 589856 | tf_op jit(solution)/shard_map/ppermute | solution.py:70
  595.4 12.7 %collective-permute-done.34 = bf16[128,2304]{1,0:T(8,128)(2,1)S(1)} collective-permute-done((bf16[128,2304]{1,0:T(8,128)(2,1)S(1)}, bf16[128,2304]{1,0:T(8,128)(2,1)S(1)}, u32[]{:S(2)}, u32[]{:S(2)}) %collective-permute-start.34) | collective-permute-done | bytes 589856 | tf_op jit(solution)/shard_map/ppermute | solution.py:70
  608.0 25.2 %collective-permute-done.33 = bf16[128,2304]{1,0:T(8,128)(2,1)S(1)} collective-permute-done((bf16[128,2304]{1,0:T(8,128)(2,1)S(1)}, bf16[128,2304]{1,0:T(8,128)(2,1)S(1)}, u32[]{:S(2)}, u32[]{:S(2)}) %collective-permute-start.33) | collective-permute-done | bytes 589856 | tf_op jit(solution)/shard_map/ppermute | solution.py:70
  648.5 16.8 %collective-permute-done.35 = bf16[128,2304]{1,0:T(8,128)(2,1)S(1)} collective-permute-done((bf16[128,2304]{1,0:T(8,128)(2,1)S(1)}, bf16[128,2304]{1,0:T(8,128)(2,1)S(1)}, u32[]{:S(2)}, u32[]{:S(2)}) %collective-permute-start.35) | collective-permute-done | bytes 589856 | tf_op jit(solution)/shard_map/ppermute | solution.py:66
  667.1 11.1 %collective-permute-done.40 = bf16[288,576]{1,0:T(8,128)(2,1)S(1)} collective-permute-done((bf16[288,576]{1,0:T(8,128)(2,1)}, bf16[288,576]{1,0:T(8,128)(2,1)S(1)}, u32[]{:S(2)}, u32[]{:S(2)}) %collective-permute-start.40) | collective-permute-done | bytes 331808 | tf_op jit(solution)/shard_map/ppermute | solution.py:70
  681.1 12.7 %shard_map.353 = (bf16[512,1024]{1,0:T(8,128)(2,1)}, f32[256,2304]{1,0:T(8,128)}, bf16[256,2304]{1,0:T(8,128)(2,1)}) custom-call(bf16[512,2304]{1,0:T(8,128)(2,1)} %constant_dynamic-update-slice_fusion.6.slopes, bf16[2304,1536]{1,0:T(8,128)(2,1)} %bitcast.36.weights, bf16[512,512]{1,0:T(8,128)(2,1)} %get-tuple-element.133.queries, ...), custom_call_target="tpu_custom_call" | custom-call | tf_op jit(solution)/shard_map/pallas_call | solution.py:673
  696.9 4.6 convolution_convert_fusion
  704.2 3.4 dynamic-slice_bitcast_fusion.3
  716.3 6.4 collective-permute-done.38
  728.7 41.7 %collective-permute-done.43.refs_2_ = bf16[288,1152]{1,0:T(8,128)(2,1)} collective-permute-done((bf16[288,1152]{1,0:T(8,128)(2,1)}, bf16[288,1152]{1,0:T(8,128)(2,1)}, u32[]{:S(2)}, u32[]{:S(2)}) %collective-permute-start.43) | collective-permute-done | bytes 663584 | tf_op jit(solution)/shard_map/ppermute | solution.py:70
  777.3 5.1 convert_add_fusion
  798.5 11.1 %collective-permute-done.49 = bf16[4,296,512]{2,1,0:T(8,128)(2,1)} collective-permute-done((bf16[4,296,512]{2,1,0:T(8,128)(2,1)}, bf16[4,296,512]{2,1,0:T(8,128)(2,1)}, u32[]{:S(2)}, u32[]{:S(2)}) %collective-permute-start.49) | collective-permute-done | bytes 1212448 | tf_op jit(solution)/shard_map/ppermute | solution.py:70
  813.9 24.6 %collective-permute-done.47 = bf16[288,1024]{1,0:T(8,128)(2,1)} collective-permute-done((bf16[288,1024]{1,0:T(8,128)(2,1)}, bf16[288,1024]{1,0:T(8,128)(2,1)}, u32[]{:S(2)}, u32[]{:S(2)}) %collective-permute-start.47) | collective-permute-done | bytes 589856 | tf_op jit(solution)/shard_map/ppermute | solution.py:70
  840.8 7.4 multiply_add_fusion
  850.9 19.7 %shard_map.354 = (f32[288,2,2304]{2,1,0:T(2,128)}, f32[288,2,2304]{2,1,0:T(2,128)}, f32[288,2,2304]{2,1,0:T(2,128)}, f32[288,2,2304]{2,1,0:T(2,128)}) custom-call(s32[1]{0:T(128)} %bitcast.90.depth, bf16[288,1152]{1,0:T(8,128)(2,1)} %get-tuple-element.158.refs_0_, bf16[288,1152]{1,0:T(8,128)(2,1)} %collective-permute-done.42.refs_1_, ...), custom_call_target="tpu_custom_call" | custom-call | tf_op jit(solution)/shard_map/pallas_call | solution.py:388
  873.5 5.2 multiply_add_fusion.2
  (412 shorter events, 200.1 us)
Async XLA Ops:
  7.2 219.8 %all-gather.3.cloned.1.call-start = ((), (), s32[]{:S(2)}) async-start(), calls=%async_computation.2 | async-start | bytes 7372800 | tf_op jit(solution)/shard_map/all_gather | solution.py:547
  21.1 36.9 %collective-permute-start.3 = (bf16[296,1536]{1,0:T(8,128)(2,1)}, bf16[296,1536]{1,0:T(8,128)(2,1)}, u32[]{:S(2)}, u32[]{:S(2)}) collective-permute-start(bf16[296,1536]{1,0:T(8,128)(2,1)} %pad_maximum_fusion.3), channel_id=1, source_target_pairs={{0,4},{4,0},{1,5},{5,1},{2,6},{6,2},{3,7},{7,3},{8,12},{12,8},{9,1... | collective-permute-start | bytes 2727944 | tf_op jit(solution)/shard_map/ppermute | solution.py:70
  26.7 31.3 %collective-permute-start.2 = (bf16[128,2304]{1,0:T(8,128)(2,1)}, bf16[128,2304]{1,0:T(8,128)(2,1)}, u32[]{:S(2)}, u32[]{:S(2)}) collective-permute-start(bf16[128,2304]{1,0:T(8,128)(2,1)} %copy.154), channel_id=1, source_target_pairs={{0,2},{2,0},{1,3},{3,1},{4,6},{6,4},{5,7},{7,5},{8,10},{10,8},{9,1... | collective-permute-start | bytes 1769480 | tf_op jit(solution)/shard_map/ppermute | solution.py:66
  26.9 29.9 %collective-permute-start.5 = (bf16[288,576]{1,0:T(8,128)(2,1)}, bf16[288,576]{1,0:T(8,128)(2,1)}, u32[]{:S(2)}, u32[]{:S(2)}) collective-permute-start(bf16[288,576]{1,0:T(8,128)(2,1)} %get-tuple-element.99), channel_id=1, source_target_pairs={{0,16},{8,24},{16,0},{24,8},{1,17},{9,25},{17,1},{25,9},{2,18},{10... | collective-permute-start | bytes 995336 | tf_op jit(solution)/shard_map/ppermute | solution.py:70
  26.9 31.0 %collective-permute-start.6 = (bf16[288,576]{1,0:T(8,128)(2,1)}, bf16[288,576]{1,0:T(8,128)(2,1)S(1)}, u32[]{:S(2)}, u32[]{:S(2)}) collective-permute-start(bf16[288,576]{1,0:T(8,128)(2,1)} %get-tuple-element.100), channel_id=1, source_target_pairs={{0,8},{8,16},{16,24},{24,0},{1,9},{9,17},{17,25},{25,1},{2,10},{10... | collective-permute-start | bytes 995336 | tf_op jit(solution)/shard_map/ppermute | solution.py:70
  59.1 286.8 %all-gather.5.cloned.1.call-start = ((), (), s32[]{:S(2)}) async-start(), calls=%async_computation.3 | async-start | bytes 13271040 | tf_op jit(solution)/shard_map/all_gather | solution.py:564
  72.9 22.2 %collective-permute-start.8 = (bf16[296,1536]{1,0:T(8,128)(2,1)}, bf16[296,1536]{1,0:T(8,128)(2,1)S(1)}, u32[]{:S(2)}, u32[]{:S(2)}) collective-permute-start(bf16[296,1536]{1,0:T(8,128)(2,1)} %pad_maximum_fusion.3), channel_id=1, source_target_pairs={{0,24},{8,0},{16,8},{24,16},{1,25},{9,1},{17,9},{25,17},{2,26},{10... | collective-permute-start | bytes 2727944 | tf_op jit(solution)/shard_map/ppermute | solution.py:70
  73.0 43.1 %collective-permute-start.9 = (bf16[296,1536]{1,0:T(8,128)(2,1)}, bf16[296,1536]{1,0:T(8,128)(2,1)S(1)}, u32[]{:S(2)}, u32[]{:S(2)}) collective-permute-start(bf16[296,1536]{1,0:T(8,128)(2,1)} %pad_maximum_fusion.3), channel_id=1, source_target_pairs={{0,8},{8,16},{16,24},{24,0},{1,9},{9,17},{17,25},{25,1},{2,10},{10... | collective-permute-start | bytes 2727944 | tf_op jit(solution)/shard_map/ppermute | solution.py:70
  116.1 41.1 %collective-permute-start.11 = (bf16[296,1536]{1,0:T(8,128)(2,1)}, bf16[296,1536]{1,0:T(8,128)(2,1)S(1)}, u32[]{:S(2)}, u32[]{:S(2)}) collective-permute-start(bf16[296,1536]{1,0:T(8,128)(2,1)} %pad_maximum_fusion.3), channel_id=1, source_target_pairs={{0,16},{8,24},{16,0},{24,8},{1,17},{9,25},{17,1},{25,9},{2,18},{10... | collective-permute-start | bytes 2727944 | tf_op jit(solution)/shard_map/ppermute | solution.py:70
  116.1 41.1 %collective-permute-start.10 = (bf16[296,1536]{1,0:T(8,128)(2,1)S(1)}, bf16[296,1536]{1,0:T(8,128)(2,1)S(1)}, u32[]{:S(2)}, u32[]{:S(2)}) collective-permute-start(bf16[296,1536]{1,0:T(8,128)(2,1)S(1)} %collective-permute-done.8), channel_id=1, source_target_pairs={{0,4},{4,0},{1,5},{5,1},{2,6},{6,2},{3,7},{7,3},{8,12},{12,8},{9,1... | collective-permute-start | bytes 2727944 | tf_op jit(solution)/shard_map/ppermute | solution.py:70
  116.9 46.7 %collective-permute-start.12 = (bf16[296,1536]{1,0:T(8,128)(2,1)S(1)}, bf16[296,1536]{1,0:T(8,128)(2,1)S(1)}, u32[]{:S(2)}, u32[]{:S(2)}) collective-permute-start(bf16[296,1536]{1,0:T(8,128)(2,1)S(1)} %collective-permute-done.9), channel_id=1, source_target_pairs={{0,4},{4,0},{1,5},{5,1},{2,6},{6,2},{3,7},{7,3},{8,12},{12,8},{9,1... | collective-permute-start | bytes 2727944 | tf_op jit(solution)/shard_map/ppermute | solution.py:70
  164.5 16.9 %collective-permute-start.16 = (bf16[288,1152]{1,0:T(8,128)(2,1)}, bf16[288,1152]{1,0:T(8,128)(2,1)S(1)}, u32[]{:S(2)}, u32[]{:S(2)}) collective-permute-start(bf16[288,1152]{1,0:T(8,128)(2,1)} %get-tuple-element.111), channel_id=1, source_target_pairs={{0,24},{8,0},{16,8},{24,16},{1,25},{9,1},{17,9},{25,17},{2,26},{10... | collective-permute-start | bytes 1990664 | tf_op jit(solution)/shard_map/ppermute | solution.py:70
  169.3 54.8 %collective-permute-start.17 = (bf16[288,1152]{1,0:T(8,128)(2,1)}, bf16[288,1152]{1,0:T(8,128)(2,1)}, u32[]{:S(2)}, u32[]{:S(2)}) collective-permute-start(bf16[288,1152]{1,0:T(8,128)(2,1)} %get-tuple-element.112), channel_id=1, source_target_pairs={{0,16},{8,24},{16,0},{24,8},{1,17},{9,25},{17,1},{25,9},{2,18},{10... | collective-permute-start | bytes 1990664 | tf_op jit(solution)/shard_map/ppermute | solution.py:70
  169.3 56.7 %collective-permute-start.18 = (bf16[288,1152]{1,0:T(8,128)(2,1)S(1)}, bf16[288,1152]{1,0:T(8,128)(2,1)S(1)}, u32[]{:S(2)}, u32[]{:S(2)}) collective-permute-start(bf16[288,1152]{1,0:T(8,128)(2,1)S(1)} %get-tuple-element.113), channel_id=1, source_target_pairs={{0,8},{8,16},{16,24},{24,0},{1,9},{9,17},{17,25},{25,1},{2,10},{10... | collective-permute-start | bytes 1990664 | tf_op jit(solution)/shard_map/ppermute | solution.py:70
  169.7 57.2 %collective-permute-start.13 = (bf16[296,1536]{1,0:T(8,128)(2,1)}, bf16[296,1536]{1,0:T(8,128)(2,1)S(1)}, u32[]{:S(2)}, u32[]{:S(2)}) collective-permute-start(bf16[296,1536]{1,0:T(8,128)(2,1)} %copy-done.34), channel_id=1, source_target_pairs={{0,4},{4,0},{1,5},{5,1},{2,6},{6,2},{3,7},{7,3},{8,12},{12,8},{9,1... | collective-permute-start | bytes 2727944 | tf_op jit(solution)/shard_map/ppermute | solution.py:70
  227.0 410.4 %reduce-scatter.3.cloned.1.call-start = ((), (), s32[]{:S(2)}) async-start(), calls=%async_computation.4 | async-start | bytes 7372800 | tf_op jit(solution)/shard_map/reduce_scatter | solution.py:643
  268.8 14.6 %collective-permute-start.15 = (bf16[128,2304]{1,0:T(8,128)(2,1)S(1)}, bf16[128,2304]{1,0:T(8,128)(2,1)S(1)}, u32[]{:S(2)}, u32[]{:S(2)}) collective-permute-start(bf16[128,2304]{1,0:T(8,128)(2,1)S(1)} %slice.524), channel_id=1, source_target_pairs={{0,2},{2,0},{1,3},{3,1},{4,6},{6,4},{5,7},{7,5},{8,10},{10,8},{9,1... | collective-permute-start | bytes 1769480 | tf_op jit(solution)/shard_map/ppermute | solution.py:66
  286.8 13.8 %collective-permute-start.19 = (bf16[128,2304]{1,0:T(8,128)(2,1)S(1)}, bf16[128,2304]{1,0:T(8,128)(2,1)S(1)}, u32[]{:S(2)}, u32[]{:S(2)}) collective-permute-start(bf16[128,2304]{1,0:T(8,128)(2,1)S(1)} %multiply_convert_fusion.1), channel_id=1, source_target_pairs={{0,24},{8,0},{16,8},{24,16},{1,25},{9,1},{17,9},{25,17},{2,26},{10... | collective-permute-start | bytes 1769480 | tf_op jit(solution)/shard_map/ppermute | solution.py:70
  286.8 51.5 %collective-permute-start.21 = (bf16[128,2304]{1,0:T(8,128)(2,1)S(1)}, bf16[128,2304]{1,0:T(8,128)(2,1)S(1)}, u32[]{:S(2)}, u32[]{:S(2)}) collective-permute-start(bf16[128,2304]{1,0:T(8,128)(2,1)S(1)} %multiply_convert_fusion.1), channel_id=1, source_target_pairs={{0,8},{8,16},{16,24},{24,0},{1,9},{9,17},{17,25},{25,1},{2,10},{10... | collective-permute-start | bytes 1769480 | tf_op jit(solution)/shard_map/ppermute | solution.py:70
  288.7 49.6 %collective-permute-start.20 = (bf16[128,2304]{1,0:T(8,128)(2,1)S(1)}, bf16[128,2304]{1,0:T(8,128)(2,1)S(1)}, u32[]{:S(2)}, u32[]{:S(2)}) collective-permute-start(bf16[128,2304]{1,0:T(8,128)(2,1)S(1)} %multiply_convert_fusion.1), channel_id=1, source_target_pairs={{0,16},{8,24},{16,0},{24,8},{1,17},{9,25},{17,1},{25,9},{2,18},{10... | collective-permute-start | bytes 1769480 | tf_op jit(solution)/shard_map/ppermute | solution.py:70
  388.7 16.9 %collective-permute-start.24 = (bf16[128,2304]{1,0:T(8,128)(2,1)}, bf16[128,2304]{1,0:T(8,128)(2,1)}, u32[]{:S(2)}, u32[]{:S(2)}) collective-permute-start(bf16[128,2304]{1,0:T(8,128)(2,1)} %get-tuple-element.287), channel_id=1, source_target_pairs={{0,8},{8,16},{16,24},{24,0},{1,9},{9,17},{17,25},{25,1},{2,10},{10... | collective-permute-start | bytes 1769480 | tf_op jit(solution)/shard_map/ppermute | solution.py:70
  388.7 27.7 %collective-permute-start.26 = (bf16[128,2304]{1,0:T(8,128)(2,1)}, bf16[128,2304]{1,0:T(8,128)(2,1)}, u32[]{:S(2)}, u32[]{:S(2)}) collective-permute-start(bf16[128,2304]{1,0:T(8,128)(2,1)} %get-tuple-element.288), channel_id=1, source_target_pairs={{0,24},{8,0},{16,8},{24,16},{1,25},{9,1},{17,9},{25,17},{2,26},{10... | collective-permute-start | bytes 1769480 | tf_op jit(solution)/shard_map/ppermute | solution.py:70
  392.0 50.8 %collective-permute-start.25 = (bf16[128,2304]{1,0:T(8,128)(2,1)}, bf16[128,2304]{1,0:T(8,128)(2,1)}, u32[]{:S(2)}, u32[]{:S(2)}) collective-permute-start(bf16[128,2304]{1,0:T(8,128)(2,1)} %get-tuple-element.289), channel_id=1, source_target_pairs={{0,16},{8,24},{16,0},{24,8},{1,17},{9,25},{17,1},{25,9},{2,18},{10... | collective-permute-start | bytes 1769480 | tf_op jit(solution)/shard_map/ppermute | solution.py:70
  447.2 15.8 %collective-permute-start.29 = (bf16[128,2304]{1,0:T(8,128)(2,1)S(1)}, bf16[128,2304]{1,0:T(8,128)(2,1)S(1)}, u32[]{:S(2)}, u32[]{:S(2)}) collective-permute-start(bf16[128,2304]{1,0:T(8,128)(2,1)S(1)} %get-tuple-element.300), channel_id=1, source_target_pairs={{0,8},{8,16},{16,24},{24,0},{1,9},{9,17},{17,25},{25,1},{2,10},{10... | collective-permute-start | bytes 1769480 | tf_op jit(solution)/shard_map/ppermute | solution.py:70
  447.2 40.5 %collective-permute-start.28 = (bf16[128,2304]{1,0:T(8,128)(2,1)S(1)}, bf16[128,2304]{1,0:T(8,128)(2,1)S(1)}, u32[]{:S(2)}, u32[]{:S(2)}) collective-permute-start(bf16[128,2304]{1,0:T(8,128)(2,1)S(1)} %get-tuple-element.300), channel_id=1, source_target_pairs={{0,16},{8,24},{16,0},{24,8},{1,17},{9,25},{17,1},{25,9},{2,18},{10... | collective-permute-start | bytes 1769480 | tf_op jit(solution)/shard_map/ppermute | solution.py:70
  447.2 40.5 %collective-permute-start.27 = (bf16[128,2304]{1,0:T(8,128)(2,1)S(1)}, bf16[128,2304]{1,0:T(8,128)(2,1)S(1)}, u32[]{:S(2)}, u32[]{:S(2)}) collective-permute-start(bf16[128,2304]{1,0:T(8,128)(2,1)S(1)} %get-tuple-element.300), channel_id=1, source_target_pairs={{0,24},{8,0},{16,8},{24,16},{1,25},{9,1},{17,9},{25,17},{2,26},{10... | collective-permute-start | bytes 1769480 | tf_op jit(solution)/shard_map/ppermute | solution.py:70
  508.4 195.8 %reduce-scatter.5.cloned.1.call-start = ((), (), s32[]{:S(2)}) async-start(), calls=%async_computation.5 | async-start | bytes 13271040 | tf_op jit(solution)/shard_map/reduce_scatter | solution.py:643
  569.9 25.5 %collective-permute-start.32 = (bf16[128,2304]{1,0:T(8,128)(2,1)S(1)}, bf16[128,2304]{1,0:T(8,128)(2,1)S(1)}, u32[]{:S(2)}, u32[]{:S(2)}) collective-permute-start(bf16[128,2304]{1,0:T(8,128)(2,1)S(1)} %get-tuple-element.284), channel_id=1, source_target_pairs={{0,8},{8,16},{16,24},{24,0},{1,9},{9,17},{17,25},{25,1},{2,10},{10... | collective-permute-start | bytes 1769480 | tf_op jit(solution)/shard_map/ppermute | solution.py:70
  582.9 25.1 %collective-permute-start.34 = (bf16[128,2304]{1,0:T(8,128)(2,1)S(1)}, bf16[128,2304]{1,0:T(8,128)(2,1)S(1)}, u32[]{:S(2)}, u32[]{:S(2)}) collective-permute-start(bf16[128,2304]{1,0:T(8,128)(2,1)S(1)} %get-tuple-element.285), channel_id=1, source_target_pairs={{0,24},{8,0},{16,8},{24,16},{1,25},{9,1},{17,9},{25,17},{2,26},{10... | collective-permute-start | bytes 1769480 | tf_op jit(solution)/shard_map/ppermute | solution.py:70
  583.1 50.1 %collective-permute-start.33 = (bf16[128,2304]{1,0:T(8,128)(2,1)S(1)}, bf16[128,2304]{1,0:T(8,128)(2,1)S(1)}, u32[]{:S(2)}, u32[]{:S(2)}) collective-permute-start(bf16[128,2304]{1,0:T(8,128)(2,1)S(1)} %get-tuple-element.286), channel_id=1, source_target_pairs={{0,16},{8,24},{16,0},{24,8},{1,17},{9,25},{17,1},{25,9},{2,18},{10... | collective-permute-start | bytes 1769480 | tf_op jit(solution)/shard_map/ppermute | solution.py:70
  639.8 25.5 %collective-permute-start.35 = (bf16[128,2304]{1,0:T(8,128)(2,1)S(1)}, bf16[128,2304]{1,0:T(8,128)(2,1)S(1)}, u32[]{:S(2)}, u32[]{:S(2)}) collective-permute-start(bf16[128,2304]{1,0:T(8,128)(2,1)S(1)} %subtract_multiply_fusion), channel_id=1, source_target_pairs={{0,2},{2,0},{1,3},{3,1},{4,6},{6,4},{5,7},{7,5},{8,10},{10,8},{9,1... | collective-permute-start | bytes 1769480 | tf_op jit(solution)/shard_map/ppermute | solution.py:66
  645.1 22.0 %collective-permute-start.39 = (bf16[288,576]{1,0:T(8,128)(2,1)}, bf16[288,576]{1,0:T(8,128)(2,1)S(1)}, u32[]{:S(2)}, u32[]{:S(2)}) collective-permute-start(bf16[288,576]{1,0:T(8,128)(2,1)} %get-tuple-element.141), channel_id=1, source_target_pairs={{0,24},{8,0},{16,8},{24,16},{1,25},{9,1},{17,9},{25,17},{2,26},{10... | collective-permute-start | bytes 995336 | tf_op jit(solution)/shard_map/ppermute | solution.py:70
  648.2 30.0 %collective-permute-start.40 = (bf16[288,576]{1,0:T(8,128)(2,1)}, bf16[288,576]{1,0:T(8,128)(2,1)S(1)}, u32[]{:S(2)}, u32[]{:S(2)}) collective-permute-start(bf16[288,576]{1,0:T(8,128)(2,1)} %get-tuple-element.142), channel_id=1, source_target_pairs={{0,16},{8,24},{16,0},{24,8},{1,17},{9,25},{17,1},{25,9},{2,18},{10... | collective-permute-start | bytes 995336 | tf_op jit(solution)/shard_map/ppermute | solution.py:70
  648.3 30.0 %collective-permute-start.41 = (bf16[288,576]{1,0:T(8,128)(2,1)S(1)}, bf16[288,576]{1,0:T(8,128)(2,1)S(1)}, u32[]{:S(2)}, u32[]{:S(2)}) collective-permute-start(bf16[288,576]{1,0:T(8,128)(2,1)S(1)} %get-tuple-element.143), channel_id=1, source_target_pairs={{0,8},{8,16},{16,24},{24,0},{1,9},{9,17},{17,25},{25,1},{2,10},{10... | collective-permute-start | bytes 995336 | tf_op jit(solution)/shard_map/ppermute | solution.py:70
  665.4 14.6 %collective-permute-start.36 = (bf16[256,2304]{1,0:T(8,128)(2,1)S(1)}, bf16[256,2304]{1,0:T(8,128)(2,1)S(1)}, u32[]{:S(2)}, u32[]{:S(2)}) collective-permute-start(bf16[256,2304]{1,0:T(8,128)(2,1)S(1)} %pad_maximum_fusion.2), channel_id=1, source_target_pairs={{0,1},{1,0},{2,3},{3,2},{4,5},{5,4},{6,7},{7,6},{8,9},{9,8},{10,11... | collective-permute-start | bytes 3538952 | tf_op jit(solution)/shard_map/ppermute | solution.py:66
  693.8 14.3 %collective-permute-start.37 = (bf16[256,2304]{1,0:T(8,128)(2,1)}, bf16[256,2304]{1,0:T(8,128)(2,1)S(1)}, u32[]{:S(2)}, u32[]{:S(2)}) collective-permute-start(bf16[256,2304]{1,0:T(8,128)(2,1)} %get-tuple-element.138), channel_id=1, source_target_pairs={{0,1},{1,0},{2,3},{3,2},{4,5},{5,4},{6,7},{7,6},{8,9},{9,8},{10,11... | collective-permute-start | bytes 3538952 | tf_op jit(solution)/shard_map/ppermute | solution.py:66
  707.6 68.7 %collective-permute-start.45 = (bf16[4,288,1024]{2,1,0:T(8,128)(2,1)}, bf16[4,288,1024]{2,1,0:T(8,128)(2,1)}, u32[]{:S(2)}, u32[]{:S(2)}) collective-permute-start(bf16[4,288,1024]{2,1,0:T(8,128)(2,1)} %get-tuple-element.148), channel_id=1, source_target_pairs={{0,4},{4,0},{1,5},{5,1},{2,6},{6,2},{3,7},{7,3},{8,12},{12,8},{9,1... | collective-permute-start | bytes 7077896 | tf_op jit(solution)/shard_map/ppermute | solution.py:70
  708.5 14.2 %collective-permute-start.38 = (bf16[128,2304]{1,0:T(8,128)(2,1)S(1)}, bf16[128,2304]{1,0:T(8,128)(2,1)S(1)}, u32[]{:S(2)}, u32[]{:S(2)}) collective-permute-start(bf16[128,2304]{1,0:T(8,128)(2,1)S(1)} %slice.523), channel_id=1, source_target_pairs={{0,2},{2,0},{1,3},{3,1},{4,6},{6,4},{5,7},{7,5},{8,10},{10,8},{9,1... | collective-permute-start | bytes 1769480 | tf_op jit(solution)/shard_map/ppermute | solution.py:66
  709.8 18.9 %collective-permute-start.42 = (bf16[288,1152]{1,0:T(8,128)(2,1)}, bf16[288,1152]{1,0:T(8,128)(2,1)}, u32[]{:S(2)}, u32[]{:S(2)}) collective-permute-start(bf16[288,1152]{1,0:T(8,128)(2,1)} %get-tuple-element.144), channel_id=1, source_target_pairs={{0,24},{8,0},{16,8},{24,16},{1,25},{9,1},{17,9},{25,17},{2,26},{10... | collective-permute-start | bytes 1990664 | tf_op jit(solution)/shard_map/ppermute | solution.py:70
  712.8 57.5 %collective-permute-start.43 = (bf16[288,1152]{1,0:T(8,128)(2,1)}, bf16[288,1152]{1,0:T(8,128)(2,1)}, u32[]{:S(2)}, u32[]{:S(2)}) collective-permute-start(bf16[288,1152]{1,0:T(8,128)(2,1)} %get-tuple-element.145), channel_id=1, source_target_pairs={{0,16},{8,24},{16,0},{24,8},{1,17},{9,25},{17,1},{25,9},{2,18},{10... | collective-permute-start | bytes 1990664 | tf_op jit(solution)/shard_map/ppermute | solution.py:70
  712.8 57.5 %collective-permute-start.44 = (bf16[288,1152]{1,0:T(8,128)(2,1)}, bf16[288,1152]{1,0:T(8,128)(2,1)}, u32[]{:S(2)}, u32[]{:S(2)}) collective-permute-start(bf16[288,1152]{1,0:T(8,128)(2,1)} %get-tuple-element.146), channel_id=1, source_target_pairs={{0,8},{8,16},{16,24},{24,0},{1,9},{9,17},{17,25},{25,1},{2,10},{10... | collective-permute-start | bytes 1990664 | tf_op jit(solution)/shard_map/ppermute | solution.py:70
  782.4 27.3 %collective-permute-start.49 = (bf16[4,296,512]{2,1,0:T(8,128)(2,1)}, bf16[4,296,512]{2,1,0:T(8,128)(2,1)}, u32[]{:S(2)}, u32[]{:S(2)}) collective-permute-start(bf16[4,296,512]{2,1,0:T(8,128)(2,1)} %dynamic-slice_bitcast_fusion.2), channel_id=1, source_target_pairs={{0,4},{4,0},{1,5},{5,1},{2,6},{6,2},{3,7},{7,3},{8,12},{12,8},{9,1... | collective-permute-start | bytes 3637256 | tf_op jit(solution)/shard_map/ppermute | solution.py:70
  784.7 13.8 %collective-permute-start.46 = (bf16[288,1024]{1,0:T(8,128)(2,1)}, bf16[288,1024]{1,0:T(8,128)(2,1)}, u32[]{:S(2)}, u32[]{:S(2)}) collective-permute-start(bf16[288,1024]{1,0:T(8,128)(2,1)} %get-tuple-element.149), channel_id=1, source_target_pairs={{0,24},{8,0},{16,8},{24,16},{1,25},{9,1},{17,9},{25,17},{2,26},{10... | collective-permute-start | bytes 1769480 | tf_op jit(solution)/shard_map/ppermute | solution.py:70
  784.7 53.8 %collective-permute-start.47 = (bf16[288,1024]{1,0:T(8,128)(2,1)}, bf16[288,1024]{1,0:T(8,128)(2,1)}, u32[]{:S(2)}, u32[]{:S(2)}) collective-permute-start(bf16[288,1024]{1,0:T(8,128)(2,1)} %get-tuple-element.150), channel_id=1, source_target_pairs={{0,16},{8,24},{16,0},{24,8},{1,17},{9,25},{17,1},{25,9},{2,18},{10... | collective-permute-start | bytes 1769480 | tf_op jit(solution)/shard_map/ppermute | solution.py:70
  787.3 51.2 %collective-permute-start.48 = (bf16[288,1024]{1,0:T(8,128)(2,1)}, bf16[288,1024]{1,0:T(8,128)(2,1)}, u32[]{:S(2)}, u32[]{:S(2)}) collective-permute-start(bf16[288,1024]{1,0:T(8,128)(2,1)} %get-tuple-element.151), channel_id=1, source_target_pairs={{0,8},{8,16},{16,24},{24,0},{1,9},{9,17},{17,25},{25,1},{2,10},{10... | collective-permute-start | bytes 1769480 | tf_op jit(solution)/shard_map/ppermute | solution.py:70
  838.5 32.1 %collective-permute-start.50 = (bf16[296,512]{1,0:T(8,128)(2,1)}, bf16[296,512]{1,0:T(8,128)(2,1)S(1)}, u32[]{:S(2)}, u32[]{:S(2)}) collective-permute-start(bf16[296,512]{1,0:T(8,128)(2,1)} %get-tuple-element.155), channel_id=1, source_target_pairs={{0,24},{8,0},{16,8},{24,16},{1,25},{9,1},{17,9},{25,17},{2,26},{10... | collective-permute-start | bytes 909320 | tf_op jit(solution)/shard_map/ppermute | solution.py:70
  838.5 32.1 %collective-permute-start.51 = (bf16[296,512]{1,0:T(8,128)(2,1)}, bf16[296,512]{1,0:T(8,128)(2,1)S(1)}, u32[]{:S(2)}, u32[]{:S(2)}) collective-permute-start(bf16[296,512]{1,0:T(8,128)(2,1)} %get-tuple-element.156), channel_id=1, source_target_pairs={{0,16},{8,24},{16,0},{24,8},{1,17},{9,25},{17,1},{25,9},{2,18},{10... | collective-permute-start | bytes 909320 | tf_op jit(solution)/shard_map/ppermute | solution.py:70
  839.2 31.5 %collective-permute-start.52 = (bf16[296,512]{1,0:T(8,128)(2,1)}, bf16[296,512]{1,0:T(8,128)(2,1)S(1)}, u32[]{:S(2)}, u32[]{:S(2)}) collective-permute-start(bf16[296,512]{1,0:T(8,128)(2,1)} %get-tuple-element.157), channel_id=1, source_target_pairs={{0,8},{8,16},{16,24},{24,0},{1,9},{9,17},{17,25},{25,1},{2,10},{10... | collective-permute-start | bytes 909320 | tf_op jit(solution)/shard_map/ppermute | solution.py:70
  (75 other events, 799.3 us)
Sparse Core Ops, SparseCore 0:
  59.2 71.3 all-gather.2
  227.1 114.9 all-gather.4
  508.6 75.7 reduce-scatter.2
  587.3 116.2 reduce-scatter.4
